TPU v7x, 32 devices: a whole 2x2x4 slice. The times are simulated.
32 devices in a mesh: expert: 16 (over z, y, x), half: 1, dp: 2 (over core).
Axes of the slice: x: 2, y: 2, z: 4, core: 2. Of those that a mesh axis runs over, the one named last changes fastest.
Arguments:
- tokens: bfloat16 [4096, 4096], P(('expert', 'dp'), 'half'), may hold values from -6 to 6
- cotangent: bfloat16 [4096, 4096], P(('expert', 'dp'), 'half'), may hold values from -12 to 12
- expert_ids: int32 [4096, 8], P(('expert', 'dp')), may hold values from 0 to 15, as said below
- slot_ids: int32 [4096, 8], P(('expert', 'dp')), may hold values from 0 to 71, as said below
- gate_weights: float32 [4096, 8], P(('expert', 'dp')), may hold values from 0.03 to 0.4
- latent_down: bfloat16 [4096, 1024], P('half', 'dp'), may hold values from -0.09375 to 0.09375
- latent_up: bfloat16 [1024, 4096], P('dp', 'half'), may hold values from -0.1875 to 0.1875
- expert_gate: bfloat16 [16, 1024, 1536], P('expert', 'dp', 'half'), may hold values from -0.1875 to 0.1875
- expert_linear: bfloat16 [16, 1024, 1536], P('expert', 'dp', 'half'), may hold values from -0.1875 to 0.1875
- expert_out: bfloat16 [16, 1536, 1024], P('expert', 'half', 'dp'), may hold values from -0.15625 to 0.15625
Outputs:
- token_grad: bfloat16 [4096, 4096], P(('expert', 'dp'), 'half')
- gate_grad: bfloat16 [16, 1024, 1536], P('expert', 'dp', 'half')
- linear_grad: bfloat16 [16, 1024, 1536], P('expert', 'dp', 'half')
- out_grad: bfloat16 [16, 1536, 1024], P('expert', 'half', 'dp')
Inputs may be any that keep to these rules, and one draw needn't show every extreme that they name: `expert_ids`: each row names 8 different experts. In each aligned block of 128 rows (the rows of one device) no expert is named by more than 72 rows, and one expert is named by exactly 72 rows in every block. `slot_ids`: within one aligned block of 128 rows, the entries that name the same expert have different slots.
All inputs are finite; a program needn't handle non-finite values.
Results may differ from a plain program's by a relative error of at most 0.013.
Values may be sent and summed in bfloat16 or wider, within the bound.
No kernel may reach another device: no remote copies, remote signals or barrier semaphores. Data moves between devices by JAX's collectives and lax.ppermute only.
A program may use at most 128 MiB of HBM per device.

v0:
```python
import functools

import jax
import jax.numpy as jnp
from jax import lax
from jax.experimental import pallas as pl
from jax.experimental.pallas import tpu as pltpu
from jax.sharding import PartitionSpec as P

BF = jnp.bfloat16
F32 = jnp.float32
PLANES = 4
SIDE = 2
META = 8
SIDE_TIE = True
SCALE = 1
MIB = 1024 * 1024
ROWS = (((0,), (0,)), ((), ()))
LAST = (((1,), (1,)), ((), ()))
ANY = pl.BlockSpec(memory_space=pl.ANY)
VMEM = pl.BlockSpec(memory_space=pltpu.VMEM)


def pad16(n):
    return (n + 15) // 16 * 16


def params(mib):
    return pltpu.CompilerParams(vmem_limit_bytes=mib * MIB)


def cost(flops, moved):
    return pl.CostEstimate(flops=int(flops * SCALE) + 1, bytes_accessed=int(moved * SCALE) + 1, transcendentals=0)


def whole(shape):
    return pl.BlockSpec(shape, lambda *_: (0,) * len(shape))


def join_body(routes, own_ref, other_ref, *refs):
    out_ref = refs[-1]
    tokens, half = own_ref.shape
    out_ref[:tokens, :half] = own_ref[...]
    out_ref[:tokens, half:] = other_ref[...]
    if routes:
        ids_ref, slots_ref, gates_ref = refs[:3]
        gates = gates_ref[...]
        high = gates.astype(BF)
        rest = gates - high.astype(F32)
        middle = rest.astype(BF)
        low = (rest - middle.astype(F32)).astype(BF)
        kinds = [ids_ref[...].astype(F32).astype(BF), slots_ref[...].astype(F32).astype(BF)]
        kinds += [high, middle, low]
        kinds += [jnp.zeros_like(low)] * (META - len(kinds))
        picks = gates.shape[0]
        table = jnp.concatenate([a.astype(F32) for a in kinds], axis=1)
        table = jnp.concatenate(
            [table, jnp.zeros((pad16(picks) - picks, table.shape[1]), F32)], axis=0
        )
        out_ref[tokens:, :] = table.astype(BF)


def join_rows(own, other, routes, deps):
    tokens, half = own.shape
    extra = pad16(routes[0].shape[0]) if routes else 0
    return pl.pallas_call(
        functools.partial(join_body, bool(routes)),
        out_shape=jax.ShapeDtypeStruct((tokens + extra, 2 * half), BF),
        in_specs=[VMEM] * (2 + len(routes)) + [ANY] * len(deps),
        out_specs=VMEM,
        compiler_params=params(8),
        cost_estimate=cost(0, 8 * tokens * half),
        name="join_rows",
    )(own, other, *routes, *deps)


def tie_body(block_ref, *refs):
    refs[-1][...] = block_ref[...]


def tie(block, deps):
    return pl.pallas_call(
        tie_body,
        out_shape=jax.ShapeDtypeStruct(block.shape, block.dtype),
        in_specs=[VMEM] + [ANY] * len(deps),
        out_specs=VMEM,
        compiler_params=params(8),
        cost_estimate=cost(0, 4 * block.size),
        name="tie_rows",
    )(block, *deps)


def one_hots(meta_refs, picks, fan, cap, weighted):
    me = lax.axis_index("expert")
    padded = pad16(len(meta_refs) * cap)
    marks, total = [], None
    for j, ref in enumerate(meta_refs):
        tokens = ref.shape[1] // META
        start = ref.shape[0] - pad16(picks)
        kinds = [
            ref[start:, i * tokens : (i + 1) * tokens].astype(F32)
            for i in range(5 if weighted else 2)
        ]
        held = kinds[0] * cap + kinds[1]
        row = lax.broadcasted_iota(jnp.int32, (padded, tokens), 0)
        inside = jnp.logical_and(row >= j * cap, row < (j + 1) * cap)
        targets = []
        for k in range(fan):
            base = lax.bitwise_xor(me, SIDE * k) * cap - j * cap
            targets.append(jnp.where(inside, row + base, -1))
        target = jnp.concatenate(targets, axis=0).astype(F32)
        mark = jnp.zeros(target.shape, F32)
        weight = jnp.zeros(target.shape, F32)
        if weighted:
            gate = kinds[2] + kinds[3] + kinds[4]
        for i in range(picks):
            equal = target == held[i : i + 1, :]
            mark = jnp.where(equal, 1.0, mark)
            if weighted:
                weight = jnp.where(equal, gate[i : i + 1, :], weight)
        marks.append(mark.astype(BF))
        if weighted:
            weight = jnp.sum(weight, axis=1, keepdims=True)
            total = weight if total is None else total + weight
    return marks, total


def select_body(count, picks, fan, cap, weighted, deps, *refs):
    meta_refs, block_refs, piece_refs = refs[:count], refs[count : 2 * count], refs[2 * count + deps :]
    marks, weight = one_hots(meta_refs, picks, fan, cap, weighted)
    tokens = marks[0].shape[1]
    rows = None
    for mark, block_ref in zip(marks, block_refs):
        term = jnp.dot(mark, block_ref[:tokens, :], preferred_element_type=F32)
        rows = term if rows is None else rows + term
    if weighted:
        rows = rows * weight
    padded = pad16(count * cap)
    for k in range(fan):
        piece_refs[k][...] = rows[k * padded : k * padded + count * cap, :].astype(BF)


def select(metas, blocks, picks, fan, cap, weighted, deps):
    count = len(blocks)
    width = blocks[0].shape[1]
    tokens = width // META
    return pl.pallas_call(
        functools.partial(select_body, count, picks, fan, cap, weighted, len(deps)),
        out_shape=[jax.ShapeDtypeStruct((count * cap, width), BF)] * fan,
        in_specs=[VMEM] * (2 * count) + [ANY] * len(deps),
        out_specs=[VMEM] * fan,
        compiler_params=params(10),
        cost_estimate=cost(
            2 * fan * count * count * cap * tokens * width, 8 * count * tokens * width
        ),
        name="select_back" if weighted else "select_latent",
    )(*metas, *blocks, *deps)


def assemble(piece_refs, out_ref):
    rows = piece_refs[0].shape[0]
    padded = pad16(rows)
    for i, ref in enumerate(piece_refs):
        if padded > rows:
            out_ref[(i + 1) * padded - 16 : (i + 1) * padded, :] = jnp.zeros(
                (16, out_ref.shape[1]), out_ref.dtype
            )
        out_ref[i * padded : i * padded + rows, :] = ref[...]


def bundle_body(parts, held_over, deps, *refs):
    at = sum(len(part[1]) for part in parts)
    ins, refs = refs[:at], refs[at + held_over + deps :]
    outs_count = sum(len(part[2]) for part in parts)
    outs, scratch = refs[:outs_count], refs[outs_count + held_over :]
    for body, operands, results, held in parts:
        body(*ins[: len(operands)], *outs[: len(results)], *scratch[: len(held)])
        ins, outs, scratch = ins[len(operands) :], outs[len(results) :], scratch[len(held) :]


def bundle(parts, through, deps):
    operands = [a for part in parts for a in part[1]]
    shapes = [a for part in parts for a in part[2]]
    sizes = sum(a.size for a in operands)
    results = pl.pallas_call(
        functools.partial(bundle_body, parts, len(through), len(deps)),
        out_shape=shapes + [jax.ShapeDtypeStruct(a.shape, a.dtype) for a in through],
        in_specs=[VMEM] * len(operands) + [ANY] * (len(through) + len(deps)),
        out_specs=[VMEM] * len(shapes) + [ANY] * len(through),
        input_output_aliases={len(operands) + i: len(shapes) + i for i in range(len(through))},
        scratch_shapes=[a for part in parts for a in part[3]],
        compiler_params=params(10),
        cost_estimate=cost(0, 4 * sizes),
        name="return_rows",
    )(*operands, *through, *deps)
    split = []
    for part in parts:
        split.append(results[: len(part[2])])
        results = results[len(part[2]) :]
    return split, results


def copy_body(count, *refs):
    for i in range(count):
        refs[count + i][...] = refs[i][...]


def copies(arrays):
    shapes = [jax.ShapeDtypeStruct(a.shape, a.dtype) for a in arrays]
    return functools.partial(copy_body, len(arrays)), list(arrays), shapes, []


def add_body(count, *refs):
    total = refs[0][...].astype(F32)
    for ref in refs[1:count]:
        total = total + ref[...].astype(F32)
    refs[count][...] = total.astype(refs[count].dtype)


def added(arrays, dtype):
    shape = jax.ShapeDtypeStruct(arrays[0].shape, dtype)
    return functools.partial(add_body, len(arrays)), list(arrays), [shape], []


def expand_body(count, picks, fan, cap, *refs):
    meta_refs, piece_refs = refs[:count], refs[count : count + fan]
    out_refs, held = refs[count + fan : -1], refs[-1]
    assemble(piece_refs, held)
    marks, _ = one_hots(meta_refs, picks, fan, cap, False)
    for mark, out_ref in zip(marks, out_refs):
        out_ref[...] = lax.dot_general(
            mark, held[...], ROWS, preferred_element_type=F32
        ).astype(out_ref.dtype)


def expanded(metas, pieces, picks, cap, dtypes):
    count, fan = len(metas), len(pieces)
    width = pieces[0].shape[1]
    return (
        functools.partial(expand_body, count, picks, fan, cap),
        [*metas, *pieces],
        [jax.ShapeDtypeStruct((width // META, width), d) for d in dtypes],
        [pltpu.VMEM((fan * pad16(count * cap), width), BF)],
    )


def tile_of(hidden):
    return 512 if hidden % 512 == 0 else 256


def forward_body(count, deps, *refs):
    piece_refs = refs[:count]
    gate_m, gate_o, linear_m, linear_o = refs[count : count + 4]
    x_ref, gate_factor_ref, linear_factor_ref, hidden_ref = refs[count + 4 + deps :]
    assemble(piece_refs, x_ref)
    half, hidden = gate_m.shape
    tile = tile_of(hidden)
    @pl.loop(0, hidden // tile)
    def _(j):
        at = pl.ds(pl.multiple_of(j * tile, tile), tile)
        pre_gate = jnp.dot(x_ref[:, :half], gate_m[:, at], preferred_element_type=F32)
        pre_gate += jnp.dot(x_ref[:, half:], gate_o[:, at], preferred_element_type=F32)
        pre_linear = jnp.dot(x_ref[:, :half], linear_m[:, at], preferred_element_type=F32)
        pre_linear += jnp.dot(x_ref[:, half:], linear_o[:, at], preferred_element_type=F32)
        logistic = jax.nn.sigmoid(pre_gate)
        scaled = pre_gate * logistic
        hidden_ref[:, at] = (scaled * pre_linear).astype(BF)
        linear_factor_ref[:, at] = scaled.astype(BF)
        gate_factor_ref[:, at] = (
            pre_linear * logistic * (1.0 + pre_gate * (1.0 - logistic))
        ).astype(BF)


def forward(pieces, gate, linear, deps):
    count = len(pieces)
    size, width = pieces[0].shape
    rows = count * pad16(size)
    hidden = gate[0].shape[1]
    return pl.pallas_call(
        functools.partial(forward_body, count, len(deps)),
        in_specs=[VMEM] * (count + 4) + [ANY] * len(deps),
        out_specs=[VMEM] * 4,
        out_shape=[jax.ShapeDtypeStruct((rows, width), BF)]
        + [jax.ShapeDtypeStruct((rows, hidden), BF)] * 3,
        compiler_params=params(10),
        cost_estimate=cost(4 * rows * width * hidden, 6 * rows * hidden + 4 * width * hidden),
        name="forward_rows",
    )(*pieces, *gate, *linear, *deps)


def backward_body(count, deps, *refs):
    piece_refs = refs[:count]
    gate_factor, linear_factor, out_m, out_o = refs[count : count + 4]
    gate_m, gate_o, linear_m, linear_o = refs[count + 4 : count + 8]
    refs = refs[count + 8 + deps :]
    b_ref, gate_delta_ref, linear_delta_ref = refs[:3]
    row_refs, total = refs[3:-1], refs[-1]
    assemble(piece_refs, b_ref)
    hidden, half = out_m.shape
    tile = tile_of(hidden)
    for start in range(0, hidden, tile):
        at = slice(start, start + tile)
        grad = lax.dot_general(b_ref[:, :half], out_m[at, :], LAST, preferred_element_type=F32)
        grad += lax.dot_general(b_ref[:, half:], out_o[at, :], LAST, preferred_element_type=F32)
        gate_delta_ref[:, at] = (grad * gate_factor[:, at].astype(F32)).astype(BF)
        linear_delta_ref[:, at] = (grad * linear_factor[:, at].astype(F32)).astype(BF)
    for start, gate, linear in ((0, gate_m, linear_m), (half, gate_o, linear_o)):
        part = lax.dot_general(gate_delta_ref[...], gate[...], LAST, preferred_element_type=F32)
        part += lax.dot_general(
            linear_delta_ref[...], linear[...], LAST, preferred_element_type=F32
        )
        total[:, start : start + half] = part
    size = row_refs[0].shape[0]
    for i, ref in enumerate(row_refs):
        start = i * pad16(size)
        ref[...] = total[start : start + size, :].astype(BF)


def backward(pieces, gate_factor, linear_factor, out, gate, linear, deps):
    count = len(pieces)
    size, width = pieces[0].shape
    rows = count * pad16(size)
    hidden = gate_factor.shape[1]
    results = pl.pallas_call(
        functools.partial(backward_body, count, len(deps)),
        in_specs=[VMEM] * (count + 8) + [ANY] * len(deps),
        out_specs=[VMEM] * (3 + count),
        out_shape=[jax.ShapeDtypeStruct((rows, width), BF)]
        + [jax.ShapeDtypeStruct((rows, hidden), BF)] * 2
        + [jax.ShapeDtypeStruct((size, width), BF)] * count,
        scratch_shapes=[pltpu.VMEM((rows, width), F32)],
        compiler_params=params(10),
        cost_estimate=cost(6 * rows * width * hidden, 8 * rows * hidden + 6 * width * hidden),
        name="backward_rows",
    )(*pieces, gate_factor, linear_factor, *out, *gate, *linear, *deps)
    return results[:3], results[3:]


def weight_body(groups, column, deps, *refs):
    outs = refs[5 * groups + deps :]
    width, hidden = refs[0].shape[1], refs[2].shape[1]
    half, tile = width // 2, tile_of(hidden)
    side = slice(column * half, (column + 1) * half)
    @pl.loop(0, hidden // tile)
    def _(j):
        at = pl.ds(pl.multiple_of(j * tile, tile), tile)
        totals = [None, None, None]
        for g in range(groups):
            x_ref, b_ref, gate_delta, linear_delta, hid = refs[5 * g : 5 * g + 5]
            for i, (a, b) in enumerate(
                (
                    (x_ref[:, side], gate_delta[:, at]),
                    (x_ref[:, side], linear_delta[:, at]),
                    (hid[:, at], b_ref[:, side]),
                )
            ):
                term = lax.dot_general(a, b, ROWS, preferred_element_type=F32)
                totals[i] = term if totals[i] is None else totals[i] + term
        outs[0][:half, at] = totals[0].astype(BF)
        outs[0][half:, at] = totals[1].astype(BF)
        outs[1][at, :] = totals[2].astype(BF)


def weight_grads(groups, column, deps):
    hidden = groups[0][2].shape[1]
    width = groups[0][0].shape[1]
    half = width // 2
    operands = [a for group in groups for a in group]
    total_rows = sum(group[0].shape[0] for group in groups)
    return pl.pallas_call(
        functools.partial(weight_body, len(groups), column, len(deps)),
        in_specs=[VMEM] * len(operands) + [ANY] * len(deps),
        out_specs=[VMEM] * 2,
        out_shape=[jax.ShapeDtypeStruct(s, BF) for s in ((width, hidden), (hidden, half))],
        compiler_params=params(12),
        cost_estimate=cost(
            3 * total_rows * width * hidden, 6 * total_rows * hidden + 3 * width * hidden
        ),
        name="weight_grads",
    )(*operands, *deps)


def split_body(mine_ref, theirs_ref, top_ref, bottom_ref):
    half = top_ref.shape[0]
    for out_ref, at in ((top_ref, slice(0, half)), (bottom_ref, slice(half, 2 * half))):
        out_ref[...] = (mine_ref[at, :].astype(F32) + theirs_ref[at, :].astype(F32)).astype(BF)


def added_halves(mine, theirs):
    rows, hidden = mine.shape
    return split_body, [mine, theirs], [jax.ShapeDtypeStruct((rows // 2, hidden), BF)] * 2, []


def finish_body(count, *refs):
    part_refs, (down_m, down_o), out_ref = refs[:count], refs[count : count + 2], refs[-1]
    total = part_refs[0][...].astype(F32)
    for ref in part_refs[1:]:
        total = total + ref[...].astype(F32)
    total = total.astype(BF)
    model, half = down_m.shape
    tile = tile_of(model)
    for start in range(0, model, tile):
        at = slice(start, start + tile)
        part = lax.dot_general(total[:, :half], down_m[at, :], LAST, preferred_element_type=F32)
        part += lax.dot_general(total[:, half:], down_o[at, :], LAST, preferred_element_type=F32)
        out_ref[:, at] = part.astype(BF)


def finish(parts, down, deps):
    tokens, model = parts[0].shape[0], down[0].shape[0]
    return pl.pallas_call(
        lambda *refs: finish_body(len(parts), *refs[: len(parts) + 2], refs[-1]),
        in_specs=[VMEM] * (len(parts) + 2) + [ANY] * len(deps),
        out_specs=VMEM,
        out_shape=jax.ShapeDtypeStruct((tokens, model), BF),
        compiler_params=params(10),
        cost_estimate=cost(2 * tokens * model * parts[0].shape[1], 4 * down[0].size),
        name="token_grad",
    )(*parts, *down, *deps)


def on_device(
    tokens,
    cotangent,
    expert_ids,
    slot_ids,
    gate_weights,
    latent_down,
    latent_up,
    expert_gate,
    expert_linear,
    expert_out,
):
    row_count = tokens.shape[0]
    pick_count = expert_ids.shape[1]
    group_count = lax.axis_size("expert")
    halves = lax.axis_size("half")
    expert_count = group_count * expert_gate.shape[0]
    capacity = min(
        row_count, 2 * ((9 * row_count * pick_count + 16 * expert_count - 1) // (16 * expert_count))
    )
    inner = group_count // PLANES
    fan = inner // SIDE

    def swap(a):
        return lax.ppermute(a, "dp", [(0, 1), (1, 0)])

    def along(a, shift):
        return lax.ppermute(
            a,
            "expert",
            [
                (z * inner + p, (z + shift) % PLANES * inner + p)
                for z in range(PLANES)
                for p in range(inner)
            ],
        )

    def beside(a):
        return lax.ppermute(a, "expert", [(i, i ^ 1) for i in range(group_count)])

    def across(parts):
        return [parts[0]] + [
            lax.ppermute(parts[k], "expert", [(i, i ^ (SIDE * k)) for i in range(group_count)])
            for k in range(1, fan)
        ]

    def summed(a):
        return lax.psum(a, "half") if halves > 1 else a

    last = []

    def deps(*extra):
        return [*last[-1:], *extra]

    def step(result):
        last.append(result[0] if isinstance(result, (list, tuple)) else result)
        return result

    def dot(a, weight, dims):
        if last:
            a = lax.optimization_barrier((a, last[-1]))[0]
        result = lax.dot_general(a, weight, dims, preferred_element_type=F32)
        return step(summed(result).astype(BF))

    def swapped_after(arrays, extra):
        held = lax.optimization_barrier((*arrays, *extra))[: len(arrays)]
        return [(a, swap(a)) for a in held]

    their_tokens, their_cotangent = swap(tokens), swap(cotangent)
    rows_first = (((1,), (0,)), ((), ()))
    latent_own = dot(tokens, latent_down, rows_first)
    latent_other = swap(dot(their_tokens, latent_down, rows_first))
    latent = step(
        join_rows(
            latent_own, latent_other, (expert_ids.T, slot_ids.T, gate_weights.T), deps()
        )
    )
    gate, linear, out = swapped_after(
        (expert_gate[0], expert_linear[0], expert_out[0]), (latent,)
    )
    back_own = dot(cotangent, latent_up, LAST)
    back_other = swap(dot(their_cotangent, latent_up, LAST))

    blocks, pairs, pieces = {("l", 0): latent}, {}, {}

    def to_plane(kind, c, *extra):
        block = blocks[kind, 0]
        if extra:
            block = step(tie(block, deps(*extra)))
        with jax.named_scope(f"plane_{kind}{c}"):
            blocks[kind, c] = along(block, c)

    def to_side(kind, c, tied=False):
        if tied:
            blocks[kind, c] = step(tie(blocks[kind, c], deps()))
        with jax.named_scope(f"side_{kind}{c}"):
            pairs[kind, c] = [blocks[kind, c], beside(blocks[kind, c])]

    def pick(kind, c, *extra):
        parts = step(
            select(
                pairs["l", c], pairs[kind, c], pick_count, fan, capacity, kind == "b", deps(*extra)
            )
        )
        with jax.named_scope(f"piece_{kind}{c}"):
            pieces[kind, c] = across(parts)

    def come(kind, c):
        return pieces[kind, c][-1]

    factors, saved, rows, partial = {}, {}, {}, {}

    def ahead(chunks):
        factors[chunks] = step(
            forward([a for c in chunks for a in pieces["l", c]], gate, linear, deps())
        )

    def behind(chunks, *extra):
        x, gate_factor, linear_factor, hid = factors[chunks]
        (b, gate_delta, linear_delta), sums = backward(
            [a for c in chunks for a in pieces["b", c]],
            gate_factor,
            linear_factor,
            out,
            gate,
            linear,
            deps(*extra),
        )
        step(b)
        saved[chunks] = (x, b, gate_delta, linear_delta, hid)
        for i, c in enumerate(chunks):
            rows[c] = sums[i * fan : (i + 1) * fan]

    def send_rows(c, operands):
        with jax.named_scope(f"piece_r{c}"):
            rows[c] = across([rows[c][0], *operands])

    def send_side(c, results):
        own, other = results
        with jax.named_scope(f"side_r{c}"):
            partial[c] = [own, beside(other)]

    def send_home(c, results):
        with jax.named_scope(f"plane_r{c}"):
            partial[c] = along(results[0], -c)

    def turn(parts, through=(), extra=()):
        results, passed = bundle(parts, list(through), deps(*extra))
        step(results[0][0])
        return [*results, *passed]

    def gathered(c):
        return expanded(pairs["l", c], rows[c], pick_count, capacity, [F32, BF])

    to_plane("l", 1)
    to_side("l", 0)
    to_plane("l", 3, gate[1])
    back = step(join_rows(back_own, back_other, (), deps()))
    blocks["b", 0] = back
    pick("l", 0, blocks["l", 1], linear[1], out[1])
    to_side("l", 1)
    to_plane("l", 2, blocks["l", 1])
    pick("l", 1, blocks["l", 3])
    to_side("l", 3)
    to_plane("b", 2, blocks["l", 3])
    pick("l", 3, come("l", 0))
    to_side("b", 0)
    pick("b", 0, come("l", 1), blocks["l", 2])
    to_side("l", 2)
    to_plane("b", 3, blocks["l", 2])
    ahead((0, 1))
    pick("l", 2, come("l", 3), blocks["b", 2])
    to_side("b", 2)
    to_plane("b", 1, blocks["b", 2])
    (down,) = swapped_after((latent_down,), last[-1:])
    pick("b", 2, come("b", 0), blocks["b", 3])
    to_side("b", 3)
    ahead((3, 2))
    pick("b", 3, come("l", 2), blocks["b", 1])
    to_side("b", 1)
    pick("b", 1, come("b", 2), down[1])
    behind((3, 2))
    send_rows(3, rows[3][1:])
    behind((0, 1))
    results = turn([gathered(3), copies(rows[2][1:])])
    send_side(3, results[0])
    send_rows(2, results[1])
    theirs = weight_grads(list(saved.values()), 1, deps())
    step(theirs)
    results = turn([gathered(2), added(partial[3], BF), copies(rows[1][1:])], theirs)
    send_side(2, results[0])
    send_home(3, results[1])
    send_rows(1, results[2])
    received = [swap(results[3])]
    ours = weight_grads(list(saved.values()), 0, deps())
    step(ours)
    results = turn(
        [gathered(1), added(partial[2], BF), copies(rows[0][1:])],
        results[4:],
        [partial[3], received[0]],
    )
    send_side(1, results[0])
    send_home(2, results[1])
    send_rows(0, results[2])
    received.append(swap(results[3]))
    (grads,) = turn([added_halves(ours[0], received[0])])
    results = turn([gathered(0), added(partial[1], BF)], (), [received[1]])
    send_side(0, results[0])
    send_home(1, results[1])
    results = turn([added([ours[1], received[1]], BF)])
    grads = [*grads, results[0][0]]
    parts = [*partial[0], partial[1], partial[2], partial[3]]
    if halves > 1:
        results = turn([added(parts, F32)])
        parts = [summed(results[0][0])]
    token_grad = finish(parts, down, deps())
    return (token_grad, grads[0][None], grads[1][None], grads[2][None])


def solution(mesh):
    in_specs = (
        P(("expert", "dp"), "half"),
        P(("expert", "dp"), "half"),
        P(("expert", "dp"), None),
        P(("expert", "dp"), None),
        P(("expert", "dp"), None),
        P("half", "dp"),
        P("dp", "half"),
        P("expert", "dp", "half"),
        P("expert", "dp", "half"),
        P("expert", "half", "dp"),
    )
    out_specs = (
        P(("expert", "dp"), "half"),
        P("expert", "dp", "half"),
        P("expert", "dp", "half"),
        P("expert", "half", "dp"),
    )
    return jax.shard_map(
        on_device, mesh=mesh, in_specs=in_specs, out_specs=out_specs, check_vma=False
    )
```

profile of v0, /device:TPU:0, one launch (start us, length us, event | category | flops | bytes accessed | tf_op | source)
XLA Modules:
  0.0 152.0 jit_solution(9646822457034286712)
XLA Ops:
  0.6 0.5 collective-permute-start
  1.2 3.5 %convolution_convert_fusion.3.own_ref = bf16[128,512]{1,0:T(8,128)(2,1)S(1)} fusion(bf16[128,4096]{1,0:T(8,128)(2,1)} %param.10, bf16[4096,512]{1,0:T(8,128)(2,1)} %refs_5_), kind=kOutput, calls=%fused_computation.3 | convolution fusion | flops 536936448 | bytes 5373952 | tf_op jit(solution)/shard_map/dot_general | solution.py:483
  4.8 0.7 convolution_convert_fusion.2.refs_3_
  5.6 1.3 collective-permute-done.1.other_ref
  8.1 2.8 %collective-permute-start.9 = (bf16[144,1024]{1,0:T(8,128)(2,1)S(1)}, bf16[144,1024]{1,0:T(8,128)(2,1)S(1)}, u32[]{:S(2)}, u32[]{:S(2)}) collective-permute-start(bf16[144,1024]{1,0:T(8,128)(2,1)S(1)} %join_rows.2.block_ref.refs_0_.refs_2_), channel_id=1, source_target_pairs={{0,8},{2,10},{4,12},{6,14},{8,16},{10,18},{12,20},{14,22},{16,24},... | collective-permute-start | bytes 884744 | tf_op jit(solution)/shard_map/plane_l1/ppermute | solution.py:449
  10.9 3.7 %convolution_convert_fusion.1.own_ref = bf16[128,512]{1,0:T(8,128)(2,1)S(1)} fusion(bf16[128,4096]{1,0:T(8,128)(2,1)S(1)} %copy-done.14, bf16[512,4096]{1,0:T(8,128)(2,1)} %param.16), kind=kOutput, calls=%fused_computation.1 | convolution fusion | flops 536936448 | bytes 5373952 | tf_op jit(solution)/shard_map/dot_general | solution.py:483
  14.6 1.5 %convolution_convert_fusion.refs_0_ = bf16[128,512]{1,0:T(8,128)(2,1)S(1)} fusion(bf16[128,4096]{1,0:T(8,128)(2,1)S(1)} %collective-permute-done.3, bf16[512,4096]{1,0:T(8,128)(2,1)S(1)} %copy-done.13), kind=kOutput, calls=%fused_computation | convolution fusion | flops 536936448 | bytes 5373952 | tf_op jit(solution)/shard_map/dot_general | solution.py:483
  16.3 1.5 collective-permute-start.2
  17.9 3.6 %collective-permute-start.7 = (bf16[144,1024]{1,0:T(8,128)(2,1)S(1)}, bf16[144,1024]{1,0:T(8,128)(2,1)S(1)}, u32[]{:S(2)}, u32[]{:S(2)}) collective-permute-start(bf16[144,1024]{1,0:T(8,128)(2,1)S(1)} %tie_rows.5.refs_0_), channel_id=1, source_target_pairs={{0,24},{2,26},{4,28},{6,30},{8,0},{10,2},{12,4},{14,6},{16,8},{18,... | collective-permute-start | bytes 884744 | tf_op jit(solution)/shard_map/plane_l3/ppermute | solution.py:449
  21.5 1.5 collective-permute-start.10
  23.0 3.1 %collective-permute-done.2.refs_1_.refs_3_ = bf16[144,1024]{1,0:T(8,128)(2,1)S(1)} collective-permute-done((bf16[144,1024]{1,0:T(8,128)(2,1)S(1)}, bf16[144,1024]{1,0:T(8,128)(2,1)S(1)}, u32[]{:S(2)}, u32[]{:S(2)}) %collective-permute-start.2) | collective-permute-done | bytes 294944 | tf_op jit(solution)/shard_map/side_l0/ppermute | solution.py:460
  26.1 0.5 select_latent.4
  26.6 2.7 %collective-permute-start.15 = (bf16[144,1024]{1,0:T(8,128)(2,1)S(1)}, bf16[144,1024]{1,0:T(8,128)(2,1)S(1)}, u32[]{:S(2)}, u32[]{:S(2)}) collective-permute-start(bf16[144,1024]{1,0:T(8,128)(2,1)S(1)} %tie_rows.6.refs_4_), channel_id=1, source_target_pairs={{0,16},{2,18},{4,20},{6,22},{8,24},{10,26},{12,28},{14,30},{16,0},... | collective-permute-start | bytes 884744 | tf_op jit(solution)/shard_map/plane_l2/ppermute | solution.py:449
  29.3 1.5 collective-permute-start.13
  30.8 1.5 collective-permute-start.8
  32.8 1.7 %collective-permute-start.14 = (bf16[144,1024]{1,0:T(8,128)(2,1)S(1)}, bf16[144,1024]{1,0:T(8,128)(2,1)S(1)}, u32[]{:S(2)}, u32[]{:S(2)}) collective-permute-start(bf16[144,1024]{1,0:T(8,128)(2,1)S(1)} %get-tuple-element.82), channel_id=1, source_target_pairs={{0,4},{2,6},{4,0},{6,2},{8,12},{10,14},{12,8},{14,10},{16,20},{18,... | collective-permute-start | bytes 884744 | tf_op jit(solution)/shard_map/piece_l1/ppermute | solution.py:464
  34.5 1.5 collective-permute-start.6
  36.0 6.0 %collective-permute-done.15.refs_6_.refs_1_.refs_0_.refs_2_ = bf16[144,1024]{1,0:T(8,128)(2,1)S(1)} collective-permute-done((bf16[144,1024]{1,0:T(8,128)(2,1)S(1)}, bf16[144,1024]{1,0:T(8,128)(2,1)S(1)}, u32[]{:S(2)}, u32[]{:S(2)}) %collective-permute-start.15) | collective-permute-done | bytes 294944 | tf_op jit(solution)/shard_map/plane_l2/ppermute | solution.py:449
  42.0 1.5 collective-permute-start.17
  43.5 0.5 select_latent.6
  44.0 1.6 %collective-permute-start.18 = (bf16[144,1024]{1,0:T(8,128)(2,1)S(1)}, bf16[144,1024]{1,0:T(8,128)(2,1)S(1)}, u32[]{:S(2)}, u32[]{:S(2)}) collective-permute-start(bf16[144,1024]{1,0:T(8,128)(2,1)S(1)} %get-tuple-element.86), channel_id=1, source_target_pairs={{0,4},{2,6},{4,0},{6,2},{8,12},{10,14},{12,8},{14,10},{16,20},{18,... | collective-permute-start | bytes 884744 | tf_op jit(solution)/shard_map/piece_l3/ppermute | solution.py:464
  46.1 4.7 %forward_rows.2 = (bf16[576,1024]{1,0:T(8,128)(2,1)S(1)}, bf16[576,1536]{1,0:T(8,128)(2,1)S(1)}, bf16[576,1536]{1,0:T(8,128)(2,1)S(1)}, bf16[576,1536]{1,0:T(8,128)(2,1)S(1)}) custom-call(bf16[144,1024]{1,0:T(8,128)(2,1)S(1)} %get-tuple-element.78.refs_0_, bf16[144,1024]{1,0:T(8,128)(2,1)S(1)} %collective-permute-done.13.refs_5_.refs_1_, ...), custom_call_target="tpu_custom_call" | custom-call | flops 3623878656 | bytes 11599873 | tf_op jit(solution)/shard_map/forward_rows/pallas_call | solution.py:279
  50.8 4.8 %collective-permute-done.19.refs_6_.refs_1_.refs_2_ = bf16[128,1024]{1,0:T(8,128)(2,1)S(1)} collective-permute-done((bf16[128,1024]{1,0:T(8,128)(2,1)S(1)}, bf16[128,1024]{1,0:T(8,128)(2,1)S(1)}, u32[]{:S(2)}, u32[]{:S(2)}) %collective-permute-start.19) | collective-permute-done | bytes 262176 | tf_op jit(solution)/shard_map/plane_b2/ppermute | solution.py:449
  55.7 0.5 select_latent.7
  56.3 1.6 %collective-permute-start.16 = (bf16[144,1024]{1,0:T(8,128)(2,1)S(1)}, bf16[144,1024]{1,0:T(8,128)(2,1)S(1)}, u32[]{:S(2)}, u32[]{:S(2)}) collective-permute-start(bf16[144,1024]{1,0:T(8,128)(2,1)S(1)} %get-tuple-element.84), channel_id=1, source_target_pairs={{0,4},{2,6},{4,0},{6,2},{8,12},{10,14},{12,8},{14,10},{16,20},{18,... | collective-permute-start | bytes 884744 | tf_op jit(solution)/shard_map/piece_b0/ppermute | solution.py:464
  57.9 0.5 collective-permute-start.24
  58.4 1.2 collective-permute-start.22
  59.6 1.5 collective-permute-start.25
  61.0 5.4 %collective-permute-done.22.refs_6_.refs_2_ = bf16[128,1024]{1,0:T(8,128)(2,1)S(1)} collective-permute-done((bf16[128,1024]{1,0:T(8,128)(2,1)S(1)}, bf16[128,1024]{1,0:T(8,128)(2,1)S(1)}, u32[]{:S(2)}, u32[]{:S(2)}) %collective-permute-start.22) | collective-permute-done | bytes 262176 | tf_op jit(solution)/shard_map/plane_b3/ppermute | solution.py:449
  66.5 1.5 collective-permute-start.23
  68.7 1.6 %collective-permute-start.26 = (bf16[144,1024]{1,0:T(8,128)(2,1)S(1)}, bf16[144,1024]{1,0:T(8,128)(2,1)S(1)}, u32[]{:S(2)}, u32[]{:S(2)}) collective-permute-start(bf16[144,1024]{1,0:T(8,128)(2,1)S(1)} %get-tuple-element.92), channel_id=1, source_target_pairs={{0,4},{2,6},{4,0},{6,2},{8,12},{10,14},{12,8},{14,10},{16,20},{18,... | collective-permute-start | bytes 884744 | tf_op jit(solution)/shard_map/piece_b2/ppermute | solution.py:464
  70.3 2.2 %collective-permute-done.24.refs_3_.refs_5_ = bf16[144,1024]{1,0:T(8,128)(2,1)S(1)} collective-permute-done((bf16[144,1024]{1,0:T(8,128)(2,1)S(1)}, bf16[144,1024]{1,0:T(8,128)(2,1)S(1)}, u32[]{:S(2)}, u32[]{:S(2)}) %collective-permute-start.24) | collective-permute-done | bytes 294944 | tf_op jit(solution)/shard_map/piece_l2/ppermute | solution.py:464
  72.5 4.7 %forward_rows.3 = (bf16[576,1024]{1,0:T(8,128)(2,1)S(1)}, bf16[576,1536]{1,0:T(8,128)(2,1)S(1)}, bf16[576,1536]{1,0:T(8,128)(2,1)S(1)}, bf16[576,1536]{1,0:T(8,128)(2,1)S(1)}) custom-call(bf16[144,1024]{1,0:T(8,128)(2,1)S(1)} %get-tuple-element.81.refs_4_.refs_0_, bf16[144,1024]{1,0:T(8,128)(2,1)S(1)} %collective-permute-done.18.refs_5_.refs_1_, ...), custom_call_target="tpu_custom_call" | custom-call | flops 3623878656 | bytes 11599873 | tf_op jit(solution)/shard_map/forward_rows/pallas_call | solution.py:279
  77.2 0.5 select_back.6
  77.7 1.6 %collective-permute-start.29 = (bf16[144,1024]{1,0:T(8,128)(2,1)S(1)}, bf16[144,1024]{1,0:T(8,128)(2,1)S(1)}, u32[]{:S(2)}, u32[]{:S(2)}) collective-permute-start(bf16[144,1024]{1,0:T(8,128)(2,1)S(1)} %get-tuple-element.98), channel_id=1, source_target_pairs={{0,4},{2,6},{4,0},{6,2},{8,12},{10,14},{12,8},{14,10},{16,20},{18,... | collective-permute-start | bytes 884744 | tf_op jit(solution)/shard_map/piece_b3/ppermute | solution.py:464
  79.3 1.5 collective-permute-start.21
  80.8 5.6 %collective-permute-done.21.refs_3_ = bf16[128,1024]{1,0:T(8,128)(2,1)S(1)} collective-permute-done((bf16[128,1024]{1,0:T(8,128)(2,1)S(1)}, bf16[128,1024]{1,0:T(8,128)(2,1)S(1)}, u32[]{:S(2)}, u32[]{:S(2)}) %collective-permute-start.21) | collective-permute-done | bytes 262176 | tf_op jit(solution)/shard_map/side_b1/ppermute | solution.py:460
  86.9 0.6 collective-permute-start.28
  87.5 5.8 %backward_rows.2 = (bf16[576,1024]{1,0:T(8,128)(2,1)S(1)}, bf16[576,1536]{1,0:T(8,128)(2,1)S(1)}, bf16[576,1536]{1,0:T(8,128)(2,1)S(1)}, bf16[144,1024]{1,0:T(8,...) custom-call(bf16[144,1024]{1,0:T(8,128)(2,1)S(1)} %get-tuple-element.91.r, ...), custom_call_target="tpu_custom_call" | custom-call | flops 5435817984 | bytes 16515073 | tf_op jit(solution)/shard_map/backward_rows/pallas_call | solution.py:324
  93.3 1.6 %collective-permute-start.30 = (bf16[144,1024]{1,0:T(8,128)(2,1)S(1)}, bf16[144,1024]{1,0:T(8,128)(2,1)S(1)}, u32[]{:S(2)}, u32[]{:S(2)}) collective-permute-start(bf16[144,1024]{1,0:T(8,128)(2,1)S(1)} %get-tuple-element.106), channel_id=1, source_target_pairs={{0,4},{2,6},{4,0},{6,2},{8,12},{10,14},{12,8},{14,10},{16,20},{18,... | collective-permute-start | bytes 884744 | tf_op jit(solution)/shard_map/piece_r3/ppermute | solution.py:464
  94.9 5.8 %backward_rows.3 = (bf16[576,1024]{1,0:T(8,128)(2,1)S(1)}, bf16[576,1536]{1,0:T(8,128)(2,1)S(1)}, bf16[576,1536]{1,0:T(8,128)(2,1)S(1)}, bf16[144,1024]{1,0:T(8,...) custom-call(bf16[144,1024]{1,0:T(8,128)(2,1)S(1)} %get-tuple-element.83.r, ...), custom_call_target="tpu_custom_call" | custom-call | flops 5435817984 | bytes 16515073 | tf_op jit(solution)/shard_map/backward_rows/pallas_call | solution.py:324
  100.8 0.5 return_rows.6
  101.3 1.6 %collective-permute-start.32 = (bf16[128,1024]{1,0:T(8,128)(2,1)S(1)}, bf16[128,1024]{1,0:T(8,128)(2,1)S(1)}, u32[]{:S(2)}, u32[]{:S(2)}) collective-permute-start(bf16[128,1024]{1,0:T(8,128)(2,1)S(1)} %get-tuple-element.111), channel_id=1, source_target_pairs={{0,2},{2,0},{4,6},{6,4},{8,10},{10,8},{12,14},{14,12},{16,18},{18,... | collective-permute-start | bytes 786440 | tf_op jit(solution)/shard_map/side_r3/ppermute | solution.py:460
  102.9 0.9 collective-permute-start.31
  103.8 7.9 %weight_grads.2 = (bf16[1024,1536]{1,0:T(8,128)(2,1)S(1)}, bf16[1536,512]{1,0:T(8,128)(2,1)S(1)}) custom-call(bf16[576,1024]{1,0:T(8,128)(2,1)S(1)} %get-tuple-element.90.refs_4_.refs_0_, bf16[576,1024]{1,0:T(8,128)(2,1)S(1)} %get-tuple-element.101.refs_12_.refs_1_, bf16[576,1536]{1,0:T(8,128)(2,1)S(1)} %get-tuple-element.113.refs_2_, ...), custom_call_target="tpu_custom_call" | custom-call | flops 5435817984 | bytes 15335425 | tf_op jit(solution)/shard_map/weight_grads/pallas_call | solution.py:370
  111.9 0.6 return_rows.7
  112.6 0.6 collective-permute-start.34
  113.4 1.2 collective-permute-start.33
  114.6 7.9 %weight_grads.3 = (bf16[1024,1536]{1,0:T(8,128)(2,1)S(1)}, bf16[1536,512]{1,0:T(8,128)(2,1)S(1)}) custom-call(bf16[576,1024]{1,0:T(8,128)(2,1)S(1)} %get-tuple-element.90.refs_4_.refs_0_, bf16[576,1024]{1,0:T(8,128)(2,1)S(1)} %copy-done.12, bf16[576,1536]{1,0:T(8,128)(2,1)S(1)} %get-tuple-element.113.refs_2_, ...), custom_call_target="tpu_custom_call" | custom-call | flops 5435817984 | bytes 15335425 | tf_op jit(solution)/shard_map/weight_grads/pallas_call | solution.py:370
  122.5 0.8 collective-permute-done.35.refs_9_.refs_4_
  123.4 0.6 return_rows.8
  124.0 1.2 collective-permute-start.37
  125.2 1.5 collective-permute-start.38
  127.1 2.3 %return_rows.9 = (bf16[512,1536]{1,0:T(8,128)(2,1)}, bf16[512,1536]{1,0:T(8,128)(2,1)}) custom-call(bf16[1024,1536]{1,0:T(8,128)(2,1)S(1)} %get-tuple-element.126.refs_8_.refs_0_, bf16[1024,1536]{1,0:T(8,128)(2,1)S(1)} %collective-permute-done.36.refs_10_.refs_1_, f32[128,1024]{1,0:T(8,128)S(1)} %get-tuple-element.130.refs_2_.refs_4_), custom_call_target="tpu_custom_call" | custom-call | flops 1 | bytes 12582913 | tf_op jit(solution)/shard_map/return_rows/pallas_call | solution.py:185
  129.4 4.2 %collective-permute-done.38.refs_5_ = bf16[128,1024]{1,0:T(8,128)(2,1)S(1)} collective-permute-done((bf16[128,1024]{1,0:T(8,128)(2,1)S(1)}, bf16[128,1024]{1,0:T(8,128)(2,1)S(1)}, u32[]{:S(2)}, u32[]{:S(2)}) %collective-permute-start.38) | collective-permute-done | bytes 262176 | tf_op jit(solution)/shard_map/side_r1/ppermute | solution.py:460
  133.6 1.4 copy-done.2
  135.0 0.6 return_rows.10
  135.6 1.6 %collective-permute-start.40 = (bf16[128,1024]{1,0:T(8,128)(2,1)S(1)}, bf16[128,1024]{1,0:T(8,128)(2,1)S(1)}, u32[]{:S(2)}, u32[]{:S(2)}) collective-permute-start(bf16[128,1024]{1,0:T(8,128)(2,1)S(1)} %get-tuple-element.135), channel_id=1, source_target_pairs={{0,2},{2,0},{4,6},{6,4},{8,10},{10,8},{12,14},{14,12},{16,18},{18,... | collective-permute-start | bytes 786440 | tf_op jit(solution)/shard_map/side_r0/ppermute | solution.py:460
  137.2 2.6 %collective-permute-start.41 = (bf16[128,1024]{1,0:T(8,128)(2,1)S(1)}, bf16[128,1024]{1,0:T(8,128)(2,1)S(1)}, u32[]{:S(2)}, u32[]{:S(2)}) collective-permute-start(bf16[128,1024]{1,0:T(8,128)(2,1)S(1)} %get-tuple-element.136), channel_id=1, source_target_pairs={{0,24},{2,26},{4,28},{6,30},{8,0},{10,2},{12,4},{14,6},{16,8},{18,... | collective-permute-start | bytes 786440 | tf_op jit(solution)/shard_map/plane_r1/ppermute | solution.py:449
  139.8 1.5 return_rows.11.refs_7_
  141.3 2.0 %collective-permute-done.40.refs_1_ = bf16[128,1024]{1,0:T(8,128)(2,1)S(1)} collective-permute-done((bf16[128,1024]{1,0:T(8,128)(2,1)S(1)}, bf16[128,1024]{1,0:T(8,128)(2,1)S(1)}, u32[]{:S(2)}, u32[]{:S(2)}) %collective-permute-start.40) | collective-permute-done | bytes 262176 | tf_op jit(solution)/shard_map/side_r0/ppermute | solution.py:460
  143.3 3.5 %collective-permute-done.41.refs_2_ = bf16[128,1024]{1,0:T(8,128)(2,1)S(1)} collective-permute-done((bf16[128,1024]{1,0:T(8,128)(2,1)S(1)}, bf16[128,1024]{1,0:T(8,128)(2,1)S(1)}, u32[]{:S(2)}, u32[]{:S(2)}) %collective-permute-start.41) | collective-permute-done | bytes 262176 | tf_op jit(solution)/shard_map/plane_r1/ppermute | solution.py:449
  146.8 1.4 copy-done.1
  148.2 3.8 %token_grad.1 = bf16[128,4096]{1,0:T(8,128)(2,1)} custom-call(f32[128,1024]{1,0:T(8,128)S(1)} %get-tuple-element.134.refs_2_.refs_0_, bf16[128,1024]{1,0:T(8,128)(2,1)S(1)} %collective-permute-done.40.refs_1_, bf16[128,1024]{1,0:T(8,128)(2,1)S(1)} %collective-permute-done.41.refs_2_, bf16[128,1024]{1,0:T(8,128)(2,1)S(1)} %collective-permute-done.42.refs_3_, ...), custom_call_target="tpu_custom_call" | custom-call | flops 1073741824 | bytes 8388609 | tf_op jit(solution)/shard_map/token_grad/pallas_call | solution.py:411
  (85 shorter events, 4.9 us)
Async XLA Ops:
  0.6 4.1 %copy-start = (bf16[4096,512]{1,0:T(8,128)(2,1)S(1)}, bf16[4096,512]{1,0:T(8,128)(2,1)}, u32[]{:S(2)}) copy-start(bf16[4096,512]{1,0:T(8,128)(2,1)} %refs_5_) | copy-start | bytes 12582916
  0.6 4.1 %collective-permute-start = (bf16[128,4096]{1,0:T(8,128)(2,1)}, bf16[128,4096]{1,0:T(8,128)(2,1)S(1)}, u32[]{:S(2)}, u32[]{:S(2)}) collective-permute-start(bf16[128,4096]{1,0:T(8,128)(2,1)} %param.10), channel_id=1, source_target_pairs={{0,1},{1,0},{2,3},{3,2},{4,5},{5,4},{6,7},{7,6},{8,9},{9,8},{10,11... | collective-permute-start | bytes 3145736 | tf_op jit(solution)/shard_map/ppermute | solution.py:446
  4.6 2.2 %copy-start.3 = (s32[128,8]{0,1:T(8,128)S(1)}, s32[128,8]{0,1:T(8,128)}, u32[]{:S(2)}) copy-start(s32[128,8]{0,1:T(8,128)} %param.12) | copy-start | bytes 12292
  4.7 2.2 %copy-start.4 = (s32[128,8]{0,1:T(8,128)S(1)}, s32[128,8]{0,1:T(8,128)}, u32[]{:S(2)}) copy-start(s32[128,8]{0,1:T(8,128)} %param.13) | copy-start | bytes 12292
  4.7 2.2 %copy-start.5 = (f32[128,8]{0,1:T(8,128)S(1)}, f32[128,8]{0,1:T(8,128)}, u32[]{:S(2)}) copy-start(f32[128,8]{0,1:T(8,128)} %param.14) | copy-start | bytes 12292
  4.7 2.3 %copy-start.6 = (bf16[1,512,1536]{2,1,0:T(8,128)(2,1)S(1)}, bf16[1,512,1536]{2,1,0:T(8,128)(2,1)}, u32[]{:S(2)}) copy-start(bf16[1,512,1536]{2,1,0:T(8,128)(2,1)} %param.17) | copy-start | bytes 4718596
  4.7 2.5 %copy-start.14 = (bf16[128,4096]{1,0:T(8,128)(2,1)S(1)}, bf16[128,4096]{1,0:T(8,128)(2,1)}, u32[]{:S(2)}) copy-start(bf16[128,4096]{1,0:T(8,128)(2,1)} %param.11) | copy-start | bytes 3145732
  4.7 2.8 %copy-start.8 = (bf16[1,1536,512]{2,1,0:T(8,128)(2,1)S(1)}, bf16[1,1536,512]{2,1,0:T(8,128)(2,1)}, u32[]{:S(2)}) copy-start(bf16[1,1536,512]{2,1,0:T(8,128)(2,1)} %param.19) | copy-start | bytes 4718596
  4.7 3.0 %copy-start.7 = (bf16[1,512,1536]{2,1,0:T(8,128)(2,1)S(1)}, bf16[1,512,1536]{2,1,0:T(8,128)(2,1)}, u32[]{:S(2)}) copy-start(bf16[1,512,1536]{2,1,0:T(8,128)(2,1)} %param.18) | copy-start | bytes 4718596
  5.5 1.4 collective-permute-start.1
  6.9 7.7 %copy-start.13 = (bf16[512,4096]{1,0:T(8,128)(2,1)S(1)}, bf16[512,4096]{1,0:T(8,128)(2,1)}, u32[]{:S(2)}) copy-start(bf16[512,4096]{1,0:T(8,128)(2,1)} %param.16) | copy-start | bytes 12582916
  7.0 9.4 %collective-permute-start.5 = (bf16[512,1536]{1,0:T(8,128)(2,1)S(1)}, bf16[512,1536]{1,0:T(8,128)(2,1)S(1)}, u32[]{:S(2)}, u32[]{:S(2)}) collective-permute-start(bf16[512,1536]{1,0:T(8,128)(2,1)S(1)} %bitcast.22), channel_id=1, source_target_pairs={{0,1},{1,0},{2,3},{3,2},{4,5},{5,4},{6,7},{7,6},{8,9},{9,8},{10,11... | collective-permute-start | bytes 4718600 | tf_op jit(solution)/shard_map/ppermute | solution.py:446
  7.2 7.4 %collective-permute-start.3 = (bf16[128,4096]{1,0:T(8,128)(2,1)S(1)}, bf16[128,4096]{1,0:T(8,128)(2,1)S(1)}, u32[]{:S(2)}, u32[]{:S(2)}) collective-permute-start(bf16[128,4096]{1,0:T(8,128)(2,1)S(1)} %copy-done.14), channel_id=1, source_target_pairs={{0,1},{1,0},{2,3},{3,2},{4,5},{5,4},{6,7},{7,6},{8,9},{9,8},{10,11... | collective-permute-start | bytes 3145736 | tf_op jit(solution)/shard_map/ppermute | solution.py:446
  7.5 18.6 %collective-permute-start.12 = (bf16[1536,512]{1,0:T(8,128)(2,1)S(1)}, bf16[1536,512]{1,0:T(8,128)(2,1)S(1)}, u32[]{:S(2)}, u32[]{:S(2)}) collective-permute-start(bf16[1536,512]{1,0:T(8,128)(2,1)S(1)} %bitcast.32), channel_id=1, source_target_pairs={{0,1},{1,0},{2,3},{3,2},{4,5},{5,4},{6,7},{7,6},{8,9},{9,8},{10,11... | collective-permute-start | bytes 4718600 | tf_op jit(solution)/shard_map/ppermute | solution.py:446
  7.7 18.5 %collective-permute-start.11 = (bf16[512,1536]{1,0:T(8,128)(2,1)S(1)}, bf16[512,1536]{1,0:T(8,128)(2,1)S(1)}, u32[]{:S(2)}, u32[]{:S(2)}) collective-permute-start(bf16[512,1536]{1,0:T(8,128)(2,1)S(1)} %bitcast.27), channel_id=1, source_target_pairs={{0,1},{1,0},{2,3},{3,2},{4,5},{5,4},{6,7},{7,6},{8,9},{9,8},{10,11... | collective-permute-start | bytes 4718600 | tf_op jit(solution)/shard_map/ppermute | solution.py:446
  8.1 13.4 %collective-permute-start.9 = (bf16[144,1024]{1,0:T(8,128)(2,1)S(1)}, bf16[144,1024]{1,0:T(8,128)(2,1)S(1)}, u32[]{:S(2)}, u32[]{:S(2)}) collective-permute-start(bf16[144,1024]{1,0:T(8,128)(2,1)S(1)} %join_rows.2.block_ref.refs_0_.refs_2_), channel_id=1, source_target_pairs={{0,8},{2,10},{4,12},{6,14},{8,16},{10,18},{12,20},{14,22},{16,24},... | collective-permute-start | bytes 884744 | tf_op jit(solution)/shard_map/plane_l1/ppermute | solution.py:449
  16.2 1.7 %collective-permute-start.4 = (bf16[128,512]{1,0:T(8,128)(2,1)S(1)}, bf16[128,512]{1,0:T(8,128)(2,1)S(1)}, u32[]{:S(2)}, u32[]{:S(2)}) collective-permute-start(bf16[128,512]{1,0:T(8,128)(2,1)S(1)} %convolution_convert_fusion.refs_0_), channel_id=1, source_target_pairs={{0,1},{1,0},{2,3},{3,2},{4,5},{5,4},{6,7},{7,6},{8,9},{9,8},{10,11... | collective-permute-start | bytes 393224 | tf_op jit(solution)/shard_map/ppermute | solution.py:446
  16.3 9.8 %collective-permute-start.2 = (bf16[144,1024]{1,0:T(8,128)(2,1)S(1)}, bf16[144,1024]{1,0:T(8,128)(2,1)S(1)}, u32[]{:S(2)}, u32[]{:S(2)}) collective-permute-start(bf16[144,1024]{1,0:T(8,128)(2,1)S(1)} %join_rows.2.block_ref.refs_0_.refs_2_), channel_id=1, source_target_pairs={{0,2},{2,0},{4,6},{6,4},{8,10},{10,8},{12,14},{14,12},{16,18},{18,... | collective-permute-start | bytes 884744 | tf_op jit(solution)/shard_map/side_l0/ppermute | solution.py:460
  17.9 13.0 %collective-permute-start.7 = (bf16[144,1024]{1,0:T(8,128)(2,1)S(1)}, bf16[144,1024]{1,0:T(8,128)(2,1)S(1)}, u32[]{:S(2)}, u32[]{:S(2)}) collective-permute-start(bf16[144,1024]{1,0:T(8,128)(2,1)S(1)} %tie_rows.5.refs_0_), channel_id=1, source_target_pairs={{0,24},{2,26},{4,28},{6,30},{8,0},{10,2},{12,4},{14,6},{16,8},{18,... | collective-permute-start | bytes 884744 | tf_op jit(solution)/shard_map/plane_l3/ppermute | solution.py:449
  21.5 10.8 %collective-permute-start.10 = (bf16[144,1024]{1,0:T(8,128)(2,1)S(1)}, bf16[144,1024]{1,0:T(8,128)(2,1)S(1)}, u32[]{:S(2)}, u32[]{:S(2)}) collective-permute-start(bf16[144,1024]{1,0:T(8,128)(2,1)S(1)} %collective-permute-done.9.refs_5_.refs_1_.refs_0_.refs_2_), channel_id=1, source_target_pairs={{0,2},{2,0},{4,6},{6,4},{8,10},{10,8},{12,14},{14,12},{16,18},{18,... | collective-permute-start | bytes 884744 | tf_op jit(solution)/shard_map/side_l1/ppermute | solution.py:460
  26.6 15.4 %collective-permute-start.15 = (bf16[144,1024]{1,0:T(8,128)(2,1)S(1)}, bf16[144,1024]{1,0:T(8,128)(2,1)S(1)}, u32[]{:S(2)}, u32[]{:S(2)}) collective-permute-start(bf16[144,1024]{1,0:T(8,128)(2,1)S(1)} %tie_rows.6.refs_4_), channel_id=1, source_target_pairs={{0,16},{2,18},{4,20},{6,22},{8,24},{10,26},{12,28},{14,30},{16,0},... | collective-permute-start | bytes 884744 | tf_op jit(solution)/shard_map/plane_l2/ppermute | solution.py:449
  29.3 12.7 %collective-permute-start.13 = (bf16[144,1024]{1,0:T(8,128)(2,1)S(1)}, bf16[144,1024]{1,0:T(8,128)(2,1)S(1)}, u32[]{:S(2)}, u32[]{:S(2)}) collective-permute-start(bf16[144,1024]{1,0:T(8,128)(2,1)S(1)} %get-tuple-element.80), channel_id=1, source_target_pairs={{0,4},{2,6},{4,0},{6,2},{8,12},{10,14},{12,8},{14,10},{16,20},{18,... | collective-permute-start | bytes 884744 | tf_op jit(solution)/shard_map/piece_l0/ppermute | solution.py:464
  30.8 12.7 %collective-permute-start.8 = (bf16[144,1024]{1,0:T(8,128)(2,1)S(1)}, bf16[144,1024]{1,0:T(8,128)(2,1)S(1)}, u32[]{:S(2)}, u32[]{:S(2)}) collective-permute-start(bf16[144,1024]{1,0:T(8,128)(2,1)S(1)} %collective-permute-done.7.refs_5_.refs_1_.refs_0_.refs_2_), channel_id=1, source_target_pairs={{0,2},{2,0},{4,6},{6,4},{8,10},{10,8},{12,14},{14,12},{16,18},{18,... | collective-permute-start | bytes 884744 | tf_op jit(solution)/shard_map/side_l3/ppermute | solution.py:460
  32.8 12.8 %collective-permute-start.14 = (bf16[144,1024]{1,0:T(8,128)(2,1)S(1)}, bf16[144,1024]{1,0:T(8,128)(2,1)S(1)}, u32[]{:S(2)}, u32[]{:S(2)}) collective-permute-start(bf16[144,1024]{1,0:T(8,128)(2,1)S(1)} %get-tuple-element.82), channel_id=1, source_target_pairs={{0,4},{2,6},{4,0},{6,2},{8,12},{10,14},{12,8},{14,10},{16,20},{18,... | collective-permute-start | bytes 884744 | tf_op jit(solution)/shard_map/piece_l1/ppermute | solution.py:464
  34.5 11.1 %collective-permute-start.6 = (bf16[128,1024]{1,0:T(8,128)(2,1)S(1)}, bf16[128,1024]{1,0:T(8,128)(2,1)S(1)}, u32[]{:S(2)}, u32[]{:S(2)}) collective-permute-start(bf16[128,1024]{1,0:T(8,128)(2,1)S(1)} %join_rows.3.refs_4_.block_ref.refs_2_), channel_id=1, source_target_pairs={{0,2},{2,0},{4,6},{6,4},{8,10},{10,8},{12,14},{14,12},{16,18},{18,... | collective-permute-start | bytes 786440 | tf_op jit(solution)/shard_map/side_b0/ppermute | solution.py:460
  42.0 13.7 %collective-permute-start.19 = (bf16[128,1024]{1,0:T(8,128)(2,1)S(1)}, bf16[128,1024]{1,0:T(8,128)(2,1)S(1)}, u32[]{:S(2)}, u32[]{:S(2)}) collective-permute-start(bf16[128,1024]{1,0:T(8,128)(2,1)S(1)} %tie_rows.7.refs_4_), channel_id=1, source_target_pairs={{0,16},{2,18},{4,20},{6,22},{8,24},{10,26},{12,28},{14,30},{16,0},... | collective-permute-start | bytes 786440 | tf_op jit(solution)/shard_map/plane_b2/ppermute | solution.py:449
  42.0 13.7 %collective-permute-start.17 = (bf16[144,1024]{1,0:T(8,128)(2,1)S(1)}, bf16[144,1024]{1,0:T(8,128)(2,1)S(1)}, u32[]{:S(2)}, u32[]{:S(2)}) collective-permute-start(bf16[144,1024]{1,0:T(8,128)(2,1)S(1)} %collective-permute-done.15.refs_6_.refs_1_.refs_0_.refs_2_), channel_id=1, source_target_pairs={{0,2},{2,0},{4,6},{6,4},{8,10},{10,8},{12,14},{14,12},{16,18},{18,... | collective-permute-start | bytes 884744 | tf_op jit(solution)/shard_map/side_l2/ppermute | solution.py:460
  44.0 11.7 %collective-permute-start.18 = (bf16[144,1024]{1,0:T(8,128)(2,1)S(1)}, bf16[144,1024]{1,0:T(8,128)(2,1)S(1)}, u32[]{:S(2)}, u32[]{:S(2)}) collective-permute-start(bf16[144,1024]{1,0:T(8,128)(2,1)S(1)} %get-tuple-element.86), channel_id=1, source_target_pairs={{0,4},{2,6},{4,0},{6,2},{8,12},{10,14},{12,8},{14,10},{16,20},{18,... | collective-permute-start | bytes 884744 | tf_op jit(solution)/shard_map/piece_l3/ppermute | solution.py:464
  56.2 30.2 %collective-permute-start.27 = (bf16[4096,512]{1,0:T(8,128)(2,1)S(1)}, bf16[4096,512]{1,0:T(8,128)(2,1)S(1)}, u32[]{:S(2)}, u32[]{:S(2)}) collective-permute-start(bf16[4096,512]{1,0:T(8,128)(2,1)S(1)} %copy-done), channel_id=1, source_target_pairs={{0,1},{1,0},{2,3},{3,2},{4,5},{5,4},{6,7},{7,6},{8,9},{9,8},{10,11... | collective-permute-start | bytes 12582920 | tf_op jit(solution)/shard_map/ppermute | solution.py:446
  56.3 11.9 %collective-permute-start.16 = (bf16[144,1024]{1,0:T(8,128)(2,1)S(1)}, bf16[144,1024]{1,0:T(8,128)(2,1)S(1)}, u32[]{:S(2)}, u32[]{:S(2)}) collective-permute-start(bf16[144,1024]{1,0:T(8,128)(2,1)S(1)} %get-tuple-element.84), channel_id=1, source_target_pairs={{0,4},{2,6},{4,0},{6,2},{8,12},{10,14},{12,8},{14,10},{16,20},{18,... | collective-permute-start | bytes 884744 | tf_op jit(solution)/shard_map/piece_b0/ppermute | solution.py:464
  57.9 14.6 %collective-permute-start.24 = (bf16[144,1024]{1,0:T(8,128)(2,1)S(1)}, bf16[144,1024]{1,0:T(8,128)(2,1)S(1)}, u32[]{:S(2)}, u32[]{:S(2)}) collective-permute-start(bf16[144,1024]{1,0:T(8,128)(2,1)S(1)} %get-tuple-element.88), channel_id=1, source_target_pairs={{0,4},{2,6},{4,0},{6,2},{8,12},{10,14},{12,8},{14,10},{16,20},{18,... | collective-permute-start | bytes 884744 | tf_op jit(solution)/shard_map/piece_l2/ppermute | solution.py:464
  58.4 8.1 %collective-permute-start.22 = (bf16[128,1024]{1,0:T(8,128)(2,1)S(1)}, bf16[128,1024]{1,0:T(8,128)(2,1)S(1)}, u32[]{:S(2)}, u32[]{:S(2)}) collective-permute-start(bf16[128,1024]{1,0:T(8,128)(2,1)S(1)} %tie_rows.8.refs_8_), channel_id=1, source_target_pairs={{0,24},{2,26},{4,28},{6,30},{8,0},{10,2},{12,4},{14,6},{16,8},{18,... | collective-permute-start | bytes 786440 | tf_op jit(solution)/shard_map/plane_b3/ppermute | solution.py:449
  59.6 8.4 %collective-permute-start.25 = (bf16[128,1024]{1,0:T(8,128)(2,1)S(1)}, bf16[128,1024]{1,0:T(8,128)(2,1)S(1)}, u32[]{:S(2)}, u32[]{:S(2)}) collective-permute-start(bf16[128,1024]{1,0:T(8,128)(2,1)S(1)} %collective-permute-done.19.refs_6_.refs_1_.refs_2_), channel_id=1, source_target_pairs={{0,2},{2,0},{4,6},{6,4},{8,10},{10,8},{12,14},{14,12},{16,18},{18,... | collective-permute-start | bytes 786440 | tf_op jit(solution)/shard_map/side_b2/ppermute | solution.py:460
  66.5 10.7 %collective-permute-start.23 = (bf16[128,1024]{1,0:T(8,128)(2,1)S(1)}, bf16[128,1024]{1,0:T(8,128)(2,1)S(1)}, u32[]{:S(2)}, u32[]{:S(2)}) collective-permute-start(bf16[128,1024]{1,0:T(8,128)(2,1)S(1)} %collective-permute-done.22.refs_6_.refs_2_), channel_id=1, source_target_pairs={{0,2},{2,0},{4,6},{6,4},{8,10},{10,8},{12,14},{14,12},{16,18},{18,... | collective-permute-start | bytes 786440 | tf_op jit(solution)/shard_map/side_b3/ppermute | solution.py:460
  68.0 9.3 %collective-permute-start.20 = (bf16[128,1024]{1,0:T(8,128)(2,1)S(1)}, bf16[128,1024]{1,0:T(8,128)(2,1)S(1)}, u32[]{:S(2)}, u32[]{:S(2)}) collective-permute-start(bf16[128,1024]{1,0:T(8,128)(2,1)S(1)} %tie_rows.9.refs_4_), channel_id=1, source_target_pairs={{0,8},{2,10},{4,12},{6,14},{8,16},{10,18},{12,20},{14,22},{16,24},... | collective-permute-start | bytes 786440 | tf_op jit(solution)/shard_map/plane_b1/ppermute | solution.py:449
  68.7 12.1 %collective-permute-start.26 = (bf16[144,1024]{1,0:T(8,128)(2,1)S(1)}, bf16[144,1024]{1,0:T(8,128)(2,1)S(1)}, u32[]{:S(2)}, u32[]{:S(2)}) collective-permute-start(bf16[144,1024]{1,0:T(8,128)(2,1)S(1)} %get-tuple-element.92), channel_id=1, source_target_pairs={{0,4},{2,6},{4,0},{6,2},{8,12},{10,14},{12,8},{14,10},{16,20},{18,... | collective-permute-start | bytes 884744 | tf_op jit(solution)/shard_map/piece_b2/ppermute | solution.py:464
  77.7 9.8 %collective-permute-start.29 = (bf16[144,1024]{1,0:T(8,128)(2,1)S(1)}, bf16[144,1024]{1,0:T(8,128)(2,1)S(1)}, u32[]{:S(2)}, u32[]{:S(2)}) collective-permute-start(bf16[144,1024]{1,0:T(8,128)(2,1)S(1)} %get-tuple-element.98), channel_id=1, source_target_pairs={{0,4},{2,6},{4,0},{6,2},{8,12},{10,14},{12,8},{14,10},{16,20},{18,... | collective-permute-start | bytes 884744 | tf_op jit(solution)/shard_map/piece_b3/ppermute | solution.py:464
  79.3 7.1 %collective-permute-start.21 = (bf16[128,1024]{1,0:T(8,128)(2,1)S(1)}, bf16[128,1024]{1,0:T(8,128)(2,1)S(1)}, u32[]{:S(2)}, u32[]{:S(2)}) collective-permute-start(bf16[128,1024]{1,0:T(8,128)(2,1)S(1)} %collective-permute-done.20.refs_6_.refs_2_), channel_id=1, source_target_pairs={{0,2},{2,0},{4,6},{6,4},{8,10},{10,8},{12,14},{14,12},{16,18},{18,... | collective-permute-start | bytes 786440 | tf_op jit(solution)/shard_map/side_b1/ppermute | solution.py:460
  86.9 8.0 %collective-permute-start.28 = (bf16[144,1024]{1,0:T(8,128)(2,1)S(1)}, bf16[144,1024]{1,0:T(8,128)(2,1)S(1)}, u32[]{:S(2)}, u32[]{:S(2)}) collective-permute-start(bf16[144,1024]{1,0:T(8,128)(2,1)S(1)} %get-tuple-element.95), channel_id=1, source_target_pairs={{0,4},{2,6},{4,0},{6,2},{8,12},{10,14},{12,8},{14,10},{16,20},{18,... | collective-permute-start | bytes 884744 | tf_op jit(solution)/shard_map/piece_b1/ppermute | solution.py:464
  93.3 10.4 %copy-start.11 = (bf16[576,1024]{1,0:T(8,128)(2,1)}, bf16[576,1024]{1,0:T(8,128)(2,1)S(1)}, u32[]{:S(2)}) copy-start(bf16[576,1024]{1,0:T(8,128)(2,1)S(1)} %get-tuple-element.101.refs_12_.refs_1_) | copy-start | bytes 3538948
  93.3 7.4 %collective-permute-start.30 = (bf16[144,1024]{1,0:T(8,128)(2,1)S(1)}, bf16[144,1024]{1,0:T(8,128)(2,1)S(1)}, u32[]{:S(2)}, u32[]{:S(2)}) collective-permute-start(bf16[144,1024]{1,0:T(8,128)(2,1)S(1)} %get-tuple-element.106), channel_id=1, source_target_pairs={{0,4},{2,6},{4,0},{6,2},{8,12},{10,14},{12,8},{14,10},{16,20},{18,... | collective-permute-start | bytes 884744 | tf_op jit(solution)/shard_map/piece_r3/ppermute | solution.py:464
  100.8 10.9 %copy-start.9 = (bf16[576,1536]{1,0:T(8,128)(2,1)}, bf16[576,1536]{1,0:T(8,128)(2,1)S(1)}, u32[]{:S(2)}) copy-start(bf16[576,1536]{1,0:T(8,128)(2,1)S(1)} %get-tuple-element.117.refs_8_) | copy-start | bytes 5308420
  101.3 10.6 %collective-permute-start.32 = (bf16[128,1024]{1,0:T(8,128)(2,1)S(1)}, bf16[128,1024]{1,0:T(8,128)(2,1)S(1)}, u32[]{:S(2)}, u32[]{:S(2)}) collective-permute-start(bf16[128,1024]{1,0:T(8,128)(2,1)S(1)} %get-tuple-element.111), channel_id=1, source_target_pairs={{0,2},{2,0},{4,6},{6,4},{8,10},{10,8},{12,14},{14,12},{16,18},{18,... | collective-permute-start | bytes 786440 | tf_op jit(solution)/shard_map/side_r3/ppermute | solution.py:460
  102.9 9.0 %collective-permute-start.31 = (bf16[144,1024]{1,0:T(8,128)(2,1)S(1)}, bf16[144,1024]{1,0:T(8,128)(2,1)S(1)}, u32[]{:S(2)}, u32[]{:S(2)}) collective-permute-start(bf16[144,1024]{1,0:T(8,128)(2,1)S(1)} %get-tuple-element.109), channel_id=1, source_target_pairs={{0,4},{2,6},{4,0},{6,2},{8,12},{10,14},{12,8},{14,10},{16,20},{18,... | collective-permute-start | bytes 884744 | tf_op jit(solution)/shard_map/piece_r2/ppermute | solution.py:464
  111.9 2.7 %copy-start.10 = (bf16[576,1536]{1,0:T(8,128)(2,1)S(1)}, bf16[576,1536]{1,0:T(8,128)(2,1)}, u32[]{:S(2)}) copy-start(bf16[576,1536]{1,0:T(8,128)(2,1)} %copy-done.9) | copy-start | bytes 5308420
  111.9 2.6 %copy-start.12 = (bf16[576,1024]{1,0:T(8,128)(2,1)S(1)}, bf16[576,1024]{1,0:T(8,128)(2,1)}, u32[]{:S(2)}) copy-start(bf16[576,1024]{1,0:T(8,128)(2,1)} %copy-done.11) | copy-start | bytes 3538948
  112.5 10.8 %collective-permute-start.36 = (bf16[1024,1536]{1,0:T(8,128)(2,1)S(1)}, bf16[1024,1536]{1,0:T(8,128)(2,1)S(1)}, u32[]{:S(2)}, u32[]{:S(2)}) collective-permute-start(bf16[1024,1536]{1,0:T(8,128)(2,1)S(1)} %get-tuple-element.128), channel_id=1, source_target_pairs={{0,1},{1,0},{2,3},{3,2},{4,5},{5,4},{6,7},{7,6},{8,9},{9,8},{10,11... | collective-permute-start | bytes 9437192 | tf_op jit(solution)/shard_map/ppermute | solution.py:446
  112.6 9.9 %collective-permute-start.34 = (bf16[128,1024]{1,0:T(8,128)(2,1)S(1)}, bf16[128,1024]{1,0:T(8,128)(2,1)S(1)}, u32[]{:S(2)}, u32[]{:S(2)}) collective-permute-start(bf16[128,1024]{1,0:T(8,128)(2,1)S(1)} %get-tuple-element.123), channel_id=1, source_target_pairs={{0,2},{2,0},{4,6},{6,4},{8,10},{10,8},{12,14},{14,12},{16,18},{18,... | collective-permute-start | bytes 786440 | tf_op jit(solution)/shard_map/side_r2/ppermute | solution.py:460
  113.2 10.2 %collective-permute-start.35 = (bf16[128,1024]{1,0:T(8,128)(2,1)S(1)}, bf16[128,1024]{1,0:T(8,128)(2,1)S(1)}, u32[]{:S(2)}, u32[]{:S(2)}) collective-permute-start(bf16[128,1024]{1,0:T(8,128)(2,1)S(1)} %get-tuple-element.127), channel_id=1, source_target_pairs={{0,8},{2,10},{4,12},{6,14},{8,16},{10,18},{12,20},{14,22},{16,24},... | collective-permute-start | bytes 786440 | tf_op jit(solution)/shard_map/plane_r3/ppermute | solution.py:449
  113.4 10.0 %collective-permute-start.33 = (bf16[144,1024]{1,0:T(8,128)(2,1)S(1)}, bf16[144,1024]{1,0:T(8,128)(2,1)S(1)}, u32[]{:S(2)}, u32[]{:S(2)}) collective-permute-start(bf16[144,1024]{1,0:T(8,128)(2,1)S(1)} %get-tuple-element.121), channel_id=1, source_target_pairs={{0,4},{2,6},{4,0},{6,2},{8,12},{10,14},{12,8},{14,10},{16,20},{18,... | collective-permute-start | bytes 884744 | tf_op jit(solution)/shard_map/piece_r1/ppermute | solution.py:464
  123.9 9.7 %collective-permute-start.39 = (bf16[1536,512]{1,0:T(8,128)(2,1)S(1)}, bf16[1536,512]{1,0:T(8,128)(2,1)S(1)}, u32[]{:S(2)}, u32[]{:S(2)}) collective-permute-start(bf16[1536,512]{1,0:T(8,128)(2,1)S(1)} %get-tuple-element.133), channel_id=1, source_target_pairs={{0,1},{1,0},{2,3},{3,2},{4,5},{5,4},{6,7},{7,6},{8,9},{9,8},{10,11... | collective-permute-start | bytes 4718600 | tf_op jit(solution)/shard_map/ppermute | solution.py:446
  124.0 9.6 %collective-permute-start.37 = (bf16[144,1024]{1,0:T(8,128)(2,1)S(1)}, bf16[144,1024]{1,0:T(8,128)(2,1)S(1)}, u32[]{:S(2)}, u32[]{:S(2)}) collective-permute-start(bf16[144,1024]{1,0:T(8,128)(2,1)S(1)} %get-tuple-element.129), channel_id=1, source_target_pairs={{0,4},{2,6},{4,0},{6,2},{8,12},{10,14},{12,8},{14,10},{16,20},{18,... | collective-permute-start | bytes 884744 | tf_op jit(solution)/shard_map/piece_r0/ppermute | solution.py:464
  125.2 8.4 %collective-permute-start.38 = (bf16[128,1024]{1,0:T(8,128)(2,1)S(1)}, bf16[128,1024]{1,0:T(8,128)(2,1)S(1)}, u32[]{:S(2)}, u32[]{:S(2)}) collective-permute-start(bf16[128,1024]{1,0:T(8,128)(2,1)S(1)} %get-tuple-element.131), channel_id=1, source_target_pairs={{0,2},{2,0},{4,6},{6,4},{8,10},{10,8},{12,14},{14,12},{16,18},{18,... | collective-permute-start | bytes 786440 | tf_op jit(solution)/shard_map/side_r1/ppermute | solution.py:460
  126.8 14.6 %collective-permute-start.42 = (bf16[128,1024]{1,0:T(8,128)(2,1)S(1)}, bf16[128,1024]{1,0:T(8,128)(2,1)S(1)}, u32[]{:S(2)}, u32[]{:S(2)}) collective-permute-start(bf16[128,1024]{1,0:T(8,128)(2,1)S(1)} %get-tuple-element.137), channel_id=1, source_target_pairs={{0,16},{2,18},{4,20},{6,22},{8,24},{10,26},{12,28},{14,30},{16,0},... | collective-permute-start | bytes 786440 | tf_op jit(solution)/shard_map/plane_r2/ppermute | solution.py:449
  133.6 1.4 copy-start.2
  135.6 7.7 %collective-permute-start.40 = (bf16[128,1024]{1,0:T(8,128)(2,1)S(1)}, bf16[128,1024]{1,0:T(8,128)(2,1)S(1)}, u32[]{:S(2)}, u32[]{:S(2)}) collective-permute-start(bf16[128,1024]{1,0:T(8,128)(2,1)S(1)} %get-tuple-element.135), channel_id=1, source_target_pairs={{0,2},{2,0},{4,6},{6,4},{8,10},{10,8},{12,14},{14,12},{16,18},{18,... | collective-permute-start | bytes 786440 | tf_op jit(solution)/shard_map/side_r0/ppermute | solution.py:460
  137.2 9.6 %collective-permute-start.41 = (bf16[128,1024]{1,0:T(8,128)(2,1)S(1)}, bf16[128,1024]{1,0:T(8,128)(2,1)S(1)}, u32[]{:S(2)}, u32[]{:S(2)}) collective-permute-start(bf16[128,1024]{1,0:T(8,128)(2,1)S(1)} %get-tuple-element.136), channel_id=1, source_target_pairs={{0,24},{2,26},{4,28},{6,30},{8,0},{10,2},{12,4},{14,6},{16,8},{18,... | collective-permute-start | bytes 786440 | tf_op jit(solution)/shard_map/plane_r1/ppermute | solution.py:449
  146.8 1.4 copy-start.1
where the time goes:
time: 152 us
  Pallas kernels  50.6 us (33%)
  starting transfers between devices  48.6 us (32%)
  waiting for transfers between devices  39.2 us (26%)
  matrix products  9.44 us (6%)
  local copies, waits for them, and re-layouts  3.1 us (2%)
    ppermute x9, waiting for transfers between devices, along(): lax.ppermute(a, 'expert', [(z * inner + p, (z + shift) % PLANES * inner +...  20.7 us
    ppermute x12, starting transfers between devices, beside(): return lax.ppermute(a, 'expert', [(i, i ^ 1) for i in range(group_count)])  17.2 us
    pallas_call x2, Pallas kernels, weight_grads(): pl.pallas_call(functools.partial(weight_body, len(groups), column, len(de...  15.8 us
    ppermute x12, starting transfers between devices, across(): lax.ppermute(parts[k], 'expert', [(i, i ^ SIDE * k) for i in range(group_...  15.5 us
    ppermute x12, waiting for transfers between devices, beside(): return lax.ppermute(a, 'expert', [(i, i ^ 1) for i in range(group_count)])  15 us
    ppermute x9, starting transfers between devices, along(): lax.ppermute(a, 'expert', [(z * inner + p, (z + shift) % PLANES * inner +...  13.8 us
    pallas_call x2, Pallas kernels, backward(): pl.pallas_call(functools.partial(backward_body, count, len(deps)), in_spe...  11.7 us
    pallas_call x2, Pallas kernels, forward(): pl.pallas_call(functools.partial(forward_body, count, len(deps)), in_spec...  9.47 us
  transfers between devices with their start and end apart: 43, of which 12 were waited for; matrix products, arithmetic and copies ran while one was open for 6% of the time, Pallas kernels for 29%

commit v1 on v0

--- a/solution.py
+++ b/solution.py
@@ -210,6 +210,13 @@
     return functools.partial(copy_body, len(arrays)), list(arrays), shapes, []
 
 
+def mark_body(mark_ref):
+    mark_ref[...] = jnp.zeros_like(mark_ref)
+
+
+MARK = (mark_body, [], [jax.ShapeDtypeStruct((8, 128), F32)], [])
+
+
 def add_body(count, *refs):
     total = refs[0][...].astype(F32)
     for ref in refs[1:count]:
@@ -251,7 +258,8 @@
 def forward_body(count, deps, *refs):
     piece_refs = refs[:count]
     gate_m, gate_o, linear_m, linear_o = refs[count : count + 4]
-    x_ref, gate_factor_ref, linear_factor_ref, hidden_ref = refs[count + 4 + deps :]
+    x_ref, gate_factor_ref, linear_factor_ref, hidden_ref, mark_ref = refs[count + 4 + deps :]
+    mark_body(mark_ref)
     assemble(piece_refs, x_ref)
     half, hidden = gate_m.shape
     tile = tile_of(hidden)
@@ -279,9 +287,10 @@
     return pl.pallas_call(
         functools.partial(forward_body, count, len(deps)),
         in_specs=[VMEM] * (count + 4) + [ANY] * len(deps),
-        out_specs=[VMEM] * 4,
+        out_specs=[VMEM] * 5,
         out_shape=[jax.ShapeDtypeStruct((rows, width), BF)]
-        + [jax.ShapeDtypeStruct((rows, hidden), BF)] * 3,
+        + [jax.ShapeDtypeStruct((rows, hidden), BF)] * 3
+        + [jax.ShapeDtypeStruct((8, 128), F32)],
         compiler_params=params(10),
         cost_estimate=cost(4 * rows * width * hidden, 6 * rows * hidden + 4 * width * hidden),
         name="forward_rows",
@@ -294,7 +303,8 @@
     gate_m, gate_o, linear_m, linear_o = refs[count + 4 : count + 8]
     refs = refs[count + 8 + deps :]
     b_ref, gate_delta_ref, linear_delta_ref = refs[:3]
-    row_refs, total = refs[3:-1], refs[-1]
+    row_refs, mark_ref, total = refs[3:-2], refs[-2], refs[-1]
+    mark_body(mark_ref)
     assemble(piece_refs, b_ref)
     hidden, half = out_m.shape
     tile = tile_of(hidden)
@@ -324,71 +334,71 @@
     results = pl.pallas_call(
         functools.partial(backward_body, count, len(deps)),
         in_specs=[VMEM] * (count + 8) + [ANY] * len(deps),
-        out_specs=[VMEM] * (3 + count),
+        out_specs=[VMEM] * (4 + count),
         out_shape=[jax.ShapeDtypeStruct((rows, width), BF)]
         + [jax.ShapeDtypeStruct((rows, hidden), BF)] * 2
-        + [jax.ShapeDtypeStruct((size, width), BF)] * count,
+        + [jax.ShapeDtypeStruct((size, width), BF)] * count
+        + [jax.ShapeDtypeStruct((8, 128), F32)],
         scratch_shapes=[pltpu.VMEM((rows, width), F32)],
         compiler_params=params(10),
         cost_estimate=cost(6 * rows * width * hidden, 8 * rows * hidden + 6 * width * hidden),
         name="backward_rows",
     )(*pieces, gate_factor, linear_factor, *out, *gate, *linear, *deps)
-    return results[:3], results[3:]
-
-
-def weight_body(groups, column, deps, *refs):
-    outs = refs[5 * groups + deps :]
+    return results[:3], results[3:-1], results[-1]
+
+
+def weight_body(groups, kinds, column, add, deps, *refs):
+    received = refs[5 * groups]
+    out_refs = refs[5 * groups + (1 if add else 0) + deps :]
+    mark_body(out_refs[-1])
     width, hidden = refs[0].shape[1], refs[2].shape[1]
     half, tile = width // 2, tile_of(hidden)
     side = slice(column * half, (column + 1) * half)
+
     @pl.loop(0, hidden // tile)
     def _(j):
         at = pl.ds(pl.multiple_of(j * tile, tile), tile)
-        totals = [None, None, None]
-        for g in range(groups):
-            x_ref, b_ref, gate_delta, linear_delta, hid = refs[5 * g : 5 * g + 5]
-            for i, (a, b) in enumerate(
-                (
-                    (x_ref[:, side], gate_delta[:, at]),
-                    (x_ref[:, side], linear_delta[:, at]),
-                    (hid[:, at], b_ref[:, side]),
+        for place, kind in enumerate(kinds):
+            total = None
+            for g in range(groups):
+                x_ref, b_ref, gate_delta, linear_delta, hid = refs[5 * g : 5 * g + 5]
+                if kind == "out":
+                    a, b = hid[:, at], b_ref[:, side]
+                else:
+                    a, b = x_ref[:, side], (gate_delta if kind == "gate" else linear_delta)[:, at]
+                term = lax.dot_general(a, b, ROWS, preferred_element_type=F32)
+                total = term if total is None else total + term
+            rows = (at, slice(None)) if kind == "out" else (pl.ds(place * half, half), at)
+            if add:
+                total = total + received[rows].astype(F32)
+                out_refs[place][at if kind == "out" else slice(None), slice(None) if kind == "out" else at] = (
+                    total.astype(BF)
                 )
-            ):
-                term = lax.dot_general(a, b, ROWS, preferred_element_type=F32)
-                totals[i] = term if totals[i] is None else totals[i] + term
-        outs[0][:half, at] = totals[0].astype(BF)
-        outs[0][half:, at] = totals[1].astype(BF)
-        outs[1][at, :] = totals[2].astype(BF)
-
-
-def weight_grads(groups, column, deps):
+            else:
+                out_refs[0][rows] = total.astype(BF)
+
+
+def weight_grads(groups, kinds, column, received, deps):
     hidden = groups[0][2].shape[1]
-    width = groups[0][0].shape[1]
-    half = width // 2
-    operands = [a for group in groups for a in group]
+    half = groups[0][0].shape[1] // 2
+    operands = [a for group in groups for a in group] + list(received)
+    one = (hidden, half) if kinds == ("out",) else (half, hidden)
+    shapes = [one] * len(kinds) if received else [(len(kinds) * one[0], one[1])]
     total_rows = sum(group[0].shape[0] for group in groups)
     return pl.pallas_call(
-        functools.partial(weight_body, len(groups), column, len(deps)),
+        functools.partial(
+            weight_body, len(groups), kinds, column, bool(received), len(deps)
+        ),
         in_specs=[VMEM] * len(operands) + [ANY] * len(deps),
-        out_specs=[VMEM] * 2,
-        out_shape=[jax.ShapeDtypeStruct(s, BF) for s in ((width, hidden), (hidden, half))],
+        out_specs=[VMEM] * (len(shapes) + 1),
+        out_shape=[jax.ShapeDtypeStruct(s, BF) for s in shapes]
+        + [jax.ShapeDtypeStruct((8, 128), F32)],
         compiler_params=params(12),
         cost_estimate=cost(
-            3 * total_rows * width * hidden, 6 * total_rows * hidden + 3 * width * hidden
+            2 * len(kinds) * total_rows * half * hidden, 4 * total_rows * hidden
         ),
         name="weight_grads",
     )(*operands, *deps)
-
-
-def split_body(mine_ref, theirs_ref, top_ref, bottom_ref):
-    half = top_ref.shape[0]
-    for out_ref, at in ((top_ref, slice(0, half)), (bottom_ref, slice(half, 2 * half))):
-        out_ref[...] = (mine_ref[at, :].astype(F32) + theirs_ref[at, :].astype(F32)).astype(BF)
-
-
-def added_halves(mine, theirs):
-    rows, hidden = mine.shape
-    return split_body, [mine, theirs], [jax.ShapeDtypeStruct((rows // 2, hidden), BF)] * 2, []
 
 
 def finish_body(count, *refs):
@@ -532,13 +542,14 @@
     factors, saved, rows, partial = {}, {}, {}, {}
 
     def ahead(chunks):
-        factors[chunks] = step(
-            forward([a for c in chunks for a in pieces["l", c]], gate, linear, deps())
+        *factors[chunks], mark = forward(
+            [a for c in chunks for a in pieces["l", c]], gate, linear, deps()
         )
+        step(mark)
 
     def behind(chunks, *extra):
         x, gate_factor, linear_factor, hid = factors[chunks]
-        (b, gate_delta, linear_delta), sums = backward(
+        (b, gate_delta, linear_delta), sums, mark = backward(
             [a for c in chunks for a in pieces["b", c]],
             gate_factor,
             linear_factor,
@@ -547,7 +558,7 @@
             linear,
             deps(*extra),
         )
-        step(b)
+        step(mark)
         saved[chunks] = (x, b, gate_delta, linear_delta, hid)
         for i, c in enumerate(chunks):
             rows[c] = sums[i * fan : (i + 1) * fan]
@@ -596,9 +607,9 @@
     (down,) = swapped_after((latent_down,), last[-1:])
     pick("b", 2, come("b", 0), blocks["b", 3])
     to_side("b", 3)
-    ahead((3, 2))
     pick("b", 3, come("l", 2), blocks["b", 1])
     to_side("b", 1)
+    ahead((3, 2))
     pick("b", 1, come("b", 2), down[1])
     behind((3, 2))
     send_rows(3, rows[3][1:])
@@ -606,30 +617,30 @@
     results = turn([gathered(3), copies(rows[2][1:])])
     send_side(3, results[0])
     send_rows(2, results[1])
-    theirs = weight_grads(list(saved.values()), 1, deps())
-    step(theirs)
-    results = turn([gathered(2), added(partial[3], BF), copies(rows[1][1:])], theirs)
+    groups = list(saved.values())
+
+    def grads_of(kinds, column, *received):
+        *results, mark = weight_grads(groups, kinds, column, received, deps())
+        step(mark)
+        return results
+
+    wide = grads_of(("gate", "linear"), 1)
+    results = turn([gathered(2), added(partial[3], BF), copies(rows[1][1:])], wide)
     send_side(2, results[0])
     send_home(3, results[1])
     send_rows(1, results[2])
-    received = [swap(results[3])]
-    ours = weight_grads(list(saved.values()), 0, deps())
-    step(ours)
-    results = turn(
-        [gathered(1), added(partial[2], BF), copies(rows[0][1:])],
-        results[4:],
-        [partial[3], received[0]],
-    )
+    wide = swap(results[3])
+    tall = grads_of(("out",), 1)
+    results = turn([gathered(1), added(partial[2], BF), copies(rows[0][1:])], tall, [partial[3]])
     send_side(1, results[0])
     send_home(2, results[1])
     send_rows(0, results[2])
-    received.append(swap(results[3]))
-    (grads,) = turn([added_halves(ours[0], received[0])])
-    results = turn([gathered(0), added(partial[1], BF)], (), [received[1]])
+    tall = swap(results[3])
+    grads = grads_of(("gate", "linear"), 0, wide)
+    results = turn([gathered(0), added(partial[1], BF)], (), [])
     send_side(0, results[0])
     send_home(1, results[1])
-    results = turn([added([ours[1], received[1]], BF)])
-    grads = [*grads, results[0][0]]
+    grads += grads_of(("out",), 0, tall)
     parts = [*partial[0], partial[1], partial[2], partial[3]]
     if halves > 1:
         results = turn([added(parts, F32)])

time: 152 us -> 146 us (0.961)
  starting transfers between devices: 48.6 us -> 44.8 us
  local copies, waits for them, and re-layouts: 3.1 us -> 0.05 us
    ppermute x12, waiting for transfers between devices: 2.23 us -> 6.86 us  [across(): lax.ppermute(parts[k], 'expert', [(i, i ^ SIDE * k) for i in range(group_...]
    pallas_call x2 -> x4, Pallas kernels: 15.8 us -> 20 us  [weight_grads(): pl.pallas_call(functools.partial(weight_body, len(groups), kinds, column,...]
    ppermute x12, waiting for transfers between devices: 15 us -> 10.9 us  [beside(): return lax.ppermute(a, 'expert', [(i, i ^ 1) for i in range(group_count)])]
    pallas_call x6 -> x4, Pallas kernels: 6 us -> 2.21 us  [bundle(): pl.pallas_call(functools.partial(bundle_body, parts, len(through), len(de...]
    unnamed x31 -> x18, local copies, waits for them, and re-layouts: 3.1 us -> 0.05 us
    ppermute x12, starting transfers between devices: 17.2 us -> 15.3 us  [beside(): return lax.ppermute(a, 'expert', [(i, i ^ 1) for i in range(group_count)])]
  transfers between devices with their start and end apart: 43 -> 43, of which waited for: 12 -> 15; matrix products, arithmetic and copies ran while one was open for 6% -> 6% of each run, Pallas kernels for 29% -> 31%
where the time goes in v1:
time: 146 us
  Pallas kernels  51.3 us (35%)
  starting transfers between devices  44.8 us (31%)
  waiting for transfers between devices  39.5 us (27%)
  matrix products  9.49 us (6%)
    ppermute x9, waiting for transfers between devices, along(): lax.ppermute(a, 'expert', [(z * inner + p, (z + shift) % PLANES * inner +...  20.4 us
    pallas_call x4, Pallas kernels, weight_grads(): pl.pallas_call(functools.partial(weight_body, len(groups), kinds, column,...  20 us
    ppermute x12, starting transfers between devices, beside(): return lax.ppermute(a, 'expert', [(i, i ^ 1) for i in range(group_count)])  15.3 us
    ppermute x12, starting transfers between devices, across(): lax.ppermute(parts[k], 'expert', [(i, i ^ SIDE * k) for i in range(group_...  15.1 us
    ppermute x9, starting transfers between devices, along(): lax.ppermute(a, 'expert', [(z * inner + p, (z + shift) % PLANES * inner +...  12.3 us
    pallas_call x2, Pallas kernels, backward(): pl.pallas_call(functools.partial(backward_body, count, len(deps)), in_spe...  11.9 us
    ppermute x12, waiting for transfers between devices, beside(): return lax.ppermute(a, 'expert', [(i, i ^ 1) for i in range(group_count)])  10.9 us
    pallas_call x2, Pallas kernels, forward(): pl.pallas_call(functools.partial(forward_body, count, len(deps)), in_spec...  9.69 us
  transfers between devices with their start and end apart: 43, of which 15 were waited for; matrix products, arithmetic and copies ran while one was open for 6% of the time, Pallas kernels for 31%

profile of v1, /device:TPU:0, one launch (start us, length us, event | category | flops | bytes accessed | tf_op | source)
XLA Modules:
  0.0 146.3 jit_solution(10063179975978088934)
XLA Ops:
  0.6 0.5 collective-permute-start
  1.2 3.5 %convolution_convert_fusion.3.own_ref = bf16[128,512]{1,0:T(8,128)(2,1)S(1)} fusion(bf16[128,4096]{1,0:T(8,128)(2,1)} %param.10, bf16[4096,512]{1,0:T(8,128)(2,1)} %refs_5_), kind=kOutput, calls=%fused_computation.3 | convolution fusion | flops 536936448 | bytes 5373952 | tf_op jit(solution)/shard_map/dot_general | solution.py:493
  4.8 0.7 convolution_convert_fusion.2.refs_3_
  5.6 1.3 collective-permute-done.1.other_ref
  8.1 2.8 %collective-permute-start.9 = (bf16[144,1024]{1,0:T(8,128)(2,1)S(1)}, bf16[144,1024]{1,0:T(8,128)(2,1)S(1)}, u32[]{:S(2)}, u32[]{:S(2)}) collective-permute-start(bf16[144,1024]{1,0:T(8,128)(2,1)S(1)} %join_rows.2.block_ref.refs_0_.refs_2_), channel_id=1, source_target_pairs={{0,8},{2,10},{4,12},{6,14},{8,16},{10,18},{12,20},{14,22},{16,24},... | collective-permute-start | bytes 884744 | tf_op jit(solution)/shard_map/plane_l1/ppermute | solution.py:459
  10.9 3.8 %convolution_convert_fusion.1.own_ref = bf16[128,512]{1,0:T(8,128)(2,1)S(1)} fusion(bf16[128,4096]{1,0:T(8,128)(2,1)S(1)} %copy-done.8, bf16[512,4096]{1,0:T(8,128)(2,1)} %param.16), kind=kOutput, calls=%fused_computation.1 | convolution fusion | flops 536936448 | bytes 5373952 | tf_op jit(solution)/shard_map/dot_general | solution.py:493
  14.7 1.5 %convolution_convert_fusion.refs_0_ = bf16[128,512]{1,0:T(8,128)(2,1)S(1)} fusion(bf16[128,4096]{1,0:T(8,128)(2,1)S(1)} %collective-permute-done.3, bf16[512,4096]{1,0:T(8,128)(2,1)S(1)} %copy-done.7), kind=kOutput, calls=%fused_computation | convolution fusion | flops 536936448 | bytes 5373952 | tf_op jit(solution)/shard_map/dot_general | solution.py:493
  16.4 1.5 %collective-permute-start.2 = (bf16[144,1024]{1,0:T(8,128)(2,1)S(1)}, bf16[144,1024]{1,0:T(8,128)(2,1)S(1)}, u32[]{:S(2)}, u32[]{:S(2)}) collective-permute-start(bf16[144,1024]{1,0:T(8,128)(2,1)S(1)} %join_rows.2.block_ref.refs_0_.refs_2_), channel_id=1, source_target_pairs={{0,2},{2,0},{4,6},{6,4},{8,10},{10,8},{12,14},{14,12},{16,18},{18,... | collective-permute-start | bytes 884744 | tf_op jit(solution)/shard_map/side_l0/ppermute | solution.py:470
  17.9 3.6 %collective-permute-start.7 = (bf16[144,1024]{1,0:T(8,128)(2,1)S(1)}, bf16[144,1024]{1,0:T(8,128)(2,1)S(1)}, u32[]{:S(2)}, u32[]{:S(2)}) collective-permute-start(bf16[144,1024]{1,0:T(8,128)(2,1)S(1)} %tie_rows.5.refs_0_), channel_id=1, source_target_pairs={{0,24},{2,26},{4,28},{6,30},{8,0},{10,2},{12,4},{14,6},{16,8},{18,... | collective-permute-start | bytes 884744 | tf_op jit(solution)/shard_map/plane_l3/ppermute | solution.py:459
  21.5 1.5 %collective-permute-start.10 = (bf16[144,1024]{1,0:T(8,128)(2,1)S(1)}, bf16[144,1024]{1,0:T(8,128)(2,1)S(1)}, u32[]{:S(2)}, u32[]{:S(2)}) collective-permute-start(bf16[144,1024]{1,0:T(8,128)(2,1)S(1)} %collective-permute-done.9.refs_5_.refs_1_.refs_0_.refs_2_), channel_id=1, source_target_pairs={{0,2},{2,0},{4,6},{6,4},{8,10},{10,8},{12,14},{14,12},{16,18},{18,... | collective-permute-start | bytes 884744 | tf_op jit(solution)/shard_map/side_l1/ppermute | solution.py:470
  23.0 3.2 %collective-permute-done.2.refs_1_.refs_3_ = bf16[144,1024]{1,0:T(8,128)(2,1)S(1)} collective-permute-done((bf16[144,1024]{1,0:T(8,128)(2,1)S(1)}, bf16[144,1024]{1,0:T(8,128)(2,1)S(1)}, u32[]{:S(2)}, u32[]{:S(2)}) %collective-permute-start.2) | collective-permute-done | bytes 294944 | tf_op jit(solution)/shard_map/side_l0/ppermute | solution.py:470
  26.7 2.7 %collective-permute-start.15 = (bf16[144,1024]{1,0:T(8,128)(2,1)S(1)}, bf16[144,1024]{1,0:T(8,128)(2,1)S(1)}, u32[]{:S(2)}, u32[]{:S(2)}) collective-permute-start(bf16[144,1024]{1,0:T(8,128)(2,1)S(1)} %tie_rows.6.refs_4_), channel_id=1, source_target_pairs={{0,16},{2,18},{4,20},{6,22},{8,24},{10,26},{12,28},{14,30},{16,0},... | collective-permute-start | bytes 884744 | tf_op jit(solution)/shard_map/plane_l2/ppermute | solution.py:459
  29.4 1.5 %collective-permute-start.13 = (bf16[144,1024]{1,0:T(8,128)(2,1)S(1)}, bf16[144,1024]{1,0:T(8,128)(2,1)S(1)}, u32[]{:S(2)}, u32[]{:S(2)}) collective-permute-start(bf16[144,1024]{1,0:T(8,128)(2,1)S(1)} %get-tuple-element.86), channel_id=1, source_target_pairs={{0,4},{2,6},{4,0},{6,2},{8,12},{10,14},{12,8},{14,10},{16,20},{18,... | collective-permute-start | bytes 884744 | tf_op jit(solution)/shard_map/piece_l0/ppermute | solution.py:474
  30.9 1.5 %collective-permute-start.8 = (bf16[144,1024]{1,0:T(8,128)(2,1)S(1)}, bf16[144,1024]{1,0:T(8,128)(2,1)S(1)}, u32[]{:S(2)}, u32[]{:S(2)}) collective-permute-start(bf16[144,1024]{1,0:T(8,128)(2,1)S(1)} %collective-permute-done.7.refs_5_.refs_1_.refs_0_.refs_2_), channel_id=1, source_target_pairs={{0,2},{2,0},{4,6},{6,4},{8,10},{10,8},{12,14},{14,12},{16,18},{18,... | collective-permute-start | bytes 884744 | tf_op jit(solution)/shard_map/side_l3/ppermute | solution.py:470
  32.8 1.7 %collective-permute-start.14 = (bf16[144,1024]{1,0:T(8,128)(2,1)S(1)}, bf16[144,1024]{1,0:T(8,128)(2,1)S(1)}, u32[]{:S(2)}, u32[]{:S(2)}) collective-permute-start(bf16[144,1024]{1,0:T(8,128)(2,1)S(1)} %get-tuple-element.88), channel_id=1, source_target_pairs={{0,4},{2,6},{4,0},{6,2},{8,12},{10,14},{12,8},{14,10},{16,20},{18,... | collective-permute-start | bytes 884744 | tf_op jit(solution)/shard_map/piece_l1/ppermute | solution.py:474
  34.6 1.5 %collective-permute-start.6 = (bf16[128,1024]{1,0:T(8,128)(2,1)S(1)}, bf16[128,1024]{1,0:T(8,128)(2,1)S(1)}, u32[]{:S(2)}, u32[]{:S(2)}) collective-permute-start(bf16[128,1024]{1,0:T(8,128)(2,1)S(1)} %join_rows.3.refs_4_.block_ref.refs_2_), channel_id=1, source_target_pairs={{0,2},{2,0},{4,6},{6,4},{8,10},{10,8},{12,14},{14,12},{16,18},{18,... | collective-permute-start | bytes 786440 | tf_op jit(solution)/shard_map/side_b0/ppermute | solution.py:470
  36.1 6.0 %collective-permute-done.15.refs_6_.refs_1_.refs_0_.refs_2_ = bf16[144,1024]{1,0:T(8,128)(2,1)S(1)} collective-permute-done((bf16[144,1024]{1,0:T(8,128)(2,1)S(1)}, bf16[144,1024]{1,0:T(8,128)(2,1)S(1)}, u32[]{:S(2)}, u32[]{:S(2)}) %collective-permute-start.15) | collective-permute-done | bytes 294944 | tf_op jit(solution)/shard_map/plane_l2/ppermute | solution.py:459
  42.1 1.5 %collective-permute-start.17 = (bf16[144,1024]{1,0:T(8,128)(2,1)S(1)}, bf16[144,1024]{1,0:T(8,128)(2,1)S(1)}, u32[]{:S(2)}, u32[]{:S(2)}) collective-permute-start(bf16[144,1024]{1,0:T(8,128)(2,1)S(1)} %collective-permute-done.15.refs_6_.refs_1_.refs_0_.refs_2_), channel_id=1, source_target_pairs={{0,2},{2,0},{4,6},{6,4},{8,10},{10,8},{12,14},{14,12},{16,18},{18,... | collective-permute-start | bytes 884744 | tf_op jit(solution)/shard_map/side_l2/ppermute | solution.py:470
  43.6 0.5 select_latent.6
  44.1 1.6 %collective-permute-start.18 = (bf16[144,1024]{1,0:T(8,128)(2,1)S(1)}, bf16[144,1024]{1,0:T(8,128)(2,1)S(1)}, u32[]{:S(2)}, u32[]{:S(2)}) collective-permute-start(bf16[144,1024]{1,0:T(8,128)(2,1)S(1)} %get-tuple-element.92), channel_id=1, source_target_pairs={{0,4},{2,6},{4,0},{6,2},{8,12},{10,14},{12,8},{14,10},{16,20},{18,... | collective-permute-start | bytes 884744 | tf_op jit(solution)/shard_map/piece_l3/ppermute | solution.py:474
  46.2 4.8 %forward_rows.2 = (bf16[576,1024]{1,0:T(8,128)(2,1)S(1)}, bf16[576,1536]{1,0:T(8,128)(2,1)S(1)}, bf16[576,1536]{1,0:T(8,128)(2,1)S(1)}, bf16[576,1536]{1,0:T(8,128)(2,1)S(1)}, f32[8,128]{1,0:T(8,128)S(1)}) custom-call(bf16[144,1024]{1,0:T(8,128)(2,1)S(1)} %get-tuple-element.84.refs_0_, bf16[144,1024]{1,0:T(8,128)(2,1)S(1)} %collective-permute-done.13.refs_5_.refs_1_, ...), custom_call_target="tpu_custom_call" | custom-call | flops 3623878656 | bytes 11599873 | tf_op jit(solution)/shard_map/forward_rows/pallas_call | solution.py:287
  50.9 4.8 %collective-permute-done.19.refs_6_.refs_1_.refs_2_ = bf16[128,1024]{1,0:T(8,128)(2,1)S(1)} collective-permute-done((bf16[128,1024]{1,0:T(8,128)(2,1)S(1)}, bf16[128,1024]{1,0:T(8,128)(2,1)S(1)}, u32[]{:S(2)}, u32[]{:S(2)}) %collective-permute-start.19) | collective-permute-done | bytes 262176 | tf_op jit(solution)/shard_map/plane_b2/ppermute | solution.py:459
  56.3 1.6 %collective-permute-start.25 = (bf16[128,1024]{1,0:T(8,128)(2,1)S(1)}, bf16[128,1024]{1,0:T(8,128)(2,1)S(1)}, u32[]{:S(2)}, u32[]{:S(2)}) collective-permute-start(bf16[128,1024]{1,0:T(8,128)(2,1)S(1)} %collective-permute-done.19.refs_6_.refs_1_.refs_2_), channel_id=1, source_target_pairs={{0,2},{2,0},{4,6},{6,4},{8,10},{10,8},{12,14},{14,12},{16,18},{18,... | collective-permute-start | bytes 786440 | tf_op jit(solution)/shard_map/side_b2/ppermute | solution.py:470
  57.9 1.2 collective-permute-start.23
  59.1 1.5 %collective-permute-start.16 = (bf16[144,1024]{1,0:T(8,128)(2,1)S(1)}, bf16[144,1024]{1,0:T(8,128)(2,1)S(1)}, u32[]{:S(2)}, u32[]{:S(2)}) collective-permute-start(bf16[144,1024]{1,0:T(8,128)(2,1)S(1)} %get-tuple-element.90), channel_id=1, source_target_pairs={{0,4},{2,6},{4,0},{6,2},{8,12},{10,14},{12,8},{14,10},{16,20},{18,... | collective-permute-start | bytes 884744 | tf_op jit(solution)/shard_map/piece_b0/ppermute | solution.py:474
  60.6 0.5 collective-permute-start.22
  61.1 3.9 %collective-permute-done.25.refs_3_ = bf16[128,1024]{1,0:T(8,128)(2,1)S(1)} collective-permute-done((bf16[128,1024]{1,0:T(8,128)(2,1)S(1)}, bf16[128,1024]{1,0:T(8,128)(2,1)S(1)}, u32[]{:S(2)}, u32[]{:S(2)}) %collective-permute-start.25) | collective-permute-done | bytes 262176 | tf_op jit(solution)/shard_map/side_b2/ppermute | solution.py:470
  65.1 1.2 collective-permute-done.23.refs_6_.refs_2_
  66.3 0.5 collective-permute-start.24
  66.8 2.2 %collective-permute-done.16.refs_5_.refs_1_ = bf16[144,1024]{1,0:T(8,128)(2,1)S(1)} collective-permute-done((bf16[144,1024]{1,0:T(8,128)(2,1)S(1)}, bf16[144,1024]{1,0:T(8,128)(2,1)S(1)}, u32[]{:S(2)}, u32[]{:S(2)}) %collective-permute-start.16) | collective-permute-done | bytes 294944 | tf_op jit(solution)/shard_map/piece_b0/ppermute | solution.py:474
  69.4 1.6 %collective-permute-start.26 = (bf16[144,1024]{1,0:T(8,128)(2,1)S(1)}, bf16[144,1024]{1,0:T(8,128)(2,1)S(1)}, u32[]{:S(2)}, u32[]{:S(2)}) collective-permute-start(bf16[144,1024]{1,0:T(8,128)(2,1)S(1)} %get-tuple-element.98), channel_id=1, source_target_pairs={{0,4},{2,6},{4,0},{6,2},{8,12},{10,14},{12,8},{14,10},{16,20},{18,... | collective-permute-start | bytes 884744 | tf_op jit(solution)/shard_map/piece_b2/ppermute | solution.py:474
  71.0 3.7 %collective-permute-done.20.refs_6_.refs_2_ = bf16[128,1024]{1,0:T(8,128)(2,1)S(1)} collective-permute-done((bf16[128,1024]{1,0:T(8,128)(2,1)S(1)}, bf16[128,1024]{1,0:T(8,128)(2,1)S(1)}, u32[]{:S(2)}, u32[]{:S(2)}) %collective-permute-start.20) | collective-permute-done | bytes 262176 | tf_op jit(solution)/shard_map/plane_b1/ppermute | solution.py:459
  74.7 1.5 %collective-permute-start.21 = (bf16[128,1024]{1,0:T(8,128)(2,1)S(1)}, bf16[128,1024]{1,0:T(8,128)(2,1)S(1)}, u32[]{:S(2)}, u32[]{:S(2)}) collective-permute-start(bf16[128,1024]{1,0:T(8,128)(2,1)S(1)} %collective-permute-done.20.refs_6_.refs_2_), channel_id=1, source_target_pairs={{0,2},{2,0},{4,6},{6,4},{8,10},{10,8},{12,14},{14,12},{16,18},{18,... | collective-permute-start | bytes 786440 | tf_op jit(solution)/shard_map/side_b1/ppermute | solution.py:470
  76.7 1.6 %collective-permute-start.29 = (bf16[144,1024]{1,0:T(8,128)(2,1)S(1)}, bf16[144,1024]{1,0:T(8,128)(2,1)S(1)}, u32[]{:S(2)}, u32[]{:S(2)}) collective-permute-start(bf16[144,1024]{1,0:T(8,128)(2,1)S(1)} %get-tuple-element.104), channel_id=1, source_target_pairs={{0,4},{2,6},{4,0},{6,2},{8,12},{10,14},{12,8},{14,10},{16,20},{18,... | collective-permute-start | bytes 884744 | tf_op jit(solution)/shard_map/piece_b3/ppermute | solution.py:474
  78.3 4.9 %forward_rows.3 = (bf16[576,1024]{1,0:T(8,128)(2,1)S(1)}, bf16[576,1536]{1,0:T(8,128)(2,1)S(1)}, bf16[576,1536]{1,0:T(8,128)(2,1)S(1)}, bf16[576,1536]{1,0:T(8,128)(2,1)S(1)}, f32[8,128]{1,0:T(8,128)S(1)}) custom-call(bf16[144,1024]{1,0:T(8,128)(2,1)S(1)} %get-tuple-element.87.refs_4_.refs_0_, bf16[144,1024]{1,0:T(8,128)(2,1)S(1)} %collective-permute-done.18.refs_5_.refs_1_, ...), custom_call_target="tpu_custom_call" | custom-call | flops 3623878656 | bytes 11599873 | tf_op jit(solution)/shard_map/forward_rows/pallas_call | solution.py:287
  83.2 0.5 select_back.7
  83.7 0.6 collective-permute-start.28
  84.3 3.6 %collective-permute-done.29.refs_1_ = bf16[144,1024]{1,0:T(8,128)(2,1)S(1)} collective-permute-done((bf16[144,1024]{1,0:T(8,128)(2,1)S(1)}, bf16[144,1024]{1,0:T(8,128)(2,1)S(1)}, u32[]{:S(2)}, u32[]{:S(2)}) %collective-permute-start.29) | collective-permute-done | bytes 294944 | tf_op jit(solution)/shard_map/piece_b3/ppermute | solution.py:474
  87.9 5.9 %backward_rows.2 = (bf16[576,1024]{1,0:T(8,128)(2,1)S(1)}, bf16[576,1536]{1,0:T(8,128)(2,1)S(1)}, bf16[576,1536]{1,0:T(8,128)(2,1)S(1)}, bf16[144,1024]{1,0:T(8,...) custom-call(bf16[144,1024]{1,0:T(8,128)(2,1)S(1)} %get-tuple-element, ...), custom_call_target="tpu_custom_call" | custom-call | flops 5435817984 | bytes 16515073 | tf_op jit(solution)/shard_map/backward_rows/pallas_call | solution.py:334
  93.9 1.6 %collective-permute-start.30 = (bf16[144,1024]{1,0:T(8,128)(2,1)S(1)}, bf16[144,1024]{1,0:T(8,128)(2,1)S(1)}, u32[]{:S(2)}, u32[]{:S(2)}) collective-permute-start(bf16[144,1024]{1,0:T(8,128)(2,1)S(1)} %get-tuple-element.112), channel_id=1, source_target_pairs={{0,4},{2,6},{4,0},{6,2},{8,12},{10,14},{12,8},{14,10},{16,20},{18,... | collective-permute-start | bytes 884744 | tf_op jit(solution)/shard_map/piece_r3/ppermute | solution.py:474
  95.4 5.9 %backward_rows.3 = (bf16[576,1024]{1,0:T(8,128)(2,1)S(1)}, bf16[576,1536]{1,0:T(8,128)(2,1)S(1)}, bf16[576,1536]{1,0:T(8,128)(2,1)S(1)}, bf16[144,1024]{1,0:T(8,...) custom-call(bf16[144,1024]{1,0:T(8,128)(2,1)S(1)} %get-tuple-element, ...), custom_call_target="tpu_custom_call" | custom-call | flops 5435817984 | bytes 16515073 | tf_op jit(solution)/shard_map/backward_rows/pallas_call | solution.py:334
  101.4 0.5 return_rows.4
  101.9 0.6 collective-permute-start.32
  102.5 0.9 collective-permute-start.31
  103.4 5.5 %weight_grads.4 = (bf16[1024,1536]{1,0:T(8,128)(2,1)S(1)}, f32[8,128]{1,0:T(8,128)S(1)}) custom-call(bf16[576,1024]{1,0:T(8,128)(2,1)S(1)} %get-tuple-element.119.refs_0_, bf16[576,1024]{1,0:T(8,128)(2,1)S(1)} %get-tuple-element.120.refs_1_, bf16[576,1536]{1,0:T(8,128)(2,1)S(1)} %get-tuple-element.121.refs_2_, ...), custom_call_target="tpu_custom_call" | custom-call | flops 3623878656 | bytes 7077889 | tf_op jit(solution)/shard_map/weight_grads/pallas_call | solution.py:388
  109.3 0.6 return_rows.5
  109.9 0.9 collective-permute-start.33
  110.9 1.5 %collective-permute-start.34 = (bf16[128,1024]{1,0:T(8,128)(2,1)S(1)}, bf16[128,1024]{1,0:T(8,128)(2,1)S(1)}, u32[]{:S(2)}, u32[]{:S(2)}) collective-permute-start(bf16[128,1024]{1,0:T(8,128)(2,1)S(1)} %get-tuple-element.133), channel_id=1, source_target_pairs={{0,2},{2,0},{4,6},{6,4},{8,10},{10,8},{12,14},{14,12},{16,18},{18,... | collective-permute-start | bytes 786440 | tf_op jit(solution)/shard_map/side_r2/ppermute | solution.py:470
  112.3 0.8 collective-permute-start.35
  113.2 3.0 %weight_grads.5 = (bf16[1536,512]{1,0:T(8,128)(2,1)S(1)}, f32[8,128]{1,0:T(8,128)S(1)}) custom-call(bf16[576,1024]{1,0:T(8,128)(2,1)S(1)} %get-tuple-element.119.refs_0_, bf16[576,1024]{1,0:T(8,128)(2,1)S(1)} %get-tuple-element.120.refs_1_, bf16[576,1536]{1,0:T(8,128)(2,1)S(1)} %get-tuple-element.121.refs_2_, ...), custom_call_target="tpu_custom_call" | custom-call | flops 1811939328 | bytes 7077889 | tf_op jit(solution)/shard_map/weight_grads/pallas_call | solution.py:388
  116.2 3.0 %collective-permute-done.34.refs_5_ = bf16[128,1024]{1,0:T(8,128)(2,1)S(1)} collective-permute-done((bf16[128,1024]{1,0:T(8,128)(2,1)S(1)}, bf16[128,1024]{1,0:T(8,128)(2,1)S(1)}, u32[]{:S(2)}, u32[]{:S(2)}) %collective-permute-start.34) | collective-permute-done | bytes 262176 | tf_op jit(solution)/shard_map/side_r2/ppermute | solution.py:470
  119.2 3.0 %collective-permute-done.35.refs_9_.refs_4_ = bf16[128,1024]{1,0:T(8,128)(2,1)S(1)} collective-permute-done((bf16[128,1024]{1,0:T(8,128)(2,1)S(1)}, bf16[128,1024]{1,0:T(8,128)(2,1)S(1)}, u32[]{:S(2)}, u32[]{:S(2)}) %collective-permute-start.35) | collective-permute-done | bytes 262176 | tf_op jit(solution)/shard_map/plane_r3/ppermute | solution.py:459
  122.2 0.6 return_rows.6
  122.9 0.6 collective-permute-start.37
  123.5 1.1 collective-permute-start.36
  124.6 7.2 %weight_grads.6 = (bf16[512,1536]{1,0:T(8,128)(2,1)}, bf16[512,1536]{1,0:T(8,128)(2,1)}, f32[8,128]{1,0:T(8,128)S(1)}) custom-call(bf16[576,1024]{1,0:T(8,128)(2,1)S(1)} %get-tuple-element.119.refs_0_, bf16[576,1024]{1,0:T(8,128)(2,1)S(1)} %get-tuple-element.120.refs_1_, bf16[576,1536]{1,0:T(8,128)(2,1)S(1)} %get-tuple-element.121.refs_2_, ...), custom_call_target="tpu_custom_call" | custom-call | flops 3623878656 | bytes 7077889 | tf_op jit(solution)/shard_map/weight_grads/pallas_call | solution.py:388
  131.8 0.7 collective-permute-done.36.refs_3_
  132.6 0.6 return_rows.7
  133.1 1.6 %collective-permute-start.39 = (bf16[128,1024]{1,0:T(8,128)(2,1)S(1)}, bf16[128,1024]{1,0:T(8,128)(2,1)S(1)}, u32[]{:S(2)}, u32[]{:S(2)}) collective-permute-start(bf16[128,1024]{1,0:T(8,128)(2,1)S(1)} %get-tuple-element.144), channel_id=1, source_target_pairs={{0,2},{2,0},{4,6},{6,4},{8,10},{10,8},{12,14},{14,12},{16,18},{18,... | collective-permute-start | bytes 786440 | tf_op jit(solution)/shard_map/side_r0/ppermute | solution.py:470
  134.7 1.1 collective-permute-start.40
  135.8 4.2 %weight_grads.7 = (bf16[1536,512]{1,0:T(8,128)(2,1)}, f32[8,128]{1,0:T(8,128)S(1)}) custom-call(bf16[576,1024]{1,0:T(8,128)(2,1)S(1)} %get-tuple-element.119.refs_0_, bf16[576,1024]{1,0:T(8,128)(2,1)S(1)} %get-tuple-element.120.refs_1_, bf16[576,1536]{1,0:T(8,128)(2,1)S(1)} %get-tuple-element.121.refs_2_, bf16[576,1536]{1,0:T(8,128)(2,1)S(1)} %get-tuple-element.122.refs_3_, ...), custom_call_target="tpu_custom_call" | custom-call | flops 1811939328 | bytes 7077889 | tf_op jit(solution)/shard_map/weight_grads/pallas_call | solution.py:388
  140.0 0.7 collective-permute-done.39.refs_1_
  140.8 1.7 %collective-permute-done.40.refs_2_ = bf16[128,1024]{1,0:T(8,128)(2,1)S(1)} collective-permute-done((bf16[128,1024]{1,0:T(8,128)(2,1)S(1)}, bf16[128,1024]{1,0:T(8,128)(2,1)S(1)}, u32[]{:S(2)}, u32[]{:S(2)}) %collective-permute-start.40) | collective-permute-done | bytes 262176 | tf_op jit(solution)/shard_map/plane_r1/ppermute | solution.py:459
  142.5 3.8 %token_grad.1 = bf16[128,4096]{1,0:T(8,128)(2,1)} custom-call(f32[128,1024]{1,0:T(8,128)S(1)} %get-tuple-element.143.refs_11_.refs_0_, bf16[128,1024]{1,0:T(8,128)(2,1)S(1)} %collective-permute-done.39.refs_1_, bf16[128,1024]{1,0:T(8,128)(2,1)S(1)} %collective-permute-done.40.refs_2_, bf16[128,1024]{1,0:T(8,128)(2,1)S(1)} %collective-permute-done.41.refs_3_, ...), custom_call_target="tpu_custom_call" | custom-call | flops 1073741824 | bytes 8388609 | tf_op jit(solution)/shard_map/token_grad/pallas_call | solution.py:421
  (72 shorter events, 5.0 us)
Async XLA Ops:
  0.6 4.1 %copy-start = (bf16[4096,512]{1,0:T(8,128)(2,1)S(1)}, bf16[4096,512]{1,0:T(8,128)(2,1)}, u32[]{:S(2)}) copy-start(bf16[4096,512]{1,0:T(8,128)(2,1)} %refs_5_) | copy-start | bytes 12582916
  0.6 4.1 %collective-permute-start = (bf16[128,4096]{1,0:T(8,128)(2,1)}, bf16[128,4096]{1,0:T(8,128)(2,1)S(1)}, u32[]{:S(2)}, u32[]{:S(2)}) collective-permute-start(bf16[128,4096]{1,0:T(8,128)(2,1)} %param.10), channel_id=1, source_target_pairs={{0,1},{1,0},{2,3},{3,2},{4,5},{5,4},{6,7},{7,6},{8,9},{9,8},{10,11... | collective-permute-start | bytes 3145736 | tf_op jit(solution)/shard_map/ppermute | solution.py:456
  4.6 2.2 %copy-start.1 = (s32[128,8]{0,1:T(8,128)S(1)}, s32[128,8]{0,1:T(8,128)}, u32[]{:S(2)}) copy-start(s32[128,8]{0,1:T(8,128)} %param.12) | copy-start | bytes 12292
  4.7 2.2 %copy-start.2 = (s32[128,8]{0,1:T(8,128)S(1)}, s32[128,8]{0,1:T(8,128)}, u32[]{:S(2)}) copy-start(s32[128,8]{0,1:T(8,128)} %param.13) | copy-start | bytes 12292
  4.7 2.2 %copy-start.3 = (f32[128,8]{0,1:T(8,128)S(1)}, f32[128,8]{0,1:T(8,128)}, u32[]{:S(2)}) copy-start(f32[128,8]{0,1:T(8,128)} %param.14) | copy-start | bytes 12292
  4.7 2.3 %copy-start.4 = (bf16[1,512,1536]{2,1,0:T(8,128)(2,1)S(1)}, bf16[1,512,1536]{2,1,0:T(8,128)(2,1)}, u32[]{:S(2)}) copy-start(bf16[1,512,1536]{2,1,0:T(8,128)(2,1)} %param.17) | copy-start | bytes 4718596
  4.7 2.5 %copy-start.8 = (bf16[128,4096]{1,0:T(8,128)(2,1)S(1)}, bf16[128,4096]{1,0:T(8,128)(2,1)}, u32[]{:S(2)}) copy-start(bf16[128,4096]{1,0:T(8,128)(2,1)} %param.11) | copy-start | bytes 3145732
  4.7 2.8 %copy-start.6 = (bf16[1,1536,512]{2,1,0:T(8,128)(2,1)S(1)}, bf16[1,1536,512]{2,1,0:T(8,128)(2,1)}, u32[]{:S(2)}) copy-start(bf16[1,1536,512]{2,1,0:T(8,128)(2,1)} %param.19) | copy-start | bytes 4718596
  4.7 3.0 %copy-start.5 = (bf16[1,512,1536]{2,1,0:T(8,128)(2,1)S(1)}, bf16[1,512,1536]{2,1,0:T(8,128)(2,1)}, u32[]{:S(2)}) copy-start(bf16[1,512,1536]{2,1,0:T(8,128)(2,1)} %param.18) | copy-start | bytes 4718596
  5.5 1.4 collective-permute-start.1
  6.9 7.7 %copy-start.7 = (bf16[512,4096]{1,0:T(8,128)(2,1)S(1)}, bf16[512,4096]{1,0:T(8,128)(2,1)}, u32[]{:S(2)}) copy-start(bf16[512,4096]{1,0:T(8,128)(2,1)} %param.16) | copy-start | bytes 12582916
  7.0 9.4 %collective-permute-start.5 = (bf16[512,1536]{1,0:T(8,128)(2,1)S(1)}, bf16[512,1536]{1,0:T(8,128)(2,1)S(1)}, u32[]{:S(2)}, u32[]{:S(2)}) collective-permute-start(bf16[512,1536]{1,0:T(8,128)(2,1)S(1)} %bitcast.20), channel_id=1, source_target_pairs={{0,1},{1,0},{2,3},{3,2},{4,5},{5,4},{6,7},{7,6},{8,9},{9,8},{10,11... | collective-permute-start | bytes 4718600 | tf_op jit(solution)/shard_map/ppermute | solution.py:456
  7.2 7.5 %collective-permute-start.3 = (bf16[128,4096]{1,0:T(8,128)(2,1)S(1)}, bf16[128,4096]{1,0:T(8,128)(2,1)S(1)}, u32[]{:S(2)}, u32[]{:S(2)}) collective-permute-start(bf16[128,4096]{1,0:T(8,128)(2,1)S(1)} %copy-done.8), channel_id=1, source_target_pairs={{0,1},{1,0},{2,3},{3,2},{4,5},{5,4},{6,7},{7,6},{8,9},{9,8},{10,11... | collective-permute-start | bytes 3145736 | tf_op jit(solution)/shard_map/ppermute | solution.py:456
  7.5 18.7 %collective-permute-start.12 = (bf16[1536,512]{1,0:T(8,128)(2,1)S(1)}, bf16[1536,512]{1,0:T(8,128)(2,1)S(1)}, u32[]{:S(2)}, u32[]{:S(2)}) collective-permute-start(bf16[1536,512]{1,0:T(8,128)(2,1)S(1)} %bitcast.30), channel_id=1, source_target_pairs={{0,1},{1,0},{2,3},{3,2},{4,5},{5,4},{6,7},{7,6},{8,9},{9,8},{10,11... | collective-permute-start | bytes 4718600 | tf_op jit(solution)/shard_map/ppermute | solution.py:456
  7.7 18.5 %collective-permute-start.11 = (bf16[512,1536]{1,0:T(8,128)(2,1)S(1)}, bf16[512,1536]{1,0:T(8,128)(2,1)S(1)}, u32[]{:S(2)}, u32[]{:S(2)}) collective-permute-start(bf16[512,1536]{1,0:T(8,128)(2,1)S(1)} %bitcast.25), channel_id=1, source_target_pairs={{0,1},{1,0},{2,3},{3,2},{4,5},{5,4},{6,7},{7,6},{8,9},{9,8},{10,11... | collective-permute-start | bytes 4718600 | tf_op jit(solution)/shard_map/ppermute | solution.py:456
  8.1 13.4 %collective-permute-start.9 = (bf16[144,1024]{1,0:T(8,128)(2,1)S(1)}, bf16[144,1024]{1,0:T(8,128)(2,1)S(1)}, u32[]{:S(2)}, u32[]{:S(2)}) collective-permute-start(bf16[144,1024]{1,0:T(8,128)(2,1)S(1)} %join_rows.2.block_ref.refs_0_.refs_2_), channel_id=1, source_target_pairs={{0,8},{2,10},{4,12},{6,14},{8,16},{10,18},{12,20},{14,22},{16,24},... | collective-permute-start | bytes 884744 | tf_op jit(solution)/shard_map/plane_l1/ppermute | solution.py:459
  16.2 1.7 %collective-permute-start.4 = (bf16[128,512]{1,0:T(8,128)(2,1)S(1)}, bf16[128,512]{1,0:T(8,128)(2,1)S(1)}, u32[]{:S(2)}, u32[]{:S(2)}) collective-permute-start(bf16[128,512]{1,0:T(8,128)(2,1)S(1)} %convolution_convert_fusion.refs_0_), channel_id=1, source_target_pairs={{0,1},{1,0},{2,3},{3,2},{4,5},{5,4},{6,7},{7,6},{8,9},{9,8},{10,11... | collective-permute-start | bytes 393224 | tf_op jit(solution)/shard_map/ppermute | solution.py:456
  16.4 9.8 %collective-permute-start.2 = (bf16[144,1024]{1,0:T(8,128)(2,1)S(1)}, bf16[144,1024]{1,0:T(8,128)(2,1)S(1)}, u32[]{:S(2)}, u32[]{:S(2)}) collective-permute-start(bf16[144,1024]{1,0:T(8,128)(2,1)S(1)} %join_rows.2.block_ref.refs_0_.refs_2_), channel_id=1, source_target_pairs={{0,2},{2,0},{4,6},{6,4},{8,10},{10,8},{12,14},{14,12},{16,18},{18,... | collective-permute-start | bytes 884744 | tf_op jit(solution)/shard_map/side_l0/ppermute | solution.py:470
  17.9 13.0 %collective-permute-start.7 = (bf16[144,1024]{1,0:T(8,128)(2,1)S(1)}, bf16[144,1024]{1,0:T(8,128)(2,1)S(1)}, u32[]{:S(2)}, u32[]{:S(2)}) collective-permute-start(bf16[144,1024]{1,0:T(8,128)(2,1)S(1)} %tie_rows.5.refs_0_), channel_id=1, source_target_pairs={{0,24},{2,26},{4,28},{6,30},{8,0},{10,2},{12,4},{14,6},{16,8},{18,... | collective-permute-start | bytes 884744 | tf_op jit(solution)/shard_map/plane_l3/ppermute | solution.py:459
  21.5 10.9 %collective-permute-start.10 = (bf16[144,1024]{1,0:T(8,128)(2,1)S(1)}, bf16[144,1024]{1,0:T(8,128)(2,1)S(1)}, u32[]{:S(2)}, u32[]{:S(2)}) collective-permute-start(bf16[144,1024]{1,0:T(8,128)(2,1)S(1)} %collective-permute-done.9.refs_5_.refs_1_.refs_0_.refs_2_), channel_id=1, source_target_pairs={{0,2},{2,0},{4,6},{6,4},{8,10},{10,8},{12,14},{14,12},{16,18},{18,... | collective-permute-start | bytes 884744 | tf_op jit(solution)/shard_map/side_l1/ppermute | solution.py:470
  26.7 15.4 %collective-permute-start.15 = (bf16[144,1024]{1,0:T(8,128)(2,1)S(1)}, bf16[144,1024]{1,0:T(8,128)(2,1)S(1)}, u32[]{:S(2)}, u32[]{:S(2)}) collective-permute-start(bf16[144,1024]{1,0:T(8,128)(2,1)S(1)} %tie_rows.6.refs_4_), channel_id=1, source_target_pairs={{0,16},{2,18},{4,20},{6,22},{8,24},{10,26},{12,28},{14,30},{16,0},... | collective-permute-start | bytes 884744 | tf_op jit(solution)/shard_map/plane_l2/ppermute | solution.py:459
  29.4 12.7 %collective-permute-start.13 = (bf16[144,1024]{1,0:T(8,128)(2,1)S(1)}, bf16[144,1024]{1,0:T(8,128)(2,1)S(1)}, u32[]{:S(2)}, u32[]{:S(2)}) collective-permute-start(bf16[144,1024]{1,0:T(8,128)(2,1)S(1)} %get-tuple-element.86), channel_id=1, source_target_pairs={{0,4},{2,6},{4,0},{6,2},{8,12},{10,14},{12,8},{14,10},{16,20},{18,... | collective-permute-start | bytes 884744 | tf_op jit(solution)/shard_map/piece_l0/ppermute | solution.py:474
  30.9 12.7 %collective-permute-start.8 = (bf16[144,1024]{1,0:T(8,128)(2,1)S(1)}, bf16[144,1024]{1,0:T(8,128)(2,1)S(1)}, u32[]{:S(2)}, u32[]{:S(2)}) collective-permute-start(bf16[144,1024]{1,0:T(8,128)(2,1)S(1)} %collective-permute-done.7.refs_5_.refs_1_.refs_0_.refs_2_), channel_id=1, source_target_pairs={{0,2},{2,0},{4,6},{6,4},{8,10},{10,8},{12,14},{14,12},{16,18},{18,... | collective-permute-start | bytes 884744 | tf_op jit(solution)/shard_map/side_l3/ppermute | solution.py:470
  32.8 12.8 %collective-permute-start.14 = (bf16[144,1024]{1,0:T(8,128)(2,1)S(1)}, bf16[144,1024]{1,0:T(8,128)(2,1)S(1)}, u32[]{:S(2)}, u32[]{:S(2)}) collective-permute-start(bf16[144,1024]{1,0:T(8,128)(2,1)S(1)} %get-tuple-element.88), channel_id=1, source_target_pairs={{0,4},{2,6},{4,0},{6,2},{8,12},{10,14},{12,8},{14,10},{16,20},{18,... | collective-permute-start | bytes 884744 | tf_op jit(solution)/shard_map/piece_l1/ppermute | solution.py:474
  34.6 11.1 %collective-permute-start.6 = (bf16[128,1024]{1,0:T(8,128)(2,1)S(1)}, bf16[128,1024]{1,0:T(8,128)(2,1)S(1)}, u32[]{:S(2)}, u32[]{:S(2)}) collective-permute-start(bf16[128,1024]{1,0:T(8,128)(2,1)S(1)} %join_rows.3.refs_4_.block_ref.refs_2_), channel_id=1, source_target_pairs={{0,2},{2,0},{4,6},{6,4},{8,10},{10,8},{12,14},{14,12},{16,18},{18,... | collective-permute-start | bytes 786440 | tf_op jit(solution)/shard_map/side_b0/ppermute | solution.py:470
  42.1 13.7 %collective-permute-start.19 = (bf16[128,1024]{1,0:T(8,128)(2,1)S(1)}, bf16[128,1024]{1,0:T(8,128)(2,1)S(1)}, u32[]{:S(2)}, u32[]{:S(2)}) collective-permute-start(bf16[128,1024]{1,0:T(8,128)(2,1)S(1)} %tie_rows.7.refs_4_), channel_id=1, source_target_pairs={{0,16},{2,18},{4,20},{6,22},{8,24},{10,26},{12,28},{14,30},{16,0},... | collective-permute-start | bytes 786440 | tf_op jit(solution)/shard_map/plane_b2/ppermute | solution.py:459
  42.1 13.7 %collective-permute-start.17 = (bf16[144,1024]{1,0:T(8,128)(2,1)S(1)}, bf16[144,1024]{1,0:T(8,128)(2,1)S(1)}, u32[]{:S(2)}, u32[]{:S(2)}) collective-permute-start(bf16[144,1024]{1,0:T(8,128)(2,1)S(1)} %collective-permute-done.15.refs_6_.refs_1_.refs_0_.refs_2_), channel_id=1, source_target_pairs={{0,2},{2,0},{4,6},{6,4},{8,10},{10,8},{12,14},{14,12},{16,18},{18,... | collective-permute-start | bytes 884744 | tf_op jit(solution)/shard_map/side_l2/ppermute | solution.py:470
  44.1 11.7 %collective-permute-start.18 = (bf16[144,1024]{1,0:T(8,128)(2,1)S(1)}, bf16[144,1024]{1,0:T(8,128)(2,1)S(1)}, u32[]{:S(2)}, u32[]{:S(2)}) collective-permute-start(bf16[144,1024]{1,0:T(8,128)(2,1)S(1)} %get-tuple-element.92), channel_id=1, source_target_pairs={{0,4},{2,6},{4,0},{6,2},{8,12},{10,14},{12,8},{14,10},{16,20},{18,... | collective-permute-start | bytes 884744 | tf_op jit(solution)/shard_map/piece_l3/ppermute | solution.py:474
  56.3 27.0 %collective-permute-start.27 = (bf16[4096,512]{1,0:T(8,128)(2,1)S(1)}, bf16[4096,512]{1,0:T(8,128)(2,1)S(1)}, u32[]{:S(2)}, u32[]{:S(2)}) collective-permute-start(bf16[4096,512]{1,0:T(8,128)(2,1)S(1)} %copy-done), channel_id=1, source_target_pairs={{0,1},{1,0},{2,3},{3,2},{4,5},{5,4},{6,7},{7,6},{8,9},{9,8},{10,11... | collective-permute-start | bytes 12582920 | tf_op jit(solution)/shard_map/ppermute | solution.py:456
  56.3 8.7 %collective-permute-start.25 = (bf16[128,1024]{1,0:T(8,128)(2,1)S(1)}, bf16[128,1024]{1,0:T(8,128)(2,1)S(1)}, u32[]{:S(2)}, u32[]{:S(2)}) collective-permute-start(bf16[128,1024]{1,0:T(8,128)(2,1)S(1)} %collective-permute-done.19.refs_6_.refs_1_.refs_2_), channel_id=1, source_target_pairs={{0,2},{2,0},{4,6},{6,4},{8,10},{10,8},{12,14},{14,12},{16,18},{18,... | collective-permute-start | bytes 786440 | tf_op jit(solution)/shard_map/side_b2/ppermute | solution.py:470
  57.9 8.4 %collective-permute-start.23 = (bf16[128,1024]{1,0:T(8,128)(2,1)S(1)}, bf16[128,1024]{1,0:T(8,128)(2,1)S(1)}, u32[]{:S(2)}, u32[]{:S(2)}) collective-permute-start(bf16[128,1024]{1,0:T(8,128)(2,1)S(1)} %tie_rows.8.refs_8_), channel_id=1, source_target_pairs={{0,24},{2,26},{4,28},{6,30},{8,0},{10,2},{12,4},{14,6},{16,8},{18,... | collective-permute-start | bytes 786440 | tf_op jit(solution)/shard_map/plane_b3/ppermute | solution.py:459
  59.1 9.9 %collective-permute-start.16 = (bf16[144,1024]{1,0:T(8,128)(2,1)S(1)}, bf16[144,1024]{1,0:T(8,128)(2,1)S(1)}, u32[]{:S(2)}, u32[]{:S(2)}) collective-permute-start(bf16[144,1024]{1,0:T(8,128)(2,1)S(1)} %get-tuple-element.90), channel_id=1, source_target_pairs={{0,4},{2,6},{4,0},{6,2},{8,12},{10,14},{12,8},{14,10},{16,20},{18,... | collective-permute-start | bytes 884744 | tf_op jit(solution)/shard_map/piece_b0/ppermute | solution.py:474
  60.6 15.6 %collective-permute-start.22 = (bf16[144,1024]{1,0:T(8,128)(2,1)S(1)}, bf16[144,1024]{1,0:T(8,128)(2,1)S(1)}, u32[]{:S(2)}, u32[]{:S(2)}) collective-permute-start(bf16[144,1024]{1,0:T(8,128)(2,1)S(1)} %get-tuple-element.94), channel_id=1, source_target_pairs={{0,4},{2,6},{4,0},{6,2},{8,12},{10,14},{12,8},{14,10},{16,20},{18,... | collective-permute-start | bytes 884744 | tf_op jit(solution)/shard_map/piece_l2/ppermute | solution.py:474
  65.1 9.7 %collective-permute-start.20 = (bf16[128,1024]{1,0:T(8,128)(2,1)S(1)}, bf16[128,1024]{1,0:T(8,128)(2,1)S(1)}, u32[]{:S(2)}, u32[]{:S(2)}) collective-permute-start(bf16[128,1024]{1,0:T(8,128)(2,1)S(1)} %tie_rows.9.refs_4_), channel_id=1, source_target_pairs={{0,8},{2,10},{4,12},{6,14},{8,16},{10,18},{12,20},{14,22},{16,24},... | collective-permute-start | bytes 786440 | tf_op jit(solution)/shard_map/plane_b1/ppermute | solution.py:459
  66.3 10.0 %collective-permute-start.24 = (bf16[128,1024]{1,0:T(8,128)(2,1)S(1)}, bf16[128,1024]{1,0:T(8,128)(2,1)S(1)}, u32[]{:S(2)}, u32[]{:S(2)}) collective-permute-start(bf16[128,1024]{1,0:T(8,128)(2,1)S(1)} %collective-permute-done.23.refs_6_.refs_2_), channel_id=1, source_target_pairs={{0,2},{2,0},{4,6},{6,4},{8,10},{10,8},{12,14},{14,12},{16,18},{18,... | collective-permute-start | bytes 786440 | tf_op jit(solution)/shard_map/side_b3/ppermute | solution.py:470
  69.4 13.7 %collective-permute-start.26 = (bf16[144,1024]{1,0:T(8,128)(2,1)S(1)}, bf16[144,1024]{1,0:T(8,128)(2,1)S(1)}, u32[]{:S(2)}, u32[]{:S(2)}) collective-permute-start(bf16[144,1024]{1,0:T(8,128)(2,1)S(1)} %get-tuple-element.98), channel_id=1, source_target_pairs={{0,4},{2,6},{4,0},{6,2},{8,12},{10,14},{12,8},{14,10},{16,20},{18,... | collective-permute-start | bytes 884744 | tf_op jit(solution)/shard_map/piece_b2/ppermute | solution.py:474
  74.7 8.5 %collective-permute-start.21 = (bf16[128,1024]{1,0:T(8,128)(2,1)S(1)}, bf16[128,1024]{1,0:T(8,128)(2,1)S(1)}, u32[]{:S(2)}, u32[]{:S(2)}) collective-permute-start(bf16[128,1024]{1,0:T(8,128)(2,1)S(1)} %collective-permute-done.20.refs_6_.refs_2_), channel_id=1, source_target_pairs={{0,2},{2,0},{4,6},{6,4},{8,10},{10,8},{12,14},{14,12},{16,18},{18,... | collective-permute-start | bytes 786440 | tf_op jit(solution)/shard_map/side_b1/ppermute | solution.py:470
  76.7 11.2 %collective-permute-start.29 = (bf16[144,1024]{1,0:T(8,128)(2,1)S(1)}, bf16[144,1024]{1,0:T(8,128)(2,1)S(1)}, u32[]{:S(2)}, u32[]{:S(2)}) collective-permute-start(bf16[144,1024]{1,0:T(8,128)(2,1)S(1)} %get-tuple-element.104), channel_id=1, source_target_pairs={{0,4},{2,6},{4,0},{6,2},{8,12},{10,14},{12,8},{14,10},{16,20},{18,... | collective-permute-start | bytes 884744 | tf_op jit(solution)/shard_map/piece_b3/ppermute | solution.py:474
  83.7 11.8 %collective-permute-start.28 = (bf16[144,1024]{1,0:T(8,128)(2,1)S(1)}, bf16[144,1024]{1,0:T(8,128)(2,1)S(1)}, u32[]{:S(2)}, u32[]{:S(2)}) collective-permute-start(bf16[144,1024]{1,0:T(8,128)(2,1)S(1)} %get-tuple-element.101), channel_id=1, source_target_pairs={{0,4},{2,6},{4,0},{6,2},{8,12},{10,14},{12,8},{14,10},{16,20},{18,... | collective-permute-start | bytes 884744 | tf_op jit(solution)/shard_map/piece_b1/ppermute | solution.py:474
  93.9 7.5 %collective-permute-start.30 = (bf16[144,1024]{1,0:T(8,128)(2,1)S(1)}, bf16[144,1024]{1,0:T(8,128)(2,1)S(1)}, u32[]{:S(2)}, u32[]{:S(2)}) collective-permute-start(bf16[144,1024]{1,0:T(8,128)(2,1)S(1)} %get-tuple-element.112), channel_id=1, source_target_pairs={{0,4},{2,6},{4,0},{6,2},{8,12},{10,14},{12,8},{14,10},{16,20},{18,... | collective-permute-start | bytes 884744 | tf_op jit(solution)/shard_map/piece_r3/ppermute | solution.py:474
  101.9 7.0 %collective-permute-start.32 = (bf16[128,1024]{1,0:T(8,128)(2,1)S(1)}, bf16[128,1024]{1,0:T(8,128)(2,1)S(1)}, u32[]{:S(2)}, u32[]{:S(2)}) collective-permute-start(bf16[128,1024]{1,0:T(8,128)(2,1)S(1)} %get-tuple-element.117), channel_id=1, source_target_pairs={{0,2},{2,0},{4,6},{6,4},{8,10},{10,8},{12,14},{14,12},{16,18},{18,... | collective-permute-start | bytes 786440 | tf_op jit(solution)/shard_map/side_r3/ppermute | solution.py:470
  102.5 6.7 %collective-permute-start.31 = (bf16[144,1024]{1,0:T(8,128)(2,1)S(1)}, bf16[144,1024]{1,0:T(8,128)(2,1)S(1)}, u32[]{:S(2)}, u32[]{:S(2)}) collective-permute-start(bf16[144,1024]{1,0:T(8,128)(2,1)S(1)} %get-tuple-element.115), channel_id=1, source_target_pairs={{0,4},{2,6},{4,0},{6,2},{8,12},{10,14},{12,8},{14,10},{16,20},{18,... | collective-permute-start | bytes 884744 | tf_op jit(solution)/shard_map/piece_r2/ppermute | solution.py:474
  109.8 14.8 %collective-permute-start.38 = (bf16[1024,1536]{1,0:T(8,128)(2,1)S(1)}, bf16[1024,1536]{1,0:T(8,128)(2,1)S(1)}, u32[]{:S(2)}, u32[]{:S(2)}) collective-permute-start(bf16[1024,1536]{1,0:T(8,128)(2,1)S(1)} %get-tuple-element.141), channel_id=1, source_target_pairs={{0,1},{1,0},{2,3},{3,2},{4,5},{5,4},{6,7},{7,6},{8,9},{9,8},{10,11... | collective-permute-start | bytes 9437192 | tf_op jit(solution)/shard_map/ppermute | solution.py:456
  109.9 12.3 %collective-permute-start.33 = (bf16[144,1024]{1,0:T(8,128)(2,1)S(1)}, bf16[144,1024]{1,0:T(8,128)(2,1)S(1)}, u32[]{:S(2)}, u32[]{:S(2)}) collective-permute-start(bf16[144,1024]{1,0:T(8,128)(2,1)S(1)} %get-tuple-element.131), channel_id=1, source_target_pairs={{0,4},{2,6},{4,0},{6,2},{8,12},{10,14},{12,8},{14,10},{16,20},{18,... | collective-permute-start | bytes 884744 | tf_op jit(solution)/shard_map/piece_r1/ppermute | solution.py:474
  110.9 8.4 %collective-permute-start.34 = (bf16[128,1024]{1,0:T(8,128)(2,1)S(1)}, bf16[128,1024]{1,0:T(8,128)(2,1)S(1)}, u32[]{:S(2)}, u32[]{:S(2)}) collective-permute-start(bf16[128,1024]{1,0:T(8,128)(2,1)S(1)} %get-tuple-element.133), channel_id=1, source_target_pairs={{0,2},{2,0},{4,6},{6,4},{8,10},{10,8},{12,14},{14,12},{16,18},{18,... | collective-permute-start | bytes 786440 | tf_op jit(solution)/shard_map/side_r2/ppermute | solution.py:470
  112.3 9.9 %collective-permute-start.35 = (bf16[128,1024]{1,0:T(8,128)(2,1)S(1)}, bf16[128,1024]{1,0:T(8,128)(2,1)S(1)}, u32[]{:S(2)}, u32[]{:S(2)}) collective-permute-start(bf16[128,1024]{1,0:T(8,128)(2,1)S(1)} %get-tuple-element.137), channel_id=1, source_target_pairs={{0,8},{2,10},{4,12},{6,14},{8,16},{10,18},{12,20},{14,22},{16,24},... | collective-permute-start | bytes 786440 | tf_op jit(solution)/shard_map/plane_r3/ppermute | solution.py:459
  122.8 13.0 %collective-permute-start.42 = (bf16[1536,512]{1,0:T(8,128)(2,1)S(1)}, bf16[1536,512]{1,0:T(8,128)(2,1)S(1)}, u32[]{:S(2)}, u32[]{:S(2)}) collective-permute-start(bf16[1536,512]{1,0:T(8,128)(2,1)S(1)} %get-tuple-element.147), channel_id=1, source_target_pairs={{0,1},{1,0},{2,3},{3,2},{4,5},{5,4},{6,7},{7,6},{8,9},{9,8},{10,11... | collective-permute-start | bytes 4718600 | tf_op jit(solution)/shard_map/ppermute | solution.py:456
  122.9 8.9 %collective-permute-start.37 = (bf16[128,1024]{1,0:T(8,128)(2,1)S(1)}, bf16[128,1024]{1,0:T(8,128)(2,1)S(1)}, u32[]{:S(2)}, u32[]{:S(2)}) collective-permute-start(bf16[128,1024]{1,0:T(8,128)(2,1)S(1)} %get-tuple-element.140), channel_id=1, source_target_pairs={{0,2},{2,0},{4,6},{6,4},{8,10},{10,8},{12,14},{14,12},{16,18},{18,... | collective-permute-start | bytes 786440 | tf_op jit(solution)/shard_map/side_r1/ppermute | solution.py:470
  123.5 16.5 %collective-permute-start.41 = (bf16[128,1024]{1,0:T(8,128)(2,1)S(1)}, bf16[128,1024]{1,0:T(8,128)(2,1)S(1)}, u32[]{:S(2)}, u32[]{:S(2)}) collective-permute-start(bf16[128,1024]{1,0:T(8,128)(2,1)S(1)} %get-tuple-element.146), channel_id=1, source_target_pairs={{0,16},{2,18},{4,20},{6,22},{8,24},{10,26},{12,28},{14,30},{16,0},... | collective-permute-start | bytes 786440 | tf_op jit(solution)/shard_map/plane_r2/ppermute | solution.py:459
  123.5 9.1 %collective-permute-start.36 = (bf16[144,1024]{1,0:T(8,128)(2,1)S(1)}, bf16[144,1024]{1,0:T(8,128)(2,1)S(1)}, u32[]{:S(2)}, u32[]{:S(2)}) collective-permute-start(bf16[144,1024]{1,0:T(8,128)(2,1)S(1)} %get-tuple-element.138), channel_id=1, source_target_pairs={{0,4},{2,6},{4,0},{6,2},{8,12},{10,14},{12,8},{14,10},{16,20},{18,... | collective-permute-start | bytes 884744 | tf_op jit(solution)/shard_map/piece_r0/ppermute | solution.py:474
  133.1 7.6 %collective-permute-start.39 = (bf16[128,1024]{1,0:T(8,128)(2,1)S(1)}, bf16[128,1024]{1,0:T(8,128)(2,1)S(1)}, u32[]{:S(2)}, u32[]{:S(2)}) collective-permute-start(bf16[128,1024]{1,0:T(8,128)(2,1)S(1)} %get-tuple-element.144), channel_id=1, source_target_pairs={{0,2},{2,0},{4,6},{6,4},{8,10},{10,8},{12,14},{14,12},{16,18},{18,... | collective-permute-start | bytes 786440 | tf_op jit(solution)/shard_map/side_r0/ppermute | solution.py:470
  134.7 7.8 %collective-permute-start.40 = (bf16[128,1024]{1,0:T(8,128)(2,1)S(1)}, bf16[128,1024]{1,0:T(8,128)(2,1)S(1)}, u32[]{:S(2)}, u32[]{:S(2)}) collective-permute-start(bf16[128,1024]{1,0:T(8,128)(2,1)S(1)} %get-tuple-element.145), channel_id=1, source_target_pairs={{0,24},{2,26},{4,28},{6,30},{8,0},{10,2},{12,4},{14,6},{16,8},{18,... | collective-permute-start | bytes 786440 | tf_op jit(solution)/shard_map/plane_r1/ppermute | solution.py:459

commit v2 on v1

--- a/solution.py
+++ b/solution.py
@@ -610,7 +610,7 @@
     pick("b", 3, come("l", 2), blocks["b", 1])
     to_side("b", 1)
     ahead((3, 2))
-    pick("b", 1, come("b", 2), down[1])
+    pick("b", 1, come("b", 2))
     behind((3, 2))
     send_rows(3, rows[3][1:])
     behind((0, 1))

time: 146 us -> 144 us (0.986)
    ppermute x12, waiting for transfers between devices: 10.9 us -> 16.4 us  [beside(): return lax.ppermute(a, 'expert', [(i, i ^ 1) for i in range(group_count)])]
    ppermute x9, waiting for transfers between devices: 20.4 us -> 16.4 us  [along(): lax.ppermute(a, 'expert', [(z * inner + p, (z + shift) % PLANES * inner +...]
    ppermute x12, starting transfers between devices: 15.1 us -> 12.2 us  [across(): lax.ppermute(parts[k], 'expert', [(i, i ^ SIDE * k) for i in range(group_...]
    ppermute x9, starting transfers between devices: 12.3 us -> 15.1 us  [along(): lax.ppermute(a, 'expert', [(z * inner + p, (z + shift) % PLANES * inner +...]
    ppermute x12, waiting for transfers between devices: 6.86 us -> 4.39 us  [across(): lax.ppermute(parts[k], 'expert', [(i, i ^ SIDE * k) for i in range(group_...]
  transfers between devices with their start and end apart: 43 -> 43, of which waited for: 15 -> 15; matrix products, arithmetic and copies ran while one was open for 6% -> 6% of each run, Pallas kernels for 31% -> 33%
where the time goes in v2:
time: 144 us
  Pallas kernels  51.4 us (36%)
  starting transfers between devices  43.6 us (30%)
  waiting for transfers between devices  38.5 us (27%)
  matrix products  9.49 us (7%)
    pallas_call x4, Pallas kernels, weight_grads(): pl.pallas_call(functools.partial(weight_body, len(groups), kinds, column,...  20 us
    ppermute x12, waiting for transfers between devices, beside(): return lax.ppermute(a, 'expert', [(i, i ^ 1) for i in range(group_count)])  16.4 us
    ppermute x9, waiting for transfers between devices, along(): lax.ppermute(a, 'expert', [(z * inner + p, (z + shift) % PLANES * inner +...  16.4 us
    ppermute x9, starting transfers between devices, along(): lax.ppermute(a, 'expert', [(z * inner + p, (z + shift) % PLANES * inner +...  15.1 us
    ppermute x12, starting transfers between devices, beside(): return lax.ppermute(a, 'expert', [(i, i ^ 1) for i in range(group_count)])  14.2 us
    ppermute x12, starting transfers between devices, across(): lax.ppermute(parts[k], 'expert', [(i, i ^ SIDE * k) for i in range(group_...  12.2 us
    pallas_call x2, Pallas kernels, backward(): pl.pallas_call(functools.partial(backward_body, count, len(deps)), in_spe...  11.9 us
    pallas_call x2, Pallas kernels, forward(): pl.pallas_call(functools.partial(forward_body, count, len(deps)), in_spec...  9.68 us
  transfers between devices with their start and end apart: 43, of which 15 were waited for; matrix products, arithmetic and copies ran while one was open for 6% of the time, Pallas kernels for 33%

profile of v2, /device:TPU:0, one launch (start us, length us, event | category | flops | bytes accessed | tf_op | source)
XLA Modules:
  0.0 144.1 jit_solution(14182652268131752461)
XLA Ops:
  0.6 0.5 collective-permute-start
  1.2 3.5 %convolution_convert_fusion.3.own_ref = bf16[128,512]{1,0:T(8,128)(2,1)S(1)} fusion(bf16[128,4096]{1,0:T(8,128)(2,1)} %param.10, bf16[4096,512]{1,0:T(8,128)(2,1)} %refs_5_), kind=kOutput, calls=%fused_computation.3 | convolution fusion | flops 536936448 | bytes 5373952 | tf_op jit(solution)/shard_map/dot_general | solution.py:493
  4.8 0.7 convolution_convert_fusion.2.refs_3_
  5.6 1.3 collective-permute-done.1.other_ref
  8.1 2.8 %collective-permute-start.9 = (bf16[144,1024]{1,0:T(8,128)(2,1)S(1)}, bf16[144,1024]{1,0:T(8,128)(2,1)S(1)}, u32[]{:S(2)}, u32[]{:S(2)}) collective-permute-start(bf16[144,1024]{1,0:T(8,128)(2,1)S(1)} %join_rows.2.block_ref.refs_0_.refs_2_), channel_id=1, source_target_pairs={{0,8},{2,10},{4,12},{6,14},{8,16},{10,18},{12,20},{14,22},{16,24},... | collective-permute-start | bytes 884744 | tf_op jit(solution)/shard_map/plane_l1/ppermute | solution.py:459
  10.9 3.8 %convolution_convert_fusion.1.own_ref = bf16[128,512]{1,0:T(8,128)(2,1)S(1)} fusion(bf16[128,4096]{1,0:T(8,128)(2,1)S(1)} %copy-done.8, bf16[512,4096]{1,0:T(8,128)(2,1)} %param.16), kind=kOutput, calls=%fused_computation.1 | convolution fusion | flops 536936448 | bytes 5373952 | tf_op jit(solution)/shard_map/dot_general | solution.py:493
  14.7 1.5 %convolution_convert_fusion.refs_0_ = bf16[128,512]{1,0:T(8,128)(2,1)S(1)} fusion(bf16[128,4096]{1,0:T(8,128)(2,1)S(1)} %collective-permute-done.3, bf16[512,4096]{1,0:T(8,128)(2,1)S(1)} %copy-done.7), kind=kOutput, calls=%fused_computation | convolution fusion | flops 536936448 | bytes 5373952 | tf_op jit(solution)/shard_map/dot_general | solution.py:493
  16.4 1.5 %collective-permute-start.2 = (bf16[144,1024]{1,0:T(8,128)(2,1)S(1)}, bf16[144,1024]{1,0:T(8,128)(2,1)S(1)}, u32[]{:S(2)}, u32[]{:S(2)}) collective-permute-start(bf16[144,1024]{1,0:T(8,128)(2,1)S(1)} %join_rows.2.block_ref.refs_0_.refs_2_), channel_id=1, source_target_pairs={{0,2},{2,0},{4,6},{6,4},{8,10},{10,8},{12,14},{14,12},{16,18},{18,... | collective-permute-start | bytes 884744 | tf_op jit(solution)/shard_map/side_l0/ppermute | solution.py:470
  17.9 3.6 %collective-permute-start.7 = (bf16[144,1024]{1,0:T(8,128)(2,1)S(1)}, bf16[144,1024]{1,0:T(8,128)(2,1)S(1)}, u32[]{:S(2)}, u32[]{:S(2)}) collective-permute-start(bf16[144,1024]{1,0:T(8,128)(2,1)S(1)} %tie_rows.5.refs_0_), channel_id=1, source_target_pairs={{0,24},{2,26},{4,28},{6,30},{8,0},{10,2},{12,4},{14,6},{16,8},{18,... | collective-permute-start | bytes 884744 | tf_op jit(solution)/shard_map/plane_l3/ppermute | solution.py:459
  21.5 1.5 %collective-permute-start.10 = (bf16[144,1024]{1,0:T(8,128)(2,1)S(1)}, bf16[144,1024]{1,0:T(8,128)(2,1)S(1)}, u32[]{:S(2)}, u32[]{:S(2)}) collective-permute-start(bf16[144,1024]{1,0:T(8,128)(2,1)S(1)} %collective-permute-done.9.refs_5_.refs_1_.refs_0_.refs_2_), channel_id=1, source_target_pairs={{0,2},{2,0},{4,6},{6,4},{8,10},{10,8},{12,14},{14,12},{16,18},{18,... | collective-permute-start | bytes 884744 | tf_op jit(solution)/shard_map/side_l1/ppermute | solution.py:470
  23.0 3.2 %collective-permute-done.2.refs_1_.refs_3_ = bf16[144,1024]{1,0:T(8,128)(2,1)S(1)} collective-permute-done((bf16[144,1024]{1,0:T(8,128)(2,1)S(1)}, bf16[144,1024]{1,0:T(8,128)(2,1)S(1)}, u32[]{:S(2)}, u32[]{:S(2)}) %collective-permute-start.2) | collective-permute-done | bytes 294944 | tf_op jit(solution)/shard_map/side_l0/ppermute | solution.py:470
  26.2 0.5 select_latent.4
  26.7 1.6 %collective-permute-start.13 = (bf16[144,1024]{1,0:T(8,128)(2,1)S(1)}, bf16[144,1024]{1,0:T(8,128)(2,1)S(1)}, u32[]{:S(2)}, u32[]{:S(2)}) collective-permute-start(bf16[144,1024]{1,0:T(8,128)(2,1)S(1)} %get-tuple-element.86), channel_id=1, source_target_pairs={{0,4},{2,6},{4,0},{6,2},{8,12},{10,14},{12,8},{14,10},{16,20},{18,... | collective-permute-start | bytes 884744 | tf_op jit(solution)/shard_map/piece_l0/ppermute | solution.py:474
  28.3 2.7 %collective-permute-start.15 = (bf16[144,1024]{1,0:T(8,128)(2,1)S(1)}, bf16[144,1024]{1,0:T(8,128)(2,1)S(1)}, u32[]{:S(2)}, u32[]{:S(2)}) collective-permute-start(bf16[144,1024]{1,0:T(8,128)(2,1)S(1)} %tie_rows.6.refs_4_), channel_id=1, source_target_pairs={{0,16},{2,18},{4,20},{6,22},{8,24},{10,26},{12,28},{14,30},{16,0},... | collective-permute-start | bytes 884744 | tf_op jit(solution)/shard_map/plane_l2/ppermute | solution.py:459
  30.9 1.5 %collective-permute-start.8 = (bf16[144,1024]{1,0:T(8,128)(2,1)S(1)}, bf16[144,1024]{1,0:T(8,128)(2,1)S(1)}, u32[]{:S(2)}, u32[]{:S(2)}) collective-permute-start(bf16[144,1024]{1,0:T(8,128)(2,1)S(1)} %collective-permute-done.7.refs_5_.refs_1_.refs_0_.refs_2_), channel_id=1, source_target_pairs={{0,2},{2,0},{4,6},{6,4},{8,10},{10,8},{12,14},{14,12},{16,18},{18,... | collective-permute-start | bytes 884744 | tf_op jit(solution)/shard_map/side_l3/ppermute | solution.py:470
  32.4 0.5 select_latent.5
  32.9 1.7 %collective-permute-start.14 = (bf16[144,1024]{1,0:T(8,128)(2,1)S(1)}, bf16[144,1024]{1,0:T(8,128)(2,1)S(1)}, u32[]{:S(2)}, u32[]{:S(2)}) collective-permute-start(bf16[144,1024]{1,0:T(8,128)(2,1)S(1)} %get-tuple-element.88), channel_id=1, source_target_pairs={{0,4},{2,6},{4,0},{6,2},{8,12},{10,14},{12,8},{14,10},{16,20},{18,... | collective-permute-start | bytes 884744 | tf_op jit(solution)/shard_map/piece_l1/ppermute | solution.py:474
  34.6 1.5 %collective-permute-start.6 = (bf16[128,1024]{1,0:T(8,128)(2,1)S(1)}, bf16[128,1024]{1,0:T(8,128)(2,1)S(1)}, u32[]{:S(2)}, u32[]{:S(2)}) collective-permute-start(bf16[128,1024]{1,0:T(8,128)(2,1)S(1)} %join_rows.3.refs_4_.block_ref.refs_2_), channel_id=1, source_target_pairs={{0,2},{2,0},{4,6},{6,4},{8,10},{10,8},{12,14},{14,12},{16,18},{18,... | collective-permute-start | bytes 786440 | tf_op jit(solution)/shard_map/side_b0/ppermute | solution.py:470
  36.1 2.6 %collective-permute-start.19 = (bf16[128,1024]{1,0:T(8,128)(2,1)S(1)}, bf16[128,1024]{1,0:T(8,128)(2,1)S(1)}, u32[]{:S(2)}, u32[]{:S(2)}) collective-permute-start(bf16[128,1024]{1,0:T(8,128)(2,1)S(1)} %tie_rows.7.refs_4_), channel_id=1, source_target_pairs={{0,16},{2,18},{4,20},{6,22},{8,24},{10,26},{12,28},{14,30},{16,0},... | collective-permute-start | bytes 786440 | tf_op jit(solution)/shard_map/plane_b2/ppermute | solution.py:459
  38.7 11.4 %collective-permute-done.15.refs_6_.refs_1_.refs_0_.refs_2_ = bf16[144,1024]{1,0:T(8,128)(2,1)S(1)} collective-permute-done((bf16[144,1024]{1,0:T(8,128)(2,1)S(1)}, bf16[144,1024]{1,0:T(8,128)(2,1)S(1)}, u32[]{:S(2)}, u32[]{:S(2)}) %collective-permute-start.15) | collective-permute-done | bytes 294944 | tf_op jit(solution)/shard_map/plane_l2/ppermute | solution.py:459
  50.2 1.5 %collective-permute-start.17 = (bf16[144,1024]{1,0:T(8,128)(2,1)S(1)}, bf16[144,1024]{1,0:T(8,128)(2,1)S(1)}, u32[]{:S(2)}, u32[]{:S(2)}) collective-permute-start(bf16[144,1024]{1,0:T(8,128)(2,1)S(1)} %collective-permute-done.15.refs_6_.refs_1_.refs_0_.refs_2_), channel_id=1, source_target_pairs={{0,2},{2,0},{4,6},{6,4},{8,10},{10,8},{12,14},{14,12},{16,18},{18,... | collective-permute-start | bytes 884744 | tf_op jit(solution)/shard_map/side_l2/ppermute | solution.py:470
  52.1 0.6 collective-permute-start.18
  52.7 0.5 select_back.4
  53.2 2.5 %collective-permute-start.23 = (bf16[128,1024]{1,0:T(8,128)(2,1)S(1)}, bf16[128,1024]{1,0:T(8,128)(2,1)S(1)}, u32[]{:S(2)}, u32[]{:S(2)}) collective-permute-start(bf16[128,1024]{1,0:T(8,128)(2,1)S(1)} %tie_rows.8.refs_8_), channel_id=1, source_target_pairs={{0,24},{2,26},{4,28},{6,30},{8,0},{10,2},{12,4},{14,6},{16,8},{18,... | collective-permute-start | bytes 786440 | tf_op jit(solution)/shard_map/plane_b3/ppermute | solution.py:459
  55.7 1.5 %collective-permute-start.16 = (bf16[144,1024]{1,0:T(8,128)(2,1)S(1)}, bf16[144,1024]{1,0:T(8,128)(2,1)S(1)}, u32[]{:S(2)}, u32[]{:S(2)}) collective-permute-start(bf16[144,1024]{1,0:T(8,128)(2,1)S(1)} %get-tuple-element.90), channel_id=1, source_target_pairs={{0,4},{2,6},{4,0},{6,2},{8,12},{10,14},{12,8},{14,10},{16,20},{18,... | collective-permute-start | bytes 884744 | tf_op jit(solution)/shard_map/piece_b0/ppermute | solution.py:474
  57.3 4.8 %forward_rows.2 = (bf16[576,1024]{1,0:T(8,128)(2,1)S(1)}, bf16[576,1536]{1,0:T(8,128)(2,1)S(1)}, bf16[576,1536]{1,0:T(8,128)(2,1)S(1)}, bf16[576,1536]{1,0:T(8,128)(2,1)S(1)}, f32[8,128]{1,0:T(8,128)S(1)}) custom-call(bf16[144,1024]{1,0:T(8,128)(2,1)S(1)} %get-tuple-element.84.refs_0_, bf16[144,1024]{1,0:T(8,128)(2,1)S(1)} %collective-permute-done.13.refs_5_.refs_1_, ...), custom_call_target="tpu_custom_call" | custom-call | flops 3623878656 | bytes 11599873 | tf_op jit(solution)/shard_map/forward_rows/pallas_call | solution.py:287
  62.1 0.5 select_latent.7
  62.6 0.6 collective-permute-start.22
  63.1 0.5 collective-permute-start.25
  63.8 1.6 %collective-permute-start.24 = (bf16[128,1024]{1,0:T(8,128)(2,1)S(1)}, bf16[128,1024]{1,0:T(8,128)(2,1)S(1)}, u32[]{:S(2)}, u32[]{:S(2)}) collective-permute-start(bf16[128,1024]{1,0:T(8,128)(2,1)S(1)} %collective-permute-done.23.refs_6_.refs_2_), channel_id=1, source_target_pairs={{0,2},{2,0},{4,6},{6,4},{8,10},{10,8},{12,14},{14,12},{16,18},{18,... | collective-permute-start | bytes 786440 | tf_op jit(solution)/shard_map/side_b3/ppermute | solution.py:470
  65.3 5.9 %collective-permute-done.25.refs_3_ = bf16[128,1024]{1,0:T(8,128)(2,1)S(1)} collective-permute-done((bf16[128,1024]{1,0:T(8,128)(2,1)S(1)}, bf16[128,1024]{1,0:T(8,128)(2,1)S(1)}, u32[]{:S(2)}, u32[]{:S(2)}) %collective-permute-start.25) | collective-permute-done | bytes 262176 | tf_op jit(solution)/shard_map/side_b2/ppermute | solution.py:470
  71.2 0.5 select_back.5
  72.1 1.3 collective-permute-start.21
  73.4 0.6 collective-permute-done.24.refs_3_
  74.2 0.5 select_back.6
  74.7 0.8 collective-permute-start.28
  75.5 4.9 %forward_rows.3 = (bf16[576,1024]{1,0:T(8,128)(2,1)S(1)}, bf16[576,1536]{1,0:T(8,128)(2,1)S(1)}, bf16[576,1536]{1,0:T(8,128)(2,1)S(1)}, bf16[576,1536]{1,0:T(8,128)(2,1)S(1)}, f32[8,128]{1,0:T(8,128)S(1)}) custom-call(bf16[144,1024]{1,0:T(8,128)(2,1)S(1)} %get-tuple-element.87.refs_4_.refs_0_, bf16[144,1024]{1,0:T(8,128)(2,1)S(1)} %collective-permute-done.18.refs_5_.refs_1_, ...), custom_call_target="tpu_custom_call" | custom-call | flops 3623878656 | bytes 11599873 | tf_op jit(solution)/shard_map/forward_rows/pallas_call | solution.py:287
  80.4 0.6 collective-permute-done.26.refs_5_.refs_3_
  81.0 0.5 select_back.7
  81.5 1.6 %collective-permute-start.27 = (bf16[144,1024]{1,0:T(8,128)(2,1)S(1)}, bf16[144,1024]{1,0:T(8,128)(2,1)S(1)}, u32[]{:S(2)}, u32[]{:S(2)}) collective-permute-start(bf16[144,1024]{1,0:T(8,128)(2,1)S(1)} %get-tuple-element.100), channel_id=1, source_target_pairs={{0,4},{2,6},{4,0},{6,2},{8,12},{10,14},{12,8},{14,10},{16,20},{18,... | collective-permute-start | bytes 884744 | tf_op jit(solution)/shard_map/piece_b1/ppermute | solution.py:474
  83.0 2.8 %collective-permute-done.28.refs_1_ = bf16[144,1024]{1,0:T(8,128)(2,1)S(1)} collective-permute-done((bf16[144,1024]{1,0:T(8,128)(2,1)S(1)}, bf16[144,1024]{1,0:T(8,128)(2,1)S(1)}, u32[]{:S(2)}, u32[]{:S(2)}) %collective-permute-start.28) | collective-permute-done | bytes 294944 | tf_op jit(solution)/shard_map/piece_b3/ppermute | solution.py:474
  85.8 5.9 %backward_rows.2 = (bf16[576,1024]{1,0:T(8,128)(2,1)S(1)}, bf16[576,1536]{1,0:T(8,128)(2,1)S(1)}, bf16[576,1536]{1,0:T(8,128)(2,1)S(1)}, bf16[144,1024]{1,0:T(8,...) custom-call(bf16[144,1024]{1,0:T(8,128)(2,1)S(1)} %get-tuple-element, ...), custom_call_target="tpu_custom_call" | custom-call | flops 5435817984 | bytes 16515073 | tf_op jit(solution)/shard_map/backward_rows/pallas_call | solution.py:334
  91.9 5.9 %backward_rows.3 = (bf16[576,1024]{1,0:T(8,128)(2,1)S(1)}, bf16[576,1536]{1,0:T(8,128)(2,1)S(1)}, bf16[576,1536]{1,0:T(8,128)(2,1)S(1)}, bf16[144,1024]{1,0:T(8,...) custom-call(bf16[144,1024]{1,0:T(8,128)(2,1)S(1)} %get-tuple-element, ...), custom_call_target="tpu_custom_call" | custom-call | flops 5435817984 | bytes 16515073 | tf_op jit(solution)/shard_map/backward_rows/pallas_call | solution.py:334
  97.8 0.8 collective-permute-done.29.refs_3_
  98.6 0.5 return_rows.4
  99.1 1.3 collective-permute-start.30
  100.8 5.5 %weight_grads.4 = (bf16[1024,1536]{1,0:T(8,128)(2,1)S(1)}, f32[8,128]{1,0:T(8,128)S(1)}) custom-call(bf16[576,1024]{1,0:T(8,128)(2,1)S(1)} %get-tuple-element.118.refs_0_, bf16[576,1024]{1,0:T(8,128)(2,1)S(1)} %get-tuple-element.119.refs_1_, bf16[576,1536]{1,0:T(8,128)(2,1)S(1)} %get-tuple-element.120.refs_2_, ...), custom_call_target="tpu_custom_call" | custom-call | flops 3623878656 | bytes 7077889 | tf_op jit(solution)/shard_map/weight_grads/pallas_call | solution.py:388
  106.8 0.6 return_rows.5
  107.4 0.8 collective-permute-start.32
  108.3 1.2 collective-permute-start.33
  109.5 3.0 %weight_grads.5 = (bf16[1536,512]{1,0:T(8,128)(2,1)S(1)}, f32[8,128]{1,0:T(8,128)S(1)}) custom-call(bf16[576,1024]{1,0:T(8,128)(2,1)S(1)} %get-tuple-element.118.refs_0_, bf16[576,1024]{1,0:T(8,128)(2,1)S(1)} %get-tuple-element.119.refs_1_, bf16[576,1536]{1,0:T(8,128)(2,1)S(1)} %get-tuple-element.120.refs_2_, ...), custom_call_target="tpu_custom_call" | custom-call | flops 1811939328 | bytes 7077889 | tf_op jit(solution)/shard_map/weight_grads/pallas_call | solution.py:388
  112.6 4.1 %collective-permute-done.33.refs_5_ = bf16[128,1024]{1,0:T(8,128)(2,1)S(1)} collective-permute-done((bf16[128,1024]{1,0:T(8,128)(2,1)S(1)}, bf16[128,1024]{1,0:T(8,128)(2,1)S(1)}, u32[]{:S(2)}, u32[]{:S(2)}) %collective-permute-start.33) | collective-permute-done | bytes 262176 | tf_op jit(solution)/shard_map/side_r2/ppermute | solution.py:470
  116.6 2.7 %collective-permute-done.34.refs_9_.refs_4_ = bf16[128,1024]{1,0:T(8,128)(2,1)S(1)} collective-permute-done((bf16[128,1024]{1,0:T(8,128)(2,1)S(1)}, bf16[128,1024]{1,0:T(8,128)(2,1)S(1)}, u32[]{:S(2)}, u32[]{:S(2)}) %collective-permute-start.34) | collective-permute-done | bytes 262176 | tf_op jit(solution)/shard_map/plane_r3/ppermute | solution.py:459
  119.4 0.6 return_rows.6
  120.0 1.3 collective-permute-start.35
  121.4 0.8 collective-permute-start.36
  122.2 7.2 %weight_grads.6 = (bf16[512,1536]{1,0:T(8,128)(2,1)}, bf16[512,1536]{1,0:T(8,128)(2,1)}, f32[8,128]{1,0:T(8,128)S(1)}) custom-call(bf16[576,1024]{1,0:T(8,128)(2,1)S(1)} %get-tuple-element.118.refs_0_, bf16[576,1024]{1,0:T(8,128)(2,1)S(1)} %get-tuple-element.119.refs_1_, bf16[576,1536]{1,0:T(8,128)(2,1)S(1)} %get-tuple-element.120.refs_2_, ...), custom_call_target="tpu_custom_call" | custom-call | flops 3623878656 | bytes 7077889 | tf_op jit(solution)/shard_map/weight_grads/pallas_call | solution.py:388
  129.7 0.6 return_rows.7
  130.3 0.9 collective-permute-start.38
  131.2 0.8 collective-permute-start.39
  132.1 4.2 %weight_grads.7 = (bf16[1536,512]{1,0:T(8,128)(2,1)}, f32[8,128]{1,0:T(8,128)S(1)}) custom-call(bf16[576,1024]{1,0:T(8,128)(2,1)S(1)} %get-tuple-element.118.refs_0_, bf16[576,1024]{1,0:T(8,128)(2,1)S(1)} %get-tuple-element.119.refs_1_, bf16[576,1536]{1,0:T(8,128)(2,1)S(1)} %get-tuple-element.120.refs_2_, bf16[576,1536]{1,0:T(8,128)(2,1)S(1)} %get-tuple-element.121.refs_3_, ...), custom_call_target="tpu_custom_call" | custom-call | flops 1811939328 | bytes 7077889 | tf_op jit(solution)/shard_map/weight_grads/pallas_call | solution.py:388
  136.3 1.8 %collective-permute-done.38.refs_1_ = bf16[128,1024]{1,0:T(8,128)(2,1)S(1)} collective-permute-done((bf16[128,1024]{1,0:T(8,128)(2,1)S(1)}, bf16[128,1024]{1,0:T(8,128)(2,1)S(1)}, u32[]{:S(2)}, u32[]{:S(2)}) %collective-permute-start.38) | collective-permute-done | bytes 262176 | tf_op jit(solution)/shard_map/side_r0/ppermute | solution.py:470
  138.1 2.2 %collective-permute-done.39.refs_2_ = bf16[128,1024]{1,0:T(8,128)(2,1)S(1)} collective-permute-done((bf16[128,1024]{1,0:T(8,128)(2,1)S(1)}, bf16[128,1024]{1,0:T(8,128)(2,1)S(1)}, u32[]{:S(2)}, u32[]{:S(2)}) %collective-permute-start.39) | collective-permute-done | bytes 262176 | tf_op jit(solution)/shard_map/plane_r1/ppermute | solution.py:459
  140.3 3.8 %token_grad.1 = bf16[128,4096]{1,0:T(8,128)(2,1)} custom-call(f32[128,1024]{1,0:T(8,128)S(1)} %get-tuple-element.142.refs_11_.refs_0_, bf16[128,1024]{1,0:T(8,128)(2,1)S(1)} %collective-permute-done.38.refs_1_, bf16[128,1024]{1,0:T(8,128)(2,1)S(1)} %collective-permute-done.39.refs_2_, bf16[128,1024]{1,0:T(8,128)(2,1)S(1)} %collective-permute-done.40.refs_3_, ...), custom_call_target="tpu_custom_call" | custom-call | flops 1073741824 | bytes 8388609 | tf_op jit(solution)/shard_map/token_grad/pallas_call | solution.py:421
  (72 shorter events, 4.2 us)
Async XLA Ops:
  0.6 4.1 %copy-start = (bf16[4096,512]{1,0:T(8,128)(2,1)S(1)}, bf16[4096,512]{1,0:T(8,128)(2,1)}, u32[]{:S(2)}) copy-start(bf16[4096,512]{1,0:T(8,128)(2,1)} %refs_5_) | copy-start | bytes 12582916
  0.6 4.1 %collective-permute-start = (bf16[128,4096]{1,0:T(8,128)(2,1)}, bf16[128,4096]{1,0:T(8,128)(2,1)S(1)}, u32[]{:S(2)}, u32[]{:S(2)}) collective-permute-start(bf16[128,4096]{1,0:T(8,128)(2,1)} %param.10), channel_id=1, source_target_pairs={{0,1},{1,0},{2,3},{3,2},{4,5},{5,4},{6,7},{7,6},{8,9},{9,8},{10,11... | collective-permute-start | bytes 3145736 | tf_op jit(solution)/shard_map/ppermute | solution.py:456
  4.6 2.2 %copy-start.1 = (s32[128,8]{0,1:T(8,128)S(1)}, s32[128,8]{0,1:T(8,128)}, u32[]{:S(2)}) copy-start(s32[128,8]{0,1:T(8,128)} %param.12) | copy-start | bytes 12292
  4.7 2.2 %copy-start.2 = (s32[128,8]{0,1:T(8,128)S(1)}, s32[128,8]{0,1:T(8,128)}, u32[]{:S(2)}) copy-start(s32[128,8]{0,1:T(8,128)} %param.13) | copy-start | bytes 12292
  4.7 2.2 %copy-start.3 = (f32[128,8]{0,1:T(8,128)S(1)}, f32[128,8]{0,1:T(8,128)}, u32[]{:S(2)}) copy-start(f32[128,8]{0,1:T(8,128)} %param.14) | copy-start | bytes 12292
  4.7 2.3 %copy-start.4 = (bf16[1,512,1536]{2,1,0:T(8,128)(2,1)S(1)}, bf16[1,512,1536]{2,1,0:T(8,128)(2,1)}, u32[]{:S(2)}) copy-start(bf16[1,512,1536]{2,1,0:T(8,128)(2,1)} %param.17) | copy-start | bytes 4718596
  4.7 2.5 %copy-start.8 = (bf16[128,4096]{1,0:T(8,128)(2,1)S(1)}, bf16[128,4096]{1,0:T(8,128)(2,1)}, u32[]{:S(2)}) copy-start(bf16[128,4096]{1,0:T(8,128)(2,1)} %param.11) | copy-start | bytes 3145732
  4.7 2.8 %copy-start.5 = (bf16[1,512,1536]{2,1,0:T(8,128)(2,1)S(1)}, bf16[1,512,1536]{2,1,0:T(8,128)(2,1)}, u32[]{:S(2)}) copy-start(bf16[1,512,1536]{2,1,0:T(8,128)(2,1)} %param.18) | copy-start | bytes 4718596
  4.7 3.0 %copy-start.6 = (bf16[1,1536,512]{2,1,0:T(8,128)(2,1)S(1)}, bf16[1,1536,512]{2,1,0:T(8,128)(2,1)}, u32[]{:S(2)}) copy-start(bf16[1,1536,512]{2,1,0:T(8,128)(2,1)} %param.19) | copy-start | bytes 4718596
  5.5 1.4 collective-permute-start.1
  6.9 7.7 %copy-start.7 = (bf16[512,4096]{1,0:T(8,128)(2,1)S(1)}, bf16[512,4096]{1,0:T(8,128)(2,1)}, u32[]{:S(2)}) copy-start(bf16[512,4096]{1,0:T(8,128)(2,1)} %param.16) | copy-start | bytes 12582916
  7.0 9.4 %collective-permute-start.5 = (bf16[512,1536]{1,0:T(8,128)(2,1)S(1)}, bf16[512,1536]{1,0:T(8,128)(2,1)S(1)}, u32[]{:S(2)}, u32[]{:S(2)}) collective-permute-start(bf16[512,1536]{1,0:T(8,128)(2,1)S(1)} %bitcast.20), channel_id=1, source_target_pairs={{0,1},{1,0},{2,3},{3,2},{4,5},{5,4},{6,7},{7,6},{8,9},{9,8},{10,11... | collective-permute-start | bytes 4718600 | tf_op jit(solution)/shard_map/ppermute | solution.py:456
  7.2 7.5 %collective-permute-start.3 = (bf16[128,4096]{1,0:T(8,128)(2,1)S(1)}, bf16[128,4096]{1,0:T(8,128)(2,1)S(1)}, u32[]{:S(2)}, u32[]{:S(2)}) collective-permute-start(bf16[128,4096]{1,0:T(8,128)(2,1)S(1)} %copy-done.8), channel_id=1, source_target_pairs={{0,1},{1,0},{2,3},{3,2},{4,5},{5,4},{6,7},{7,6},{8,9},{9,8},{10,11... | collective-permute-start | bytes 3145736 | tf_op jit(solution)/shard_map/ppermute | solution.py:456
  7.5 18.7 %collective-permute-start.11 = (bf16[512,1536]{1,0:T(8,128)(2,1)S(1)}, bf16[512,1536]{1,0:T(8,128)(2,1)S(1)}, u32[]{:S(2)}, u32[]{:S(2)}) collective-permute-start(bf16[512,1536]{1,0:T(8,128)(2,1)S(1)} %bitcast.25), channel_id=1, source_target_pairs={{0,1},{1,0},{2,3},{3,2},{4,5},{5,4},{6,7},{7,6},{8,9},{9,8},{10,11... | collective-permute-start | bytes 4718600 | tf_op jit(solution)/shard_map/ppermute | solution.py:456
  7.7 18.5 %collective-permute-start.12 = (bf16[1536,512]{1,0:T(8,128)(2,1)S(1)}, bf16[1536,512]{1,0:T(8,128)(2,1)S(1)}, u32[]{:S(2)}, u32[]{:S(2)}) collective-permute-start(bf16[1536,512]{1,0:T(8,128)(2,1)S(1)} %bitcast.30), channel_id=1, source_target_pairs={{0,1},{1,0},{2,3},{3,2},{4,5},{5,4},{6,7},{7,6},{8,9},{9,8},{10,11... | collective-permute-start | bytes 4718600 | tf_op jit(solution)/shard_map/ppermute | solution.py:456
  8.1 13.4 %collective-permute-start.9 = (bf16[144,1024]{1,0:T(8,128)(2,1)S(1)}, bf16[144,1024]{1,0:T(8,128)(2,1)S(1)}, u32[]{:S(2)}, u32[]{:S(2)}) collective-permute-start(bf16[144,1024]{1,0:T(8,128)(2,1)S(1)} %join_rows.2.block_ref.refs_0_.refs_2_), channel_id=1, source_target_pairs={{0,8},{2,10},{4,12},{6,14},{8,16},{10,18},{12,20},{14,22},{16,24},... | collective-permute-start | bytes 884744 | tf_op jit(solution)/shard_map/plane_l1/ppermute | solution.py:459
  16.2 1.7 %collective-permute-start.4 = (bf16[128,512]{1,0:T(8,128)(2,1)S(1)}, bf16[128,512]{1,0:T(8,128)(2,1)S(1)}, u32[]{:S(2)}, u32[]{:S(2)}) collective-permute-start(bf16[128,512]{1,0:T(8,128)(2,1)S(1)} %convolution_convert_fusion.refs_0_), channel_id=1, source_target_pairs={{0,1},{1,0},{2,3},{3,2},{4,5},{5,4},{6,7},{7,6},{8,9},{9,8},{10,11... | collective-permute-start | bytes 393224 | tf_op jit(solution)/shard_map/ppermute | solution.py:456
  16.4 9.8 %collective-permute-start.2 = (bf16[144,1024]{1,0:T(8,128)(2,1)S(1)}, bf16[144,1024]{1,0:T(8,128)(2,1)S(1)}, u32[]{:S(2)}, u32[]{:S(2)}) collective-permute-start(bf16[144,1024]{1,0:T(8,128)(2,1)S(1)} %join_rows.2.block_ref.refs_0_.refs_2_), channel_id=1, source_target_pairs={{0,2},{2,0},{4,6},{6,4},{8,10},{10,8},{12,14},{14,12},{16,18},{18,... | collective-permute-start | bytes 884744 | tf_op jit(solution)/shard_map/side_l0/ppermute | solution.py:470
  17.9 13.0 %collective-permute-start.7 = (bf16[144,1024]{1,0:T(8,128)(2,1)S(1)}, bf16[144,1024]{1,0:T(8,128)(2,1)S(1)}, u32[]{:S(2)}, u32[]{:S(2)}) collective-permute-start(bf16[144,1024]{1,0:T(8,128)(2,1)S(1)} %tie_rows.5.refs_0_), channel_id=1, source_target_pairs={{0,24},{2,26},{4,28},{6,30},{8,0},{10,2},{12,4},{14,6},{16,8},{18,... | collective-permute-start | bytes 884744 | tf_op jit(solution)/shard_map/plane_l3/ppermute | solution.py:459
  21.5 10.9 %collective-permute-start.10 = (bf16[144,1024]{1,0:T(8,128)(2,1)S(1)}, bf16[144,1024]{1,0:T(8,128)(2,1)S(1)}, u32[]{:S(2)}, u32[]{:S(2)}) collective-permute-start(bf16[144,1024]{1,0:T(8,128)(2,1)S(1)} %collective-permute-done.9.refs_5_.refs_1_.refs_0_.refs_2_), channel_id=1, source_target_pairs={{0,2},{2,0},{4,6},{6,4},{8,10},{10,8},{12,14},{14,12},{16,18},{18,... | collective-permute-start | bytes 884744 | tf_op jit(solution)/shard_map/side_l1/ppermute | solution.py:470
  26.7 9.4 %collective-permute-start.13 = (bf16[144,1024]{1,0:T(8,128)(2,1)S(1)}, bf16[144,1024]{1,0:T(8,128)(2,1)S(1)}, u32[]{:S(2)}, u32[]{:S(2)}) collective-permute-start(bf16[144,1024]{1,0:T(8,128)(2,1)S(1)} %get-tuple-element.86), channel_id=1, source_target_pairs={{0,4},{2,6},{4,0},{6,2},{8,12},{10,14},{12,8},{14,10},{16,20},{18,... | collective-permute-start | bytes 884744 | tf_op jit(solution)/shard_map/piece_l0/ppermute | solution.py:474
  28.3 21.9 %collective-permute-start.15 = (bf16[144,1024]{1,0:T(8,128)(2,1)S(1)}, bf16[144,1024]{1,0:T(8,128)(2,1)S(1)}, u32[]{:S(2)}, u32[]{:S(2)}) collective-permute-start(bf16[144,1024]{1,0:T(8,128)(2,1)S(1)} %tie_rows.6.refs_4_), channel_id=1, source_target_pairs={{0,16},{2,18},{4,20},{6,22},{8,24},{10,26},{12,28},{14,30},{16,0},... | collective-permute-start | bytes 884744 | tf_op jit(solution)/shard_map/plane_l2/ppermute | solution.py:459
  30.9 20.7 %collective-permute-start.8 = (bf16[144,1024]{1,0:T(8,128)(2,1)S(1)}, bf16[144,1024]{1,0:T(8,128)(2,1)S(1)}, u32[]{:S(2)}, u32[]{:S(2)}) collective-permute-start(bf16[144,1024]{1,0:T(8,128)(2,1)S(1)} %collective-permute-done.7.refs_5_.refs_1_.refs_0_.refs_2_), channel_id=1, source_target_pairs={{0,2},{2,0},{4,6},{6,4},{8,10},{10,8},{12,14},{14,12},{16,18},{18,... | collective-permute-start | bytes 884744 | tf_op jit(solution)/shard_map/side_l3/ppermute | solution.py:470
  32.9 19.8 %collective-permute-start.14 = (bf16[144,1024]{1,0:T(8,128)(2,1)S(1)}, bf16[144,1024]{1,0:T(8,128)(2,1)S(1)}, u32[]{:S(2)}, u32[]{:S(2)}) collective-permute-start(bf16[144,1024]{1,0:T(8,128)(2,1)S(1)} %get-tuple-element.88), channel_id=1, source_target_pairs={{0,4},{2,6},{4,0},{6,2},{8,12},{10,14},{12,8},{14,10},{16,20},{18,... | collective-permute-start | bytes 884744 | tf_op jit(solution)/shard_map/piece_l1/ppermute | solution.py:474
  34.6 18.2 %collective-permute-start.6 = (bf16[128,1024]{1,0:T(8,128)(2,1)S(1)}, bf16[128,1024]{1,0:T(8,128)(2,1)S(1)}, u32[]{:S(2)}, u32[]{:S(2)}) collective-permute-start(bf16[128,1024]{1,0:T(8,128)(2,1)S(1)} %join_rows.3.refs_4_.block_ref.refs_2_), channel_id=1, source_target_pairs={{0,2},{2,0},{4,6},{6,4},{8,10},{10,8},{12,14},{14,12},{16,18},{18,... | collective-permute-start | bytes 786440 | tf_op jit(solution)/shard_map/side_b0/ppermute | solution.py:470
  36.1 25.9 %collective-permute-start.19 = (bf16[128,1024]{1,0:T(8,128)(2,1)S(1)}, bf16[128,1024]{1,0:T(8,128)(2,1)S(1)}, u32[]{:S(2)}, u32[]{:S(2)}) collective-permute-start(bf16[128,1024]{1,0:T(8,128)(2,1)S(1)} %tie_rows.7.refs_4_), channel_id=1, source_target_pairs={{0,16},{2,18},{4,20},{6,22},{8,24},{10,26},{12,28},{14,30},{16,0},... | collective-permute-start | bytes 786440 | tf_op jit(solution)/shard_map/plane_b2/ppermute | solution.py:459
  50.2 11.9 %collective-permute-start.17 = (bf16[144,1024]{1,0:T(8,128)(2,1)S(1)}, bf16[144,1024]{1,0:T(8,128)(2,1)S(1)}, u32[]{:S(2)}, u32[]{:S(2)}) collective-permute-start(bf16[144,1024]{1,0:T(8,128)(2,1)S(1)} %collective-permute-done.15.refs_6_.refs_1_.refs_0_.refs_2_), channel_id=1, source_target_pairs={{0,2},{2,0},{4,6},{6,4},{8,10},{10,8},{12,14},{14,12},{16,18},{18,... | collective-permute-start | bytes 884744 | tf_op jit(solution)/shard_map/side_l2/ppermute | solution.py:470
  52.1 9.9 %collective-permute-start.18 = (bf16[144,1024]{1,0:T(8,128)(2,1)S(1)}, bf16[144,1024]{1,0:T(8,128)(2,1)S(1)}, u32[]{:S(2)}, u32[]{:S(2)}) collective-permute-start(bf16[144,1024]{1,0:T(8,128)(2,1)S(1)} %get-tuple-element.92), channel_id=1, source_target_pairs={{0,4},{2,6},{4,0},{6,2},{8,12},{10,14},{12,8},{14,10},{16,20},{18,... | collective-permute-start | bytes 884744 | tf_op jit(solution)/shard_map/piece_l3/ppermute | solution.py:474
  53.2 10.5 %collective-permute-start.23 = (bf16[128,1024]{1,0:T(8,128)(2,1)S(1)}, bf16[128,1024]{1,0:T(8,128)(2,1)S(1)}, u32[]{:S(2)}, u32[]{:S(2)}) collective-permute-start(bf16[128,1024]{1,0:T(8,128)(2,1)S(1)} %tie_rows.8.refs_8_), channel_id=1, source_target_pairs={{0,24},{2,26},{4,28},{6,30},{8,0},{10,2},{12,4},{14,6},{16,8},{18,... | collective-permute-start | bytes 786440 | tf_op jit(solution)/shard_map/plane_b3/ppermute | solution.py:459
  55.7 15.5 %collective-permute-start.16 = (bf16[144,1024]{1,0:T(8,128)(2,1)S(1)}, bf16[144,1024]{1,0:T(8,128)(2,1)S(1)}, u32[]{:S(2)}, u32[]{:S(2)}) collective-permute-start(bf16[144,1024]{1,0:T(8,128)(2,1)S(1)} %get-tuple-element.90), channel_id=1, source_target_pairs={{0,4},{2,6},{4,0},{6,2},{8,12},{10,14},{12,8},{14,10},{16,20},{18,... | collective-permute-start | bytes 884744 | tf_op jit(solution)/shard_map/piece_b0/ppermute | solution.py:474
  62.6 11.7 %collective-permute-start.22 = (bf16[144,1024]{1,0:T(8,128)(2,1)S(1)}, bf16[144,1024]{1,0:T(8,128)(2,1)S(1)}, u32[]{:S(2)}, u32[]{:S(2)}) collective-permute-start(bf16[144,1024]{1,0:T(8,128)(2,1)S(1)} %get-tuple-element.94), channel_id=1, source_target_pairs={{0,4},{2,6},{4,0},{6,2},{8,12},{10,14},{12,8},{14,10},{16,20},{18,... | collective-permute-start | bytes 884744 | tf_op jit(solution)/shard_map/piece_l2/ppermute | solution.py:474
  63.1 8.1 %collective-permute-start.25 = (bf16[128,1024]{1,0:T(8,128)(2,1)S(1)}, bf16[128,1024]{1,0:T(8,128)(2,1)S(1)}, u32[]{:S(2)}, u32[]{:S(2)}) collective-permute-start(bf16[128,1024]{1,0:T(8,128)(2,1)S(1)} %collective-permute-done.19.refs_6_.refs_1_.refs_2_), channel_id=1, source_target_pairs={{0,2},{2,0},{4,6},{6,4},{8,10},{10,8},{12,14},{14,12},{16,18},{18,... | collective-permute-start | bytes 786440 | tf_op jit(solution)/shard_map/side_b2/ppermute | solution.py:470
  63.7 8.4 %collective-permute-start.20 = (bf16[128,1024]{1,0:T(8,128)(2,1)S(1)}, bf16[128,1024]{1,0:T(8,128)(2,1)S(1)}, u32[]{:S(2)}, u32[]{:S(2)}) collective-permute-start(bf16[128,1024]{1,0:T(8,128)(2,1)S(1)} %tie_rows.9.refs_4_), channel_id=1, source_target_pairs={{0,8},{2,10},{4,12},{6,14},{8,16},{10,18},{12,20},{14,22},{16,24},... | collective-permute-start | bytes 786440 | tf_op jit(solution)/shard_map/plane_b1/ppermute | solution.py:459
  63.8 10.3 %collective-permute-start.24 = (bf16[128,1024]{1,0:T(8,128)(2,1)S(1)}, bf16[128,1024]{1,0:T(8,128)(2,1)S(1)}, u32[]{:S(2)}, u32[]{:S(2)}) collective-permute-start(bf16[128,1024]{1,0:T(8,128)(2,1)S(1)} %collective-permute-done.23.refs_6_.refs_2_), channel_id=1, source_target_pairs={{0,2},{2,0},{4,6},{6,4},{8,10},{10,8},{12,14},{14,12},{16,18},{18,... | collective-permute-start | bytes 786440 | tf_op jit(solution)/shard_map/side_b3/ppermute | solution.py:470
  71.7 9.3 %collective-permute-start.26 = (bf16[144,1024]{1,0:T(8,128)(2,1)S(1)}, bf16[144,1024]{1,0:T(8,128)(2,1)S(1)}, u32[]{:S(2)}, u32[]{:S(2)}) collective-permute-start(bf16[144,1024]{1,0:T(8,128)(2,1)S(1)} %get-tuple-element.98), channel_id=1, source_target_pairs={{0,4},{2,6},{4,0},{6,2},{8,12},{10,14},{12,8},{14,10},{16,20},{18,... | collective-permute-start | bytes 884744 | tf_op jit(solution)/shard_map/piece_b2/ppermute | solution.py:474
  72.1 64.2 %collective-permute-start.41 = (bf16[4096,512]{1,0:T(8,128)(2,1)S(1)}, bf16[4096,512]{1,0:T(8,128)(2,1)S(1)}, u32[]{:S(2)}, u32[]{:S(2)}) collective-permute-start(bf16[4096,512]{1,0:T(8,128)(2,1)S(1)} %copy-done), channel_id=1, source_target_pairs={{0,1},{1,0},{2,3},{3,2},{4,5},{5,4},{6,7},{7,6},{8,9},{9,8},{10,11... | collective-permute-start | bytes 12582920 | tf_op jit(solution)/shard_map/ppermute | solution.py:456
  72.1 8.9 %collective-permute-start.21 = (bf16[128,1024]{1,0:T(8,128)(2,1)S(1)}, bf16[128,1024]{1,0:T(8,128)(2,1)S(1)}, u32[]{:S(2)}, u32[]{:S(2)}) collective-permute-start(bf16[128,1024]{1,0:T(8,128)(2,1)S(1)} %collective-permute-done.20.refs_6_.refs_2_), channel_id=1, source_target_pairs={{0,2},{2,0},{4,6},{6,4},{8,10},{10,8},{12,14},{14,12},{16,18},{18,... | collective-permute-start | bytes 786440 | tf_op jit(solution)/shard_map/side_b1/ppermute | solution.py:470
  74.7 11.1 %collective-permute-start.28 = (bf16[144,1024]{1,0:T(8,128)(2,1)S(1)}, bf16[144,1024]{1,0:T(8,128)(2,1)S(1)}, u32[]{:S(2)}, u32[]{:S(2)}) collective-permute-start(bf16[144,1024]{1,0:T(8,128)(2,1)S(1)} %get-tuple-element.103), channel_id=1, source_target_pairs={{0,4},{2,6},{4,0},{6,2},{8,12},{10,14},{12,8},{14,10},{16,20},{18,... | collective-permute-start | bytes 884744 | tf_op jit(solution)/shard_map/piece_b3/ppermute | solution.py:474
  81.5 10.4 %collective-permute-start.27 = (bf16[144,1024]{1,0:T(8,128)(2,1)S(1)}, bf16[144,1024]{1,0:T(8,128)(2,1)S(1)}, u32[]{:S(2)}, u32[]{:S(2)}) collective-permute-start(bf16[144,1024]{1,0:T(8,128)(2,1)S(1)} %get-tuple-element.100), channel_id=1, source_target_pairs={{0,4},{2,6},{4,0},{6,2},{8,12},{10,14},{12,8},{14,10},{16,20},{18,... | collective-permute-start | bytes 884744 | tf_op jit(solution)/shard_map/piece_b1/ppermute | solution.py:474
  91.8 6.8 %collective-permute-start.29 = (bf16[144,1024]{1,0:T(8,128)(2,1)S(1)}, bf16[144,1024]{1,0:T(8,128)(2,1)S(1)}, u32[]{:S(2)}, u32[]{:S(2)}) collective-permute-start(bf16[144,1024]{1,0:T(8,128)(2,1)S(1)} %get-tuple-element.111), channel_id=1, source_target_pairs={{0,4},{2,6},{4,0},{6,2},{8,12},{10,14},{12,8},{14,10},{16,20},{18,... | collective-permute-start | bytes 884744 | tf_op jit(solution)/shard_map/piece_r3/ppermute | solution.py:474
  99.1 7.7 %collective-permute-start.30 = (bf16[144,1024]{1,0:T(8,128)(2,1)S(1)}, bf16[144,1024]{1,0:T(8,128)(2,1)S(1)}, u32[]{:S(2)}, u32[]{:S(2)}) collective-permute-start(bf16[144,1024]{1,0:T(8,128)(2,1)S(1)} %get-tuple-element.114), channel_id=1, source_target_pairs={{0,4},{2,6},{4,0},{6,2},{8,12},{10,14},{12,8},{14,10},{16,20},{18,... | collective-permute-start | bytes 884744 | tf_op jit(solution)/shard_map/piece_r2/ppermute | solution.py:474
  100.4 6.4 %collective-permute-start.31 = (bf16[128,1024]{1,0:T(8,128)(2,1)S(1)}, bf16[128,1024]{1,0:T(8,128)(2,1)S(1)}, u32[]{:S(2)}, u32[]{:S(2)}) collective-permute-start(bf16[128,1024]{1,0:T(8,128)(2,1)S(1)} %get-tuple-element.116), channel_id=1, source_target_pairs={{0,2},{2,0},{4,6},{6,4},{8,10},{10,8},{12,14},{14,12},{16,18},{18,... | collective-permute-start | bytes 786440 | tf_op jit(solution)/shard_map/side_r3/ppermute | solution.py:470
  107.4 14.8 %collective-permute-start.37 = (bf16[1024,1536]{1,0:T(8,128)(2,1)S(1)}, bf16[1024,1536]{1,0:T(8,128)(2,1)S(1)}, u32[]{:S(2)}, u32[]{:S(2)}) collective-permute-start(bf16[1024,1536]{1,0:T(8,128)(2,1)S(1)} %get-tuple-element.140), channel_id=1, source_target_pairs={{0,1},{1,0},{2,3},{3,2},{4,5},{5,4},{6,7},{7,6},{8,9},{9,8},{10,11... | collective-permute-start | bytes 9437192 | tf_op jit(solution)/shard_map/ppermute | solution.py:456
  107.4 12.0 %collective-permute-start.32 = (bf16[144,1024]{1,0:T(8,128)(2,1)S(1)}, bf16[144,1024]{1,0:T(8,128)(2,1)S(1)}, u32[]{:S(2)}, u32[]{:S(2)}) collective-permute-start(bf16[144,1024]{1,0:T(8,128)(2,1)S(1)} %get-tuple-element.130), channel_id=1, source_target_pairs={{0,4},{2,6},{4,0},{6,2},{8,12},{10,14},{12,8},{14,10},{16,20},{18,... | collective-permute-start | bytes 884744 | tf_op jit(solution)/shard_map/piece_r1/ppermute | solution.py:474
  108.3 8.4 %collective-permute-start.33 = (bf16[128,1024]{1,0:T(8,128)(2,1)S(1)}, bf16[128,1024]{1,0:T(8,128)(2,1)S(1)}, u32[]{:S(2)}, u32[]{:S(2)}) collective-permute-start(bf16[128,1024]{1,0:T(8,128)(2,1)S(1)} %get-tuple-element.132), channel_id=1, source_target_pairs={{0,2},{2,0},{4,6},{6,4},{8,10},{10,8},{12,14},{14,12},{16,18},{18,... | collective-permute-start | bytes 786440 | tf_op jit(solution)/shard_map/side_r2/ppermute | solution.py:470
  109.5 9.9 %collective-permute-start.34 = (bf16[128,1024]{1,0:T(8,128)(2,1)S(1)}, bf16[128,1024]{1,0:T(8,128)(2,1)S(1)}, u32[]{:S(2)}, u32[]{:S(2)}) collective-permute-start(bf16[128,1024]{1,0:T(8,128)(2,1)S(1)} %get-tuple-element.136), channel_id=1, source_target_pairs={{0,8},{2,10},{4,12},{6,14},{8,16},{10,18},{12,20},{14,22},{16,24},... | collective-permute-start | bytes 786440 | tf_op jit(solution)/shard_map/plane_r3/ppermute | solution.py:459
  120.0 12.1 %collective-permute-start.42 = (bf16[1536,512]{1,0:T(8,128)(2,1)S(1)}, bf16[1536,512]{1,0:T(8,128)(2,1)S(1)}, u32[]{:S(2)}, u32[]{:S(2)}) collective-permute-start(bf16[1536,512]{1,0:T(8,128)(2,1)S(1)} %get-tuple-element.147), channel_id=1, source_target_pairs={{0,1},{1,0},{2,3},{3,2},{4,5},{5,4},{6,7},{7,6},{8,9},{9,8},{10,11... | collective-permute-start | bytes 4718600 | tf_op jit(solution)/shard_map/ppermute | solution.py:456
  120.0 9.7 %collective-permute-start.35 = (bf16[144,1024]{1,0:T(8,128)(2,1)S(1)}, bf16[144,1024]{1,0:T(8,128)(2,1)S(1)}, u32[]{:S(2)}, u32[]{:S(2)}) collective-permute-start(bf16[144,1024]{1,0:T(8,128)(2,1)S(1)} %get-tuple-element.137), channel_id=1, source_target_pairs={{0,4},{2,6},{4,0},{6,2},{8,12},{10,14},{12,8},{14,10},{16,20},{18,... | collective-permute-start | bytes 884744 | tf_op jit(solution)/shard_map/piece_r0/ppermute | solution.py:474
  121.4 8.4 %collective-permute-start.36 = (bf16[128,1024]{1,0:T(8,128)(2,1)S(1)}, bf16[128,1024]{1,0:T(8,128)(2,1)S(1)}, u32[]{:S(2)}, u32[]{:S(2)}) collective-permute-start(bf16[128,1024]{1,0:T(8,128)(2,1)S(1)} %get-tuple-element.139), channel_id=1, source_target_pairs={{0,2},{2,0},{4,6},{6,4},{8,10},{10,8},{12,14},{14,12},{16,18},{18,... | collective-permute-start | bytes 786440 | tf_op jit(solution)/shard_map/side_r1/ppermute | solution.py:470
  122.2 14.1 %collective-permute-start.40 = (bf16[128,1024]{1,0:T(8,128)(2,1)S(1)}, bf16[128,1024]{1,0:T(8,128)(2,1)S(1)}, u32[]{:S(2)}, u32[]{:S(2)}) collective-permute-start(bf16[128,1024]{1,0:T(8,128)(2,1)S(1)} %get-tuple-element.145), channel_id=1, source_target_pairs={{0,16},{2,18},{4,20},{6,22},{8,24},{10,26},{12,28},{14,30},{16,0},... | collective-permute-start | bytes 786440 | tf_op jit(solution)/shard_map/plane_r2/ppermute | solution.py:459
  130.3 7.8 %collective-permute-start.38 = (bf16[128,1024]{1,0:T(8,128)(2,1)S(1)}, bf16[128,1024]{1,0:T(8,128)(2,1)S(1)}, u32[]{:S(2)}, u32[]{:S(2)}) collective-permute-start(bf16[128,1024]{1,0:T(8,128)(2,1)S(1)} %get-tuple-element.143), channel_id=1, source_target_pairs={{0,2},{2,0},{4,6},{6,4},{8,10},{10,8},{12,14},{14,12},{16,18},{18,... | collective-permute-start | bytes 786440 | tf_op jit(solution)/shard_map/side_r0/ppermute | solution.py:470
  131.2 9.1 %collective-permute-start.39 = (bf16[128,1024]{1,0:T(8,128)(2,1)S(1)}, bf16[128,1024]{1,0:T(8,128)(2,1)S(1)}, u32[]{:S(2)}, u32[]{:S(2)}) collective-permute-start(bf16[128,1024]{1,0:T(8,128)(2,1)S(1)} %get-tuple-element.144), channel_id=1, source_target_pairs={{0,24},{2,26},{4,28},{6,30},{8,0},{10,2},{12,4},{14,6},{16,8},{18,... | collective-permute-start | bytes 786440 | tf_op jit(solution)/shard_map/plane_r1/ppermute | solution.py:459

commit v3 on v2

--- a/solution.py
+++ b/solution.py
@@ -597,7 +597,7 @@
     to_plane("b", 2, blocks["l", 3])
     pick("l", 3, come("l", 0))
     to_side("b", 0)
-    pick("b", 0, come("l", 1), blocks["l", 2])
+    pick("b", 0, come("l", 1))
     to_side("l", 2)
     to_plane("b", 3, blocks["l", 2])
     ahead((0, 1))

time: 144 us -> 144 us (level)
  no operation moved by 1% of the time
where the time goes in v3:
time: 144 us
  Pallas kernels  51.4 us (36%)
  starting transfers between devices  43.6 us (30%)
  waiting for transfers between devices  38.5 us (27%)
  matrix products  9.49 us (7%)
    pallas_call x4, Pallas kernels, weight_grads(): pl.pallas_call(functools.partial(weight_body, len(groups), kinds, column,...  20 us
    ppermute x12, waiting for transfers between devices, beside(): return lax.ppermute(a, 'expert', [(i, i ^ 1) for i in range(group_count)])  16.5 us
    ppermute x9, waiting for transfers between devices, along(): lax.ppermute(a, 'expert', [(z * inner + p, (z + shift) % PLANES * inner +...  16.4 us
    ppermute x9, starting transfers between devices, along(): lax.ppermute(a, 'expert', [(z * inner + p, (z + shift) % PLANES * inner +...  15.1 us
    ppermute x12, starting transfers between devices, beside(): return lax.ppermute(a, 'expert', [(i, i ^ 1) for i in range(group_count)])  14.2 us
    ppermute x12, starting transfers between devices, across(): lax.ppermute(parts[k], 'expert', [(i, i ^ SIDE * k) for i in range(group_...  12.2 us
    pallas_call x2, Pallas kernels, backward(): pl.pallas_call(functools.partial(backward_body, count, len(deps)), in_spe...  11.9 us
    pallas_call x2, Pallas kernels, forward(): pl.pallas_call(functools.partial(forward_body, count, len(deps)), in_spec...  9.68 us
  transfers between devices with their start and end apart: 43, of which 15 were waited for; matrix products, arithmetic and copies ran while one was open for 6% of the time, Pallas kernels for 33%

profile of v3, /device:TPU:0, one launch (start us, length us, event | category | flops | bytes accessed | tf_op | source)
XLA Modules:
  0.0 144.1 jit_solution(76991976933077779)
XLA Ops:
  0.6 0.5 collective-permute-start
  1.2 3.5 %convolution_convert_fusion.3.own_ref = bf16[128,512]{1,0:T(8,128)(2,1)S(1)} fusion(bf16[128,4096]{1,0:T(8,128)(2,1)} %param.10, bf16[4096,512]{1,0:T(8,128)(2,1)} %refs_5_), kind=kOutput, calls=%fused_computation.3 | convolution fusion | flops 536936448 | bytes 5373952 | tf_op jit(solution)/shard_map/dot_general | solution.py:493
  4.8 0.7 convolution_convert_fusion.2.refs_3_
  5.6 1.3 collective-permute-done.1.other_ref
  8.1 2.8 %collective-permute-start.9 = (bf16[144,1024]{1,0:T(8,128)(2,1)S(1)}, bf16[144,1024]{1,0:T(8,128)(2,1)S(1)}, u32[]{:S(2)}, u32[]{:S(2)}) collective-permute-start(bf16[144,1024]{1,0:T(8,128)(2,1)S(1)} %join_rows.2.block_ref.refs_0_.refs_2_), channel_id=1, source_target_pairs={{0,8},{2,10},{4,12},{6,14},{8,16},{10,18},{12,20},{14,22},{16,24},... | collective-permute-start | bytes 884744 | tf_op jit(solution)/shard_map/plane_l1/ppermute | solution.py:459
  10.9 3.8 %convolution_convert_fusion.1.own_ref = bf16[128,512]{1,0:T(8,128)(2,1)S(1)} fusion(bf16[128,4096]{1,0:T(8,128)(2,1)S(1)} %copy-done.8, bf16[512,4096]{1,0:T(8,128)(2,1)} %param.16), kind=kOutput, calls=%fused_computation.1 | convolution fusion | flops 536936448 | bytes 5373952 | tf_op jit(solution)/shard_map/dot_general | solution.py:493
  14.7 1.5 %convolution_convert_fusion.refs_0_ = bf16[128,512]{1,0:T(8,128)(2,1)S(1)} fusion(bf16[128,4096]{1,0:T(8,128)(2,1)S(1)} %collective-permute-done.3, bf16[512,4096]{1,0:T(8,128)(2,1)S(1)} %copy-done.7), kind=kOutput, calls=%fused_computation | convolution fusion | flops 536936448 | bytes 5373952 | tf_op jit(solution)/shard_map/dot_general | solution.py:493
  16.4 1.5 %collective-permute-start.2 = (bf16[144,1024]{1,0:T(8,128)(2,1)S(1)}, bf16[144,1024]{1,0:T(8,128)(2,1)S(1)}, u32[]{:S(2)}, u32[]{:S(2)}) collective-permute-start(bf16[144,1024]{1,0:T(8,128)(2,1)S(1)} %join_rows.2.block_ref.refs_0_.refs_2_), channel_id=1, source_target_pairs={{0,2},{2,0},{4,6},{6,4},{8,10},{10,8},{12,14},{14,12},{16,18},{18,... | collective-permute-start | bytes 884744 | tf_op jit(solution)/shard_map/side_l0/ppermute | solution.py:470
  17.9 3.6 %collective-permute-start.7 = (bf16[144,1024]{1,0:T(8,128)(2,1)S(1)}, bf16[144,1024]{1,0:T(8,128)(2,1)S(1)}, u32[]{:S(2)}, u32[]{:S(2)}) collective-permute-start(bf16[144,1024]{1,0:T(8,128)(2,1)S(1)} %tie_rows.5.refs_0_), channel_id=1, source_target_pairs={{0,24},{2,26},{4,28},{6,30},{8,0},{10,2},{12,4},{14,6},{16,8},{18,... | collective-permute-start | bytes 884744 | tf_op jit(solution)/shard_map/plane_l3/ppermute | solution.py:459
  21.5 1.5 %collective-permute-start.10 = (bf16[144,1024]{1,0:T(8,128)(2,1)S(1)}, bf16[144,1024]{1,0:T(8,128)(2,1)S(1)}, u32[]{:S(2)}, u32[]{:S(2)}) collective-permute-start(bf16[144,1024]{1,0:T(8,128)(2,1)S(1)} %collective-permute-done.9.refs_5_.refs_1_.refs_0_.refs_2_), channel_id=1, source_target_pairs={{0,2},{2,0},{4,6},{6,4},{8,10},{10,8},{12,14},{14,12},{16,18},{18,... | collective-permute-start | bytes 884744 | tf_op jit(solution)/shard_map/side_l1/ppermute | solution.py:470
  23.0 3.2 %collective-permute-done.2.refs_1_.refs_3_ = bf16[144,1024]{1,0:T(8,128)(2,1)S(1)} collective-permute-done((bf16[144,1024]{1,0:T(8,128)(2,1)S(1)}, bf16[144,1024]{1,0:T(8,128)(2,1)S(1)}, u32[]{:S(2)}, u32[]{:S(2)}) %collective-permute-start.2) | collective-permute-done | bytes 294944 | tf_op jit(solution)/shard_map/side_l0/ppermute | solution.py:470
  26.2 0.5 select_latent.4
  26.7 1.6 %collective-permute-start.13 = (bf16[144,1024]{1,0:T(8,128)(2,1)S(1)}, bf16[144,1024]{1,0:T(8,128)(2,1)S(1)}, u32[]{:S(2)}, u32[]{:S(2)}) collective-permute-start(bf16[144,1024]{1,0:T(8,128)(2,1)S(1)} %get-tuple-element.86), channel_id=1, source_target_pairs={{0,4},{2,6},{4,0},{6,2},{8,12},{10,14},{12,8},{14,10},{16,20},{18,... | collective-permute-start | bytes 884744 | tf_op jit(solution)/shard_map/piece_l0/ppermute | solution.py:474
  28.3 2.7 %collective-permute-start.16 = (bf16[144,1024]{1,0:T(8,128)(2,1)S(1)}, bf16[144,1024]{1,0:T(8,128)(2,1)S(1)}, u32[]{:S(2)}, u32[]{:S(2)}) collective-permute-start(bf16[144,1024]{1,0:T(8,128)(2,1)S(1)} %tie_rows.6.refs_4_), channel_id=1, source_target_pairs={{0,16},{2,18},{4,20},{6,22},{8,24},{10,26},{12,28},{14,30},{16,0},... | collective-permute-start | bytes 884744 | tf_op jit(solution)/shard_map/plane_l2/ppermute | solution.py:459
  30.9 1.5 %collective-permute-start.8 = (bf16[144,1024]{1,0:T(8,128)(2,1)S(1)}, bf16[144,1024]{1,0:T(8,128)(2,1)S(1)}, u32[]{:S(2)}, u32[]{:S(2)}) collective-permute-start(bf16[144,1024]{1,0:T(8,128)(2,1)S(1)} %collective-permute-done.7.refs_5_.refs_1_.refs_0_.refs_2_), channel_id=1, source_target_pairs={{0,2},{2,0},{4,6},{6,4},{8,10},{10,8},{12,14},{14,12},{16,18},{18,... | collective-permute-start | bytes 884744 | tf_op jit(solution)/shard_map/side_l3/ppermute | solution.py:470
  32.4 0.5 select_latent.5
  32.9 1.7 %collective-permute-start.14 = (bf16[144,1024]{1,0:T(8,128)(2,1)S(1)}, bf16[144,1024]{1,0:T(8,128)(2,1)S(1)}, u32[]{:S(2)}, u32[]{:S(2)}) collective-permute-start(bf16[144,1024]{1,0:T(8,128)(2,1)S(1)} %get-tuple-element.88), channel_id=1, source_target_pairs={{0,4},{2,6},{4,0},{6,2},{8,12},{10,14},{12,8},{14,10},{16,20},{18,... | collective-permute-start | bytes 884744 | tf_op jit(solution)/shard_map/piece_l1/ppermute | solution.py:474
  34.6 1.5 %collective-permute-start.6 = (bf16[128,1024]{1,0:T(8,128)(2,1)S(1)}, bf16[128,1024]{1,0:T(8,128)(2,1)S(1)}, u32[]{:S(2)}, u32[]{:S(2)}) collective-permute-start(bf16[128,1024]{1,0:T(8,128)(2,1)S(1)} %join_rows.3.refs_4_.block_ref.refs_2_), channel_id=1, source_target_pairs={{0,2},{2,0},{4,6},{6,4},{8,10},{10,8},{12,14},{14,12},{16,18},{18,... | collective-permute-start | bytes 786440 | tf_op jit(solution)/shard_map/side_b0/ppermute | solution.py:470
  36.1 2.6 %collective-permute-start.19 = (bf16[128,1024]{1,0:T(8,128)(2,1)S(1)}, bf16[128,1024]{1,0:T(8,128)(2,1)S(1)}, u32[]{:S(2)}, u32[]{:S(2)}) collective-permute-start(bf16[128,1024]{1,0:T(8,128)(2,1)S(1)} %tie_rows.7.refs_4_), channel_id=1, source_target_pairs={{0,16},{2,18},{4,20},{6,22},{8,24},{10,26},{12,28},{14,30},{16,0},... | collective-permute-start | bytes 786440 | tf_op jit(solution)/shard_map/plane_b2/ppermute | solution.py:459
  38.7 11.4 %collective-permute-done.16.refs_1_.refs_0_.refs_2_ = bf16[144,1024]{1,0:T(8,128)(2,1)S(1)} collective-permute-done((bf16[144,1024]{1,0:T(8,128)(2,1)S(1)}, bf16[144,1024]{1,0:T(8,128)(2,1)S(1)}, u32[]{:S(2)}, u32[]{:S(2)}) %collective-permute-start.16) | collective-permute-done | bytes 294944 | tf_op jit(solution)/shard_map/plane_l2/ppermute | solution.py:459
  50.2 1.5 %collective-permute-start.17 = (bf16[144,1024]{1,0:T(8,128)(2,1)S(1)}, bf16[144,1024]{1,0:T(8,128)(2,1)S(1)}, u32[]{:S(2)}, u32[]{:S(2)}) collective-permute-start(bf16[144,1024]{1,0:T(8,128)(2,1)S(1)} %collective-permute-done.16.refs_1_.refs_0_.refs_2_), channel_id=1, source_target_pairs={{0,2},{2,0},{4,6},{6,4},{8,10},{10,8},{12,14},{14,12},{16,18},{18,... | collective-permute-start | bytes 884744 | tf_op jit(solution)/shard_map/side_l2/ppermute | solution.py:470
  51.7 0.5 select_latent.6
  52.1 0.6 collective-permute-start.18
  52.7 0.5 select_back.4
  53.2 2.5 %collective-permute-start.23 = (bf16[128,1024]{1,0:T(8,128)(2,1)S(1)}, bf16[128,1024]{1,0:T(8,128)(2,1)S(1)}, u32[]{:S(2)}, u32[]{:S(2)}) collective-permute-start(bf16[128,1024]{1,0:T(8,128)(2,1)S(1)} %tie_rows.8.refs_8_), channel_id=1, source_target_pairs={{0,24},{2,26},{4,28},{6,30},{8,0},{10,2},{12,4},{14,6},{16,8},{18,... | collective-permute-start | bytes 786440 | tf_op jit(solution)/shard_map/plane_b3/ppermute | solution.py:459
  55.7 1.5 %collective-permute-start.15 = (bf16[144,1024]{1,0:T(8,128)(2,1)S(1)}, bf16[144,1024]{1,0:T(8,128)(2,1)S(1)}, u32[]{:S(2)}, u32[]{:S(2)}) collective-permute-start(bf16[144,1024]{1,0:T(8,128)(2,1)S(1)} %get-tuple-element.90), channel_id=1, source_target_pairs={{0,4},{2,6},{4,0},{6,2},{8,12},{10,14},{12,8},{14,10},{16,20},{18,... | collective-permute-start | bytes 884744 | tf_op jit(solution)/shard_map/piece_b0/ppermute | solution.py:474
  57.3 4.8 %forward_rows.2 = (bf16[576,1024]{1,0:T(8,128)(2,1)S(1)}, bf16[576,1536]{1,0:T(8,128)(2,1)S(1)}, bf16[576,1536]{1,0:T(8,128)(2,1)S(1)}, bf16[576,1536]{1,0:T(8,128)(2,1)S(1)}, f32[8,128]{1,0:T(8,128)S(1)}) custom-call(bf16[144,1024]{1,0:T(8,128)(2,1)S(1)} %get-tuple-element.84.refs_0_, bf16[144,1024]{1,0:T(8,128)(2,1)S(1)} %collective-permute-done.13.refs_5_.refs_1_, ...), custom_call_target="tpu_custom_call" | custom-call | flops 3623878656 | bytes 11599873 | tf_op jit(solution)/shard_map/forward_rows/pallas_call | solution.py:287
  62.1 0.5 select_latent.7
  62.6 0.6 collective-permute-start.22
  63.1 0.5 collective-permute-start.25
  63.8 1.6 %collective-permute-start.24 = (bf16[128,1024]{1,0:T(8,128)(2,1)S(1)}, bf16[128,1024]{1,0:T(8,128)(2,1)S(1)}, u32[]{:S(2)}, u32[]{:S(2)}) collective-permute-start(bf16[128,1024]{1,0:T(8,128)(2,1)S(1)} %collective-permute-done.23.refs_6_.refs_2_), channel_id=1, source_target_pairs={{0,2},{2,0},{4,6},{6,4},{8,10},{10,8},{12,14},{14,12},{16,18},{18,... | collective-permute-start | bytes 786440 | tf_op jit(solution)/shard_map/side_b3/ppermute | solution.py:470
  65.3 5.9 %collective-permute-done.25.refs_3_ = bf16[128,1024]{1,0:T(8,128)(2,1)S(1)} collective-permute-done((bf16[128,1024]{1,0:T(8,128)(2,1)S(1)}, bf16[128,1024]{1,0:T(8,128)(2,1)S(1)}, u32[]{:S(2)}, u32[]{:S(2)}) %collective-permute-start.25) | collective-permute-done | bytes 262176 | tf_op jit(solution)/shard_map/side_b2/ppermute | solution.py:470
  71.2 0.5 select_back.5
  72.1 1.3 collective-permute-start.21
  73.4 0.6 collective-permute-done.24.refs_3_
  74.7 0.8 collective-permute-start.28
  75.5 4.9 %forward_rows.3 = (bf16[576,1024]{1,0:T(8,128)(2,1)S(1)}, bf16[576,1536]{1,0:T(8,128)(2,1)S(1)}, bf16[576,1536]{1,0:T(8,128)(2,1)S(1)}, bf16[576,1536]{1,0:T(8,128)(2,1)S(1)}, f32[8,128]{1,0:T(8,128)S(1)}) custom-call(bf16[144,1024]{1,0:T(8,128)(2,1)S(1)} %get-tuple-element.87.refs_4_.refs_0_, bf16[144,1024]{1,0:T(8,128)(2,1)S(1)} %collective-permute-done.18.refs_5_.refs_1_, ...), custom_call_target="tpu_custom_call" | custom-call | flops 3623878656 | bytes 11599873 | tf_op jit(solution)/shard_map/forward_rows/pallas_call | solution.py:287
  80.4 0.6 collective-permute-done.26.refs_5_.refs_3_
  81.0 0.5 select_back.7
  81.5 1.6 %collective-permute-start.27 = (bf16[144,1024]{1,0:T(8,128)(2,1)S(1)}, bf16[144,1024]{1,0:T(8,128)(2,1)S(1)}, u32[]{:S(2)}, u32[]{:S(2)}) collective-permute-start(bf16[144,1024]{1,0:T(8,128)(2,1)S(1)} %get-tuple-element.100), channel_id=1, source_target_pairs={{0,4},{2,6},{4,0},{6,2},{8,12},{10,14},{12,8},{14,10},{16,20},{18,... | collective-permute-start | bytes 884744 | tf_op jit(solution)/shard_map/piece_b1/ppermute | solution.py:474
  83.0 2.8 %collective-permute-done.28.refs_1_ = bf16[144,1024]{1,0:T(8,128)(2,1)S(1)} collective-permute-done((bf16[144,1024]{1,0:T(8,128)(2,1)S(1)}, bf16[144,1024]{1,0:T(8,128)(2,1)S(1)}, u32[]{:S(2)}, u32[]{:S(2)}) %collective-permute-start.28) | collective-permute-done | bytes 294944 | tf_op jit(solution)/shard_map/piece_b3/ppermute | solution.py:474
  85.8 5.9 %backward_rows.2 = (bf16[576,1024]{1,0:T(8,128)(2,1)S(1)}, bf16[576,1536]{1,0:T(8,128)(2,1)S(1)}, bf16[576,1536]{1,0:T(8,128)(2,1)S(1)}, bf16[144,1024]{1,0:T(8,...) custom-call(bf16[144,1024]{1,0:T(8,128)(2,1)S(1)} %get-tuple-element, ...), custom_call_target="tpu_custom_call" | custom-call | flops 5435817984 | bytes 16515073 | tf_op jit(solution)/shard_map/backward_rows/pallas_call | solution.py:334
  91.9 5.9 %backward_rows.3 = (bf16[576,1024]{1,0:T(8,128)(2,1)S(1)}, bf16[576,1536]{1,0:T(8,128)(2,1)S(1)}, bf16[576,1536]{1,0:T(8,128)(2,1)S(1)}, bf16[144,1024]{1,0:T(8,...) custom-call(bf16[144,1024]{1,0:T(8,128)(2,1)S(1)} %get-tuple-element, ...), custom_call_target="tpu_custom_call" | custom-call | flops 5435817984 | bytes 16515073 | tf_op jit(solution)/shard_map/backward_rows/pallas_call | solution.py:334
  97.8 0.8 collective-permute-done.29.refs_3_
  98.6 0.5 return_rows.4
  99.1 1.3 collective-permute-start.30
  100.8 5.5 %weight_grads.4 = (bf16[1024,1536]{1,0:T(8,128)(2,1)S(1)}, f32[8,128]{1,0:T(8,128)S(1)}) custom-call(bf16[576,1024]{1,0:T(8,128)(2,1)S(1)} %get-tuple-element.118.refs_0_, bf16[576,1024]{1,0:T(8,128)(2,1)S(1)} %get-tuple-element.119.refs_1_, bf16[576,1536]{1,0:T(8,128)(2,1)S(1)} %get-tuple-element.120.refs_2_, ...), custom_call_target="tpu_custom_call" | custom-call | flops 3623878656 | bytes 7077889 | tf_op jit(solution)/shard_map/weight_grads/pallas_call | solution.py:388
  106.8 0.6 return_rows.5
  107.4 0.8 collective-permute-start.32
  108.3 1.2 collective-permute-start.33
  109.5 3.0 %weight_grads.5 = (bf16[1536,512]{1,0:T(8,128)(2,1)S(1)}, f32[8,128]{1,0:T(8,128)S(1)}) custom-call(bf16[576,1024]{1,0:T(8,128)(2,1)S(1)} %get-tuple-element.118.refs_0_, bf16[576,1024]{1,0:T(8,128)(2,1)S(1)} %get-tuple-element.119.refs_1_, bf16[576,1536]{1,0:T(8,128)(2,1)S(1)} %get-tuple-element.120.refs_2_, ...), custom_call_target="tpu_custom_call" | custom-call | flops 1811939328 | bytes 7077889 | tf_op jit(solution)/shard_map/weight_grads/pallas_call | solution.py:388
  112.5 4.1 %collective-permute-done.33.refs_5_ = bf16[128,1024]{1,0:T(8,128)(2,1)S(1)} collective-permute-done((bf16[128,1024]{1,0:T(8,128)(2,1)S(1)}, bf16[128,1024]{1,0:T(8,128)(2,1)S(1)}, u32[]{:S(2)}, u32[]{:S(2)}) %collective-permute-start.33) | collective-permute-done | bytes 262176 | tf_op jit(solution)/shard_map/side_r2/ppermute | solution.py:470
  116.6 2.7 %collective-permute-done.34.refs_9_.refs_4_ = bf16[128,1024]{1,0:T(8,128)(2,1)S(1)} collective-permute-done((bf16[128,1024]{1,0:T(8,128)(2,1)S(1)}, bf16[128,1024]{1,0:T(8,128)(2,1)S(1)}, u32[]{:S(2)}, u32[]{:S(2)}) %collective-permute-start.34) | collective-permute-done | bytes 262176 | tf_op jit(solution)/shard_map/plane_r3/ppermute | solution.py:459
  119.4 0.6 return_rows.6
  120.0 1.3 collective-permute-start.35
  121.4 0.8 collective-permute-start.36
  122.2 7.2 %weight_grads.6 = (bf16[512,1536]{1,0:T(8,128)(2,1)}, bf16[512,1536]{1,0:T(8,128)(2,1)}, f32[8,128]{1,0:T(8,128)S(1)}) custom-call(bf16[576,1024]{1,0:T(8,128)(2,1)S(1)} %get-tuple-element.118.refs_0_, bf16[576,1024]{1,0:T(8,128)(2,1)S(1)} %get-tuple-element.119.refs_1_, bf16[576,1536]{1,0:T(8,128)(2,1)S(1)} %get-tuple-element.120.refs_2_, ...), custom_call_target="tpu_custom_call" | custom-call | flops 3623878656 | bytes 7077889 | tf_op jit(solution)/shard_map/weight_grads/pallas_call | solution.py:388
  129.7 0.6 return_rows.7
  130.3 0.9 collective-permute-start.38
  131.2 0.8 collective-permute-start.39
  132.1 4.2 %weight_grads.7 = (bf16[1536,512]{1,0:T(8,128)(2,1)}, f32[8,128]{1,0:T(8,128)S(1)}) custom-call(bf16[576,1024]{1,0:T(8,128)(2,1)S(1)} %get-tuple-element.118.refs_0_, bf16[576,1024]{1,0:T(8,128)(2,1)S(1)} %get-tuple-element.119.refs_1_, bf16[576,1536]{1,0:T(8,128)(2,1)S(1)} %get-tuple-element.120.refs_2_, bf16[576,1536]{1,0:T(8,128)(2,1)S(1)} %get-tuple-element.121.refs_3_, ...), custom_call_target="tpu_custom_call" | custom-call | flops 1811939328 | bytes 7077889 | tf_op jit(solution)/shard_map/weight_grads/pallas_call | solution.py:388
  136.3 1.8 %collective-permute-done.38.refs_1_ = bf16[128,1024]{1,0:T(8,128)(2,1)S(1)} collective-permute-done((bf16[128,1024]{1,0:T(8,128)(2,1)S(1)}, bf16[128,1024]{1,0:T(8,128)(2,1)S(1)}, u32[]{:S(2)}, u32[]{:S(2)}) %collective-permute-start.38) | collective-permute-done | bytes 262176 | tf_op jit(solution)/shard_map/side_r0/ppermute | solution.py:470
  138.1 2.2 %collective-permute-done.39.refs_2_ = bf16[128,1024]{1,0:T(8,128)(2,1)S(1)} collective-permute-done((bf16[128,1024]{1,0:T(8,128)(2,1)S(1)}, bf16[128,1024]{1,0:T(8,128)(2,1)S(1)}, u32[]{:S(2)}, u32[]{:S(2)}) %collective-permute-start.39) | collective-permute-done | bytes 262176 | tf_op jit(solution)/shard_map/plane_r1/ppermute | solution.py:459
  140.3 3.8 %token_grad.1 = bf16[128,4096]{1,0:T(8,128)(2,1)} custom-call(f32[128,1024]{1,0:T(8,128)S(1)} %get-tuple-element.142.refs_11_.refs_0_, bf16[128,1024]{1,0:T(8,128)(2,1)S(1)} %collective-permute-done.38.refs_1_, bf16[128,1024]{1,0:T(8,128)(2,1)S(1)} %collective-permute-done.39.refs_2_, bf16[128,1024]{1,0:T(8,128)(2,1)S(1)} %collective-permute-done.40.refs_3_, ...), custom_call_target="tpu_custom_call" | custom-call | flops 1073741824 | bytes 8388609 | tf_op jit(solution)/shard_map/token_grad/pallas_call | solution.py:421
  (72 shorter events, 4.2 us)
Async XLA Ops:
  0.6 4.1 %copy-start = (bf16[4096,512]{1,0:T(8,128)(2,1)S(1)}, bf16[4096,512]{1,0:T(8,128)(2,1)}, u32[]{:S(2)}) copy-start(bf16[4096,512]{1,0:T(8,128)(2,1)} %refs_5_) | copy-start | bytes 12582916
  0.6 4.1 %collective-permute-start = (bf16[128,4096]{1,0:T(8,128)(2,1)}, bf16[128,4096]{1,0:T(8,128)(2,1)S(1)}, u32[]{:S(2)}, u32[]{:S(2)}) collective-permute-start(bf16[128,4096]{1,0:T(8,128)(2,1)} %param.10), channel_id=1, source_target_pairs={{0,1},{1,0},{2,3},{3,2},{4,5},{5,4},{6,7},{7,6},{8,9},{9,8},{10,11... | collective-permute-start | bytes 3145736 | tf_op jit(solution)/shard_map/ppermute | solution.py:456
  4.6 2.2 %copy-start.1 = (s32[128,8]{0,1:T(8,128)S(1)}, s32[128,8]{0,1:T(8,128)}, u32[]{:S(2)}) copy-start(s32[128,8]{0,1:T(8,128)} %param.12) | copy-start | bytes 12292
  4.7 2.2 %copy-start.2 = (s32[128,8]{0,1:T(8,128)S(1)}, s32[128,8]{0,1:T(8,128)}, u32[]{:S(2)}) copy-start(s32[128,8]{0,1:T(8,128)} %param.13) | copy-start | bytes 12292
  4.7 2.2 %copy-start.3 = (f32[128,8]{0,1:T(8,128)S(1)}, f32[128,8]{0,1:T(8,128)}, u32[]{:S(2)}) copy-start(f32[128,8]{0,1:T(8,128)} %param.14) | copy-start | bytes 12292
  4.7 2.3 %copy-start.4 = (bf16[1,512,1536]{2,1,0:T(8,128)(2,1)S(1)}, bf16[1,512,1536]{2,1,0:T(8,128)(2,1)}, u32[]{:S(2)}) copy-start(bf16[1,512,1536]{2,1,0:T(8,128)(2,1)} %param.17) | copy-start | bytes 4718596
  4.7 2.5 %copy-start.8 = (bf16[128,4096]{1,0:T(8,128)(2,1)S(1)}, bf16[128,4096]{1,0:T(8,128)(2,1)}, u32[]{:S(2)}) copy-start(bf16[128,4096]{1,0:T(8,128)(2,1)} %param.11) | copy-start | bytes 3145732
  4.7 2.8 %copy-start.5 = (bf16[1,512,1536]{2,1,0:T(8,128)(2,1)S(1)}, bf16[1,512,1536]{2,1,0:T(8,128)(2,1)}, u32[]{:S(2)}) copy-start(bf16[1,512,1536]{2,1,0:T(8,128)(2,1)} %param.18) | copy-start | bytes 4718596
  4.7 3.0 %copy-start.6 = (bf16[1,1536,512]{2,1,0:T(8,128)(2,1)S(1)}, bf16[1,1536,512]{2,1,0:T(8,128)(2,1)}, u32[]{:S(2)}) copy-start(bf16[1,1536,512]{2,1,0:T(8,128)(2,1)} %param.19) | copy-start | bytes 4718596
  5.5 1.4 collective-permute-start.1
  6.9 7.7 %copy-start.7 = (bf16[512,4096]{1,0:T(8,128)(2,1)S(1)}, bf16[512,4096]{1,0:T(8,128)(2,1)}, u32[]{:S(2)}) copy-start(bf16[512,4096]{1,0:T(8,128)(2,1)} %param.16) | copy-start | bytes 12582916
  7.0 9.4 %collective-permute-start.5 = (bf16[512,1536]{1,0:T(8,128)(2,1)S(1)}, bf16[512,1536]{1,0:T(8,128)(2,1)S(1)}, u32[]{:S(2)}, u32[]{:S(2)}) collective-permute-start(bf16[512,1536]{1,0:T(8,128)(2,1)S(1)} %bitcast.20), channel_id=1, source_target_pairs={{0,1},{1,0},{2,3},{3,2},{4,5},{5,4},{6,7},{7,6},{8,9},{9,8},{10,11... | collective-permute-start | bytes 4718600 | tf_op jit(solution)/shard_map/ppermute | solution.py:456
  7.2 7.5 %collective-permute-start.3 = (bf16[128,4096]{1,0:T(8,128)(2,1)S(1)}, bf16[128,4096]{1,0:T(8,128)(2,1)S(1)}, u32[]{:S(2)}, u32[]{:S(2)}) collective-permute-start(bf16[128,4096]{1,0:T(8,128)(2,1)S(1)} %copy-done.8), channel_id=1, source_target_pairs={{0,1},{1,0},{2,3},{3,2},{4,5},{5,4},{6,7},{7,6},{8,9},{9,8},{10,11... | collective-permute-start | bytes 3145736 | tf_op jit(solution)/shard_map/ppermute | solution.py:456
  7.5 18.7 %collective-permute-start.11 = (bf16[512,1536]{1,0:T(8,128)(2,1)S(1)}, bf16[512,1536]{1,0:T(8,128)(2,1)S(1)}, u32[]{:S(2)}, u32[]{:S(2)}) collective-permute-start(bf16[512,1536]{1,0:T(8,128)(2,1)S(1)} %bitcast.25), channel_id=1, source_target_pairs={{0,1},{1,0},{2,3},{3,2},{4,5},{5,4},{6,7},{7,6},{8,9},{9,8},{10,11... | collective-permute-start | bytes 4718600 | tf_op jit(solution)/shard_map/ppermute | solution.py:456
  7.7 18.5 %collective-permute-start.12 = (bf16[1536,512]{1,0:T(8,128)(2,1)S(1)}, bf16[1536,512]{1,0:T(8,128)(2,1)S(1)}, u32[]{:S(2)}, u32[]{:S(2)}) collective-permute-start(bf16[1536,512]{1,0:T(8,128)(2,1)S(1)} %bitcast.30), channel_id=1, source_target_pairs={{0,1},{1,0},{2,3},{3,2},{4,5},{5,4},{6,7},{7,6},{8,9},{9,8},{10,11... | collective-permute-start | bytes 4718600 | tf_op jit(solution)/shard_map/ppermute | solution.py:456
  8.1 13.4 %collective-permute-start.9 = (bf16[144,1024]{1,0:T(8,128)(2,1)S(1)}, bf16[144,1024]{1,0:T(8,128)(2,1)S(1)}, u32[]{:S(2)}, u32[]{:S(2)}) collective-permute-start(bf16[144,1024]{1,0:T(8,128)(2,1)S(1)} %join_rows.2.block_ref.refs_0_.refs_2_), channel_id=1, source_target_pairs={{0,8},{2,10},{4,12},{6,14},{8,16},{10,18},{12,20},{14,22},{16,24},... | collective-permute-start | bytes 884744 | tf_op jit(solution)/shard_map/plane_l1/ppermute | solution.py:459
  16.2 1.7 %collective-permute-start.4 = (bf16[128,512]{1,0:T(8,128)(2,1)S(1)}, bf16[128,512]{1,0:T(8,128)(2,1)S(1)}, u32[]{:S(2)}, u32[]{:S(2)}) collective-permute-start(bf16[128,512]{1,0:T(8,128)(2,1)S(1)} %convolution_convert_fusion.refs_0_), channel_id=1, source_target_pairs={{0,1},{1,0},{2,3},{3,2},{4,5},{5,4},{6,7},{7,6},{8,9},{9,8},{10,11... | collective-permute-start | bytes 393224 | tf_op jit(solution)/shard_map/ppermute | solution.py:456
  16.4 9.8 %collective-permute-start.2 = (bf16[144,1024]{1,0:T(8,128)(2,1)S(1)}, bf16[144,1024]{1,0:T(8,128)(2,1)S(1)}, u32[]{:S(2)}, u32[]{:S(2)}) collective-permute-start(bf16[144,1024]{1,0:T(8,128)(2,1)S(1)} %join_rows.2.block_ref.refs_0_.refs_2_), channel_id=1, source_target_pairs={{0,2},{2,0},{4,6},{6,4},{8,10},{10,8},{12,14},{14,12},{16,18},{18,... | collective-permute-start | bytes 884744 | tf_op jit(solution)/shard_map/side_l0/ppermute | solution.py:470
  17.9 13.0 %collective-permute-start.7 = (bf16[144,1024]{1,0:T(8,128)(2,1)S(1)}, bf16[144,1024]{1,0:T(8,128)(2,1)S(1)}, u32[]{:S(2)}, u32[]{:S(2)}) collective-permute-start(bf16[144,1024]{1,0:T(8,128)(2,1)S(1)} %tie_rows.5.refs_0_), channel_id=1, source_target_pairs={{0,24},{2,26},{4,28},{6,30},{8,0},{10,2},{12,4},{14,6},{16,8},{18,... | collective-permute-start | bytes 884744 | tf_op jit(solution)/shard_map/plane_l3/ppermute | solution.py:459
  21.5 10.9 %collective-permute-start.10 = (bf16[144,1024]{1,0:T(8,128)(2,1)S(1)}, bf16[144,1024]{1,0:T(8,128)(2,1)S(1)}, u32[]{:S(2)}, u32[]{:S(2)}) collective-permute-start(bf16[144,1024]{1,0:T(8,128)(2,1)S(1)} %collective-permute-done.9.refs_5_.refs_1_.refs_0_.refs_2_), channel_id=1, source_target_pairs={{0,2},{2,0},{4,6},{6,4},{8,10},{10,8},{12,14},{14,12},{16,18},{18,... | collective-permute-start | bytes 884744 | tf_op jit(solution)/shard_map/side_l1/ppermute | solution.py:470
  26.7 9.4 %collective-permute-start.13 = (bf16[144,1024]{1,0:T(8,128)(2,1)S(1)}, bf16[144,1024]{1,0:T(8,128)(2,1)S(1)}, u32[]{:S(2)}, u32[]{:S(2)}) collective-permute-start(bf16[144,1024]{1,0:T(8,128)(2,1)S(1)} %get-tuple-element.86), channel_id=1, source_target_pairs={{0,4},{2,6},{4,0},{6,2},{8,12},{10,14},{12,8},{14,10},{16,20},{18,... | collective-permute-start | bytes 884744 | tf_op jit(solution)/shard_map/piece_l0/ppermute | solution.py:474
  28.3 21.9 %collective-permute-start.16 = (bf16[144,1024]{1,0:T(8,128)(2,1)S(1)}, bf16[144,1024]{1,0:T(8,128)(2,1)S(1)}, u32[]{:S(2)}, u32[]{:S(2)}) collective-permute-start(bf16[144,1024]{1,0:T(8,128)(2,1)S(1)} %tie_rows.6.refs_4_), channel_id=1, source_target_pairs={{0,16},{2,18},{4,20},{6,22},{8,24},{10,26},{12,28},{14,30},{16,0},... | collective-permute-start | bytes 884744 | tf_op jit(solution)/shard_map/plane_l2/ppermute | solution.py:459
  30.9 20.7 %collective-permute-start.8 = (bf16[144,1024]{1,0:T(8,128)(2,1)S(1)}, bf16[144,1024]{1,0:T(8,128)(2,1)S(1)}, u32[]{:S(2)}, u32[]{:S(2)}) collective-permute-start(bf16[144,1024]{1,0:T(8,128)(2,1)S(1)} %collective-permute-done.7.refs_5_.refs_1_.refs_0_.refs_2_), channel_id=1, source_target_pairs={{0,2},{2,0},{4,6},{6,4},{8,10},{10,8},{12,14},{14,12},{16,18},{18,... | collective-permute-start | bytes 884744 | tf_op jit(solution)/shard_map/side_l3/ppermute | solution.py:470
  32.9 19.8 %collective-permute-start.14 = (bf16[144,1024]{1,0:T(8,128)(2,1)S(1)}, bf16[144,1024]{1,0:T(8,128)(2,1)S(1)}, u32[]{:S(2)}, u32[]{:S(2)}) collective-permute-start(bf16[144,1024]{1,0:T(8,128)(2,1)S(1)} %get-tuple-element.88), channel_id=1, source_target_pairs={{0,4},{2,6},{4,0},{6,2},{8,12},{10,14},{12,8},{14,10},{16,20},{18,... | collective-permute-start | bytes 884744 | tf_op jit(solution)/shard_map/piece_l1/ppermute | solution.py:474
  34.6 18.2 %collective-permute-start.6 = (bf16[128,1024]{1,0:T(8,128)(2,1)S(1)}, bf16[128,1024]{1,0:T(8,128)(2,1)S(1)}, u32[]{:S(2)}, u32[]{:S(2)}) collective-permute-start(bf16[128,1024]{1,0:T(8,128)(2,1)S(1)} %join_rows.3.refs_4_.block_ref.refs_2_), channel_id=1, source_target_pairs={{0,2},{2,0},{4,6},{6,4},{8,10},{10,8},{12,14},{14,12},{16,18},{18,... | collective-permute-start | bytes 786440 | tf_op jit(solution)/shard_map/side_b0/ppermute | solution.py:470
  36.1 25.9 %collective-permute-start.19 = (bf16[128,1024]{1,0:T(8,128)(2,1)S(1)}, bf16[128,1024]{1,0:T(8,128)(2,1)S(1)}, u32[]{:S(2)}, u32[]{:S(2)}) collective-permute-start(bf16[128,1024]{1,0:T(8,128)(2,1)S(1)} %tie_rows.7.refs_4_), channel_id=1, source_target_pairs={{0,16},{2,18},{4,20},{6,22},{8,24},{10,26},{12,28},{14,30},{16,0},... | collective-permute-start | bytes 786440 | tf_op jit(solution)/shard_map/plane_b2/ppermute | solution.py:459
  50.2 11.9 %collective-permute-start.17 = (bf16[144,1024]{1,0:T(8,128)(2,1)S(1)}, bf16[144,1024]{1,0:T(8,128)(2,1)S(1)}, u32[]{:S(2)}, u32[]{:S(2)}) collective-permute-start(bf16[144,1024]{1,0:T(8,128)(2,1)S(1)} %collective-permute-done.16.refs_1_.refs_0_.refs_2_), channel_id=1, source_target_pairs={{0,2},{2,0},{4,6},{6,4},{8,10},{10,8},{12,14},{14,12},{16,18},{18,... | collective-permute-start | bytes 884744 | tf_op jit(solution)/shard_map/side_l2/ppermute | solution.py:470
  52.1 9.9 %collective-permute-start.18 = (bf16[144,1024]{1,0:T(8,128)(2,1)S(1)}, bf16[144,1024]{1,0:T(8,128)(2,1)S(1)}, u32[]{:S(2)}, u32[]{:S(2)}) collective-permute-start(bf16[144,1024]{1,0:T(8,128)(2,1)S(1)} %get-tuple-element.92), channel_id=1, source_target_pairs={{0,4},{2,6},{4,0},{6,2},{8,12},{10,14},{12,8},{14,10},{16,20},{18,... | collective-permute-start | bytes 884744 | tf_op jit(solution)/shard_map/piece_l3/ppermute | solution.py:474
  53.2 10.5 %collective-permute-start.23 = (bf16[128,1024]{1,0:T(8,128)(2,1)S(1)}, bf16[128,1024]{1,0:T(8,128)(2,1)S(1)}, u32[]{:S(2)}, u32[]{:S(2)}) collective-permute-start(bf16[128,1024]{1,0:T(8,128)(2,1)S(1)} %tie_rows.8.refs_8_), channel_id=1, source_target_pairs={{0,24},{2,26},{4,28},{6,30},{8,0},{10,2},{12,4},{14,6},{16,8},{18,... | collective-permute-start | bytes 786440 | tf_op jit(solution)/shard_map/plane_b3/ppermute | solution.py:459
  55.7 15.5 %collective-permute-start.15 = (bf16[144,1024]{1,0:T(8,128)(2,1)S(1)}, bf16[144,1024]{1,0:T(8,128)(2,1)S(1)}, u32[]{:S(2)}, u32[]{:S(2)}) collective-permute-start(bf16[144,1024]{1,0:T(8,128)(2,1)S(1)} %get-tuple-element.90), channel_id=1, source_target_pairs={{0,4},{2,6},{4,0},{6,2},{8,12},{10,14},{12,8},{14,10},{16,20},{18,... | collective-permute-start | bytes 884744 | tf_op jit(solution)/shard_map/piece_b0/ppermute | solution.py:474
  62.6 11.7 %collective-permute-start.22 = (bf16[144,1024]{1,0:T(8,128)(2,1)S(1)}, bf16[144,1024]{1,0:T(8,128)(2,1)S(1)}, u32[]{:S(2)}, u32[]{:S(2)}) collective-permute-start(bf16[144,1024]{1,0:T(8,128)(2,1)S(1)} %get-tuple-element.94), channel_id=1, source_target_pairs={{0,4},{2,6},{4,0},{6,2},{8,12},{10,14},{12,8},{14,10},{16,20},{18,... | collective-permute-start | bytes 884744 | tf_op jit(solution)/shard_map/piece_l2/ppermute | solution.py:474
  63.1 8.1 %collective-permute-start.25 = (bf16[128,1024]{1,0:T(8,128)(2,1)S(1)}, bf16[128,1024]{1,0:T(8,128)(2,1)S(1)}, u32[]{:S(2)}, u32[]{:S(2)}) collective-permute-start(bf16[128,1024]{1,0:T(8,128)(2,1)S(1)} %collective-permute-done.19.refs_6_.refs_1_.refs_2_), channel_id=1, source_target_pairs={{0,2},{2,0},{4,6},{6,4},{8,10},{10,8},{12,14},{14,12},{16,18},{18,... | collective-permute-start | bytes 786440 | tf_op jit(solution)/shard_map/side_b2/ppermute | solution.py:470
  63.7 8.4 %collective-permute-start.20 = (bf16[128,1024]{1,0:T(8,128)(2,1)S(1)}, bf16[128,1024]{1,0:T(8,128)(2,1)S(1)}, u32[]{:S(2)}, u32[]{:S(2)}) collective-permute-start(bf16[128,1024]{1,0:T(8,128)(2,1)S(1)} %tie_rows.9.refs_4_), channel_id=1, source_target_pairs={{0,8},{2,10},{4,12},{6,14},{8,16},{10,18},{12,20},{14,22},{16,24},... | collective-permute-start | bytes 786440 | tf_op jit(solution)/shard_map/plane_b1/ppermute | solution.py:459
  63.8 10.3 %collective-permute-start.24 = (bf16[128,1024]{1,0:T(8,128)(2,1)S(1)}, bf16[128,1024]{1,0:T(8,128)(2,1)S(1)}, u32[]{:S(2)}, u32[]{:S(2)}) collective-permute-start(bf16[128,1024]{1,0:T(8,128)(2,1)S(1)} %collective-permute-done.23.refs_6_.refs_2_), channel_id=1, source_target_pairs={{0,2},{2,0},{4,6},{6,4},{8,10},{10,8},{12,14},{14,12},{16,18},{18,... | collective-permute-start | bytes 786440 | tf_op jit(solution)/shard_map/side_b3/ppermute | solution.py:470
  71.7 9.3 %collective-permute-start.26 = (bf16[144,1024]{1,0:T(8,128)(2,1)S(1)}, bf16[144,1024]{1,0:T(8,128)(2,1)S(1)}, u32[]{:S(2)}, u32[]{:S(2)}) collective-permute-start(bf16[144,1024]{1,0:T(8,128)(2,1)S(1)} %get-tuple-element.98), channel_id=1, source_target_pairs={{0,4},{2,6},{4,0},{6,2},{8,12},{10,14},{12,8},{14,10},{16,20},{18,... | collective-permute-start | bytes 884744 | tf_op jit(solution)/shard_map/piece_b2/ppermute | solution.py:474
  72.1 64.2 %collective-permute-start.41 = (bf16[4096,512]{1,0:T(8,128)(2,1)S(1)}, bf16[4096,512]{1,0:T(8,128)(2,1)S(1)}, u32[]{:S(2)}, u32[]{:S(2)}) collective-permute-start(bf16[4096,512]{1,0:T(8,128)(2,1)S(1)} %copy-done), channel_id=1, source_target_pairs={{0,1},{1,0},{2,3},{3,2},{4,5},{5,4},{6,7},{7,6},{8,9},{9,8},{10,11... | collective-permute-start | bytes 12582920 | tf_op jit(solution)/shard_map/ppermute | solution.py:456
  72.1 8.9 %collective-permute-start.21 = (bf16[128,1024]{1,0:T(8,128)(2,1)S(1)}, bf16[128,1024]{1,0:T(8,128)(2,1)S(1)}, u32[]{:S(2)}, u32[]{:S(2)}) collective-permute-start(bf16[128,1024]{1,0:T(8,128)(2,1)S(1)} %collective-permute-done.20.refs_6_.refs_2_), channel_id=1, source_target_pairs={{0,2},{2,0},{4,6},{6,4},{8,10},{10,8},{12,14},{14,12},{16,18},{18,... | collective-permute-start | bytes 786440 | tf_op jit(solution)/shard_map/side_b1/ppermute | solution.py:470
  74.7 11.1 %collective-permute-start.28 = (bf16[144,1024]{1,0:T(8,128)(2,1)S(1)}, bf16[144,1024]{1,0:T(8,128)(2,1)S(1)}, u32[]{:S(2)}, u32[]{:S(2)}) collective-permute-start(bf16[144,1024]{1,0:T(8,128)(2,1)S(1)} %get-tuple-element.103), channel_id=1, source_target_pairs={{0,4},{2,6},{4,0},{6,2},{8,12},{10,14},{12,8},{14,10},{16,20},{18,... | collective-permute-start | bytes 884744 | tf_op jit(solution)/shard_map/piece_b3/ppermute | solution.py:474
  81.5 10.4 %collective-permute-start.27 = (bf16[144,1024]{1,0:T(8,128)(2,1)S(1)}, bf16[144,1024]{1,0:T(8,128)(2,1)S(1)}, u32[]{:S(2)}, u32[]{:S(2)}) collective-permute-start(bf16[144,1024]{1,0:T(8,128)(2,1)S(1)} %get-tuple-element.100), channel_id=1, source_target_pairs={{0,4},{2,6},{4,0},{6,2},{8,12},{10,14},{12,8},{14,10},{16,20},{18,... | collective-permute-start | bytes 884744 | tf_op jit(solution)/shard_map/piece_b1/ppermute | solution.py:474
  91.8 6.8 %collective-permute-start.29 = (bf16[144,1024]{1,0:T(8,128)(2,1)S(1)}, bf16[144,1024]{1,0:T(8,128)(2,1)S(1)}, u32[]{:S(2)}, u32[]{:S(2)}) collective-permute-start(bf16[144,1024]{1,0:T(8,128)(2,1)S(1)} %get-tuple-element.111), channel_id=1, source_target_pairs={{0,4},{2,6},{4,0},{6,2},{8,12},{10,14},{12,8},{14,10},{16,20},{18,... | collective-permute-start | bytes 884744 | tf_op jit(solution)/shard_map/piece_r3/ppermute | solution.py:474
  99.1 7.7 %collective-permute-start.30 = (bf16[144,1024]{1,0:T(8,128)(2,1)S(1)}, bf16[144,1024]{1,0:T(8,128)(2,1)S(1)}, u32[]{:S(2)}, u32[]{:S(2)}) collective-permute-start(bf16[144,1024]{1,0:T(8,128)(2,1)S(1)} %get-tuple-element.114), channel_id=1, source_target_pairs={{0,4},{2,6},{4,0},{6,2},{8,12},{10,14},{12,8},{14,10},{16,20},{18,... | collective-permute-start | bytes 884744 | tf_op jit(solution)/shard_map/piece_r2/ppermute | solution.py:474
  100.4 6.4 %collective-permute-start.31 = (bf16[128,1024]{1,0:T(8,128)(2,1)S(1)}, bf16[128,1024]{1,0:T(8,128)(2,1)S(1)}, u32[]{:S(2)}, u32[]{:S(2)}) collective-permute-start(bf16[128,1024]{1,0:T(8,128)(2,1)S(1)} %get-tuple-element.116), channel_id=1, source_target_pairs={{0,2},{2,0},{4,6},{6,4},{8,10},{10,8},{12,14},{14,12},{16,18},{18,... | collective-permute-start | bytes 786440 | tf_op jit(solution)/shard_map/side_r3/ppermute | solution.py:470
  107.4 14.8 %collective-permute-start.37 = (bf16[1024,1536]{1,0:T(8,128)(2,1)S(1)}, bf16[1024,1536]{1,0:T(8,128)(2,1)S(1)}, u32[]{:S(2)}, u32[]{:S(2)}) collective-permute-start(bf16[1024,1536]{1,0:T(8,128)(2,1)S(1)} %get-tuple-element.140), channel_id=1, source_target_pairs={{0,1},{1,0},{2,3},{3,2},{4,5},{5,4},{6,7},{7,6},{8,9},{9,8},{10,11... | collective-permute-start | bytes 9437192 | tf_op jit(solution)/shard_map/ppermute | solution.py:456
  107.4 11.9 %collective-permute-start.32 = (bf16[144,1024]{1,0:T(8,128)(2,1)S(1)}, bf16[144,1024]{1,0:T(8,128)(2,1)S(1)}, u32[]{:S(2)}, u32[]{:S(2)}) collective-permute-start(bf16[144,1024]{1,0:T(8,128)(2,1)S(1)} %get-tuple-element.130), channel_id=1, source_target_pairs={{0,4},{2,6},{4,0},{6,2},{8,12},{10,14},{12,8},{14,10},{16,20},{18,... | collective-permute-start | bytes 884744 | tf_op jit(solution)/shard_map/piece_r1/ppermute | solution.py:474
  108.3 8.4 %collective-permute-start.33 = (bf16[128,1024]{1,0:T(8,128)(2,1)S(1)}, bf16[128,1024]{1,0:T(8,128)(2,1)S(1)}, u32[]{:S(2)}, u32[]{:S(2)}) collective-permute-start(bf16[128,1024]{1,0:T(8,128)(2,1)S(1)} %get-tuple-element.132), channel_id=1, source_target_pairs={{0,2},{2,0},{4,6},{6,4},{8,10},{10,8},{12,14},{14,12},{16,18},{18,... | collective-permute-start | bytes 786440 | tf_op jit(solution)/shard_map/side_r2/ppermute | solution.py:470
  109.5 9.9 %collective-permute-start.34 = (bf16[128,1024]{1,0:T(8,128)(2,1)S(1)}, bf16[128,1024]{1,0:T(8,128)(2,1)S(1)}, u32[]{:S(2)}, u32[]{:S(2)}) collective-permute-start(bf16[128,1024]{1,0:T(8,128)(2,1)S(1)} %get-tuple-element.136), channel_id=1, source_target_pairs={{0,8},{2,10},{4,12},{6,14},{8,16},{10,18},{12,20},{14,22},{16,24},... | collective-permute-start | bytes 786440 | tf_op jit(solution)/shard_map/plane_r3/ppermute | solution.py:459
  120.0 12.1 %collective-permute-start.42 = (bf16[1536,512]{1,0:T(8,128)(2,1)S(1)}, bf16[1536,512]{1,0:T(8,128)(2,1)S(1)}, u32[]{:S(2)}, u32[]{:S(2)}) collective-permute-start(bf16[1536,512]{1,0:T(8,128)(2,1)S(1)} %get-tuple-element.147), channel_id=1, source_target_pairs={{0,1},{1,0},{2,3},{3,2},{4,5},{5,4},{6,7},{7,6},{8,9},{9,8},{10,11... | collective-permute-start | bytes 4718600 | tf_op jit(solution)/shard_map/ppermute | solution.py:456
  120.0 9.7 %collective-permute-start.35 = (bf16[144,1024]{1,0:T(8,128)(2,1)S(1)}, bf16[144,1024]{1,0:T(8,128)(2,1)S(1)}, u32[]{:S(2)}, u32[]{:S(2)}) collective-permute-start(bf16[144,1024]{1,0:T(8,128)(2,1)S(1)} %get-tuple-element.137), channel_id=1, source_target_pairs={{0,4},{2,6},{4,0},{6,2},{8,12},{10,14},{12,8},{14,10},{16,20},{18,... | collective-permute-start | bytes 884744 | tf_op jit(solution)/shard_map/piece_r0/ppermute | solution.py:474
  121.4 8.4 %collective-permute-start.36 = (bf16[128,1024]{1,0:T(8,128)(2,1)S(1)}, bf16[128,1024]{1,0:T(8,128)(2,1)S(1)}, u32[]{:S(2)}, u32[]{:S(2)}) collective-permute-start(bf16[128,1024]{1,0:T(8,128)(2,1)S(1)} %get-tuple-element.139), channel_id=1, source_target_pairs={{0,2},{2,0},{4,6},{6,4},{8,10},{10,8},{12,14},{14,12},{16,18},{18,... | collective-permute-start | bytes 786440 | tf_op jit(solution)/shard_map/side_r1/ppermute | solution.py:470
  122.2 14.1 %collective-permute-start.40 = (bf16[128,1024]{1,0:T(8,128)(2,1)S(1)}, bf16[128,1024]{1,0:T(8,128)(2,1)S(1)}, u32[]{:S(2)}, u32[]{:S(2)}) collective-permute-start(bf16[128,1024]{1,0:T(8,128)(2,1)S(1)} %get-tuple-element.145), channel_id=1, source_target_pairs={{0,16},{2,18},{4,20},{6,22},{8,24},{10,26},{12,28},{14,30},{16,0},... | collective-permute-start | bytes 786440 | tf_op jit(solution)/shard_map/plane_r2/ppermute | solution.py:459
  130.3 7.8 %collective-permute-start.38 = (bf16[128,1024]{1,0:T(8,128)(2,1)S(1)}, bf16[128,1024]{1,0:T(8,128)(2,1)S(1)}, u32[]{:S(2)}, u32[]{:S(2)}) collective-permute-start(bf16[128,1024]{1,0:T(8,128)(2,1)S(1)} %get-tuple-element.143), channel_id=1, source_target_pairs={{0,2},{2,0},{4,6},{6,4},{8,10},{10,8},{12,14},{14,12},{16,18},{18,... | collective-permute-start | bytes 786440 | tf_op jit(solution)/shard_map/side_r0/ppermute | solution.py:470
  131.2 9.1 %collective-permute-start.39 = (bf16[128,1024]{1,0:T(8,128)(2,1)S(1)}, bf16[128,1024]{1,0:T(8,128)(2,1)S(1)}, u32[]{:S(2)}, u32[]{:S(2)}) collective-permute-start(bf16[128,1024]{1,0:T(8,128)(2,1)S(1)} %get-tuple-element.144), channel_id=1, source_target_pairs={{0,24},{2,26},{4,28},{6,30},{8,0},{10,2},{12,4},{14,6},{16,8},{18,... | collective-permute-start | bytes 786440 | tf_op jit(solution)/shard_map/plane_r1/ppermute | solution.py:459
